TPU v7x, 512 devices: a whole 4x4x16 slice. The times are simulated.
512 devices in a mesh: outer: 64 (over x_hi, z, core), inner: 8 (over y, x_lo).
Axes of the slice: x: 4 (x_hi: 2, x_lo: 2; x = x_hi * 2 + x_lo), y: 4, z: 16, core: 2. Of those that a mesh axis runs over, the one named last changes fastest.
Arguments:
- queries: bfloat16 [196608, 256], P(('outer', 'inner')), may hold values from -20 to 20
- key_rows: bfloat16 [196608, 256], P(('outer', 'inner')), may hold values from -20 to 20
- value_rows: bfloat16 [196608, 256], P(('outer', 'inner')), may hold values from -6 to 6
- outputs: bfloat16 [196608, 256], P(('outer', 'inner')), may hold values from -4 to 4
- out_grad: bfloat16 [196608, 256], P(('outer', 'inner')), may hold values from -6 to 6
Outputs:
- query_grad: bfloat16 [196608, 256], P(('outer', 'inner'))
- key_grad: bfloat16 [196608, 256], P(('outer', 'inner'))
- value_grad: bfloat16 [196608, 256], P(('outer', 'inner'))
All inputs are finite; a program needn't handle non-finite values.
Results may differ from a plain program's by a relative error of at most 0.014.
Values may be sent and summed in bfloat16 or wider, within the bound.
No kernel may reach another device: no remote copies, remote signals or barrier semaphores. Data moves between devices by JAX's collectives and lax.ppermute only.
A program may use at most 64 MiB of HBM per device.

v0:
```python
import jax
import jax.numpy as jnp
from jax import lax
from jax.sharding import PartitionSpec as P

HEADS = 2
HEAD_DIM = 128


def passed_along(value, axis, steps):
    count = lax.axis_size(axis)
    pairs = [(source, (source + steps) % count) for source in range(count)]
    return lax.ppermute(value, axis, pairs)


def split_heads(block):
    return block.reshape(block.shape[0], HEADS, HEAD_DIM)


def scores_of(query_heads, key_block, scale_factor):
    return (
        jnp.einsum(
            "qhd,khd->hqk", query_heads, split_heads(key_block), preferred_element_type=jnp.float32
        )
        * scale_factor
    )


def tile_grads(query_heads, grad_heads, lse_rows, delta_rows, key_block, value_block, scale_factor):
    scores = scores_of(query_heads, key_block, scale_factor)
    weights = jnp.exp(scores - lse_rows[:, :, None])
    weights_low = weights.astype(jnp.bfloat16)
    prob_grad = jnp.einsum(
        "qhd,khd->hqk", grad_heads, split_heads(value_block), preferred_element_type=jnp.float32
    )
    score_grad = (weights * (prob_grad - delta_rows[:, :, None]) * scale_factor).astype(
        jnp.bfloat16
    )
    grad_query = jnp.einsum(
        "hqk,khd->qhd", score_grad, split_heads(key_block), preferred_element_type=jnp.float32
    )
    grad_key = jnp.einsum(
        "hqk,qhd->khd", score_grad, query_heads, preferred_element_type=jnp.float32
    )
    grad_value = jnp.einsum(
        "hqk,qhd->khd", weights_low, grad_heads, preferred_element_type=jnp.float32
    )
    width = HEADS * HEAD_DIM
    return (
        grad_query.reshape(query_heads.shape[0], width),
        grad_key.reshape(key_block.shape[0], width),
        grad_value.reshape(key_block.shape[0], width),
    )


def on_device(queries, key_rows, value_rows, outputs, out_grad):
    scale_factor = HEAD_DIM ** (-0.5)
    rows_here = queries.shape[0]
    prior_keys, prior_values = passed_along((key_rows, value_rows), "outer", 1)
    window_keys = jnp.concatenate([key_rows, prior_keys], axis=0)
    window_values = jnp.concatenate([value_rows, prior_values], axis=0)
    query_heads = split_heads(queries)
    grad_heads = split_heads(out_grad)
    delta_rows = jnp.einsum(
        "qhd,qhd->hq", grad_heads, split_heads(outputs), preferred_element_type=jnp.float32
    )
    largest = jnp.full((HEADS, rows_here), -1e30, jnp.float32)
    scores = scores_of(
        query_heads, lax.all_gather(window_keys, "inner", axis=0, tiled=True), scale_factor
    )
    newest = jnp.maximum(largest, jnp.max(scores, axis=2))
    total = jnp.sum(jnp.exp(scores - newest[:, :, None]), axis=2)
    largest, total = (newest, total)
    lse_rows = largest + jnp.log(total)
    turns = lax.axis_size("inner")
    key_zeros = jnp.zeros(window_keys.shape, jnp.float32)
    query_zeros = jnp.zeros(queries.shape, jnp.float32)

    def query_turn(index, state):
        moving_queries, moving_grads, moving_lse, moving_delta, query_acc, key_acc, value_acc = (
            state
        )
        grad_query, grad_key, grad_value = tile_grads(
            split_heads(moving_queries),
            split_heads(moving_grads),
            moving_lse,
            moving_delta,
            window_keys,
            window_values,
            scale_factor,
        )
        moving_queries, moving_grads = passed_along((moving_queries, moving_grads), "inner", 1)
        moving_lse, moving_delta, query_acc = passed_along(
            (moving_lse, moving_delta, query_acc + grad_query), "inner", 1
        )
        return (
            moving_queries,
            moving_grads,
            moving_lse,
            moving_delta,
            query_acc,
            key_acc + grad_key,
            value_acc + grad_value,
        )

    final = lax.fori_loop(
        0,
        turns,
        query_turn,
        (queries, out_grad, lse_rows, delta_rows, query_zeros, key_zeros, key_zeros),
    )
    query_acc, key_acc, value_acc = (final[4], final[5], final[6])
    returned_keys, returned_values = (
        passed_along(key_acc[rows_here:].astype(jnp.bfloat16), "outer", -1).astype(jnp.float32),
        passed_along(value_acc[rows_here:].astype(jnp.bfloat16), "outer", -1).astype(jnp.float32),
    )
    key_grad = (key_acc[:rows_here] + returned_keys).astype(jnp.bfloat16)
    value_grad = (value_acc[:rows_here] + returned_values).astype(jnp.bfloat16)
    return (query_acc.astype(jnp.bfloat16), key_grad, value_grad)


def solution(mesh):
    return jax.shard_map(
        on_device,
        mesh=mesh,
        in_specs=(
            P(("outer", "inner"), None),
            P(("outer", "inner"), None),
            P(("outer", "inner"), None),
            P(("outer", "inner"), None),
            P(("outer", "inner"), None),
        ),
        out_specs=(
            P(("outer", "inner"), None),
            P(("outer", "inner"), None),
            P(("outer", "inner"), None),
        ),
        check_vma=False,
    )
```

profile of v0, /device:TPU:24, one launch (start us, length us, event | category | flops | bytes accessed | tf_op | source)
XLA Modules:
  0.0 390.5 jit_solution(8693476136811200022)
XLA Ops:
  10.4 14.7 %collective-permute-done.5 = bf16[384,256]{0,1:T(8,128)(2,1)S(1)} collective-permute-done((bf16[384,256]{0,1:T(8,128)(2,1)S(1)}, bf16[384,256]{0,1:T(8,128)(2,1)S(1)}, u32[]{:S(2)}, u32[]{:S(2)}) %collective-permute-start.5) | collective-permute-done | bytes 196640 | tf_op jit(solution)/shard_map/ppermute | solution.py:13
  25.9 1.9 collective-permute-start.6
  32.1 4.6 %collective-permute-done.6 = bf16[384,256]{1,0:T(8,128)(2,1)S(1)} collective-permute-done((bf16[384,256]{1,0:T(8,128)(2,1)}, bf16[384,256]{1,0:T(8,128)(2,1)S(1)}, u32[]{:S(2)}, u32[]{:S(2)}) %collective-permute-start.6) | collective-permute-done | bytes 196640 | tf_op jit(solution)/shard_map/ppermute | solution.py:13
  37.5 62.0 %all-gather.2.cloned.1.call-done = bf16[6144,256]{0,1:T(8,128)(2,1)} async-done(((bf16[768,256]{0,1:T(8,128)(2,1)}), bf16[6144,256]{0,1:T(8,128)(2,1)}) %all-gather.2.cloned.1.call-update) | async-done | bytes 3145744 | tf_op jit(solution)/shard_map/all_gather | solution.py:69
  99.5 11.4 %bitcast_reduce_fusion = (f32[2,384]{1,0:T(2,128)S(1)}, f32[2,6144,384]{2,1,0:T(8,128)}) fusion(bf16[6144,2,128]{0,2,1:T(8,128)(2,1)} %bitcast.88, bf16[384,256]{1,0:T(8,128)(2,1)S(1)} %copy-done.1), kind=kOutput, calls=%fused_computation.13 | convolution fusion | flops 1217395968 | bytes 22219776 | tf_op jit(solution)/shard_map/qhd,khd->hqk/dot_general | solution.py:22
  110.9 9.5 %fusion.9 = f32[2,384]{1,0:T(2,128)S(1)} fusion(f32[2,6144,384]{2,1,0:T(8,128)} %get-tuple-element.136, f32[2,384]{1,0:T(2,128)S(1)} %broadcast_maximum_fusion), kind=kLoop, calls=%fused_computation.15 | loop fusion | flops 14155008 | bytes 18880512 | tf_op jit(solution)/shard_map/reduce_sum | solution.py:72
  120.4 247.4 %while.23 = (s32[]{:T(128)}, bf16[384,256]{0,1:T(8,128)(2,1)}, bf16[384,256]{0,1:T(8,128)(2,1)}, f32[2,384]{1,0:T(2,128)S(1)}, f32[2,384]{1,0:T(2,128)S(1)}, /*i...) while((s32[]{:T(128)}, bf16[384,256]{0,1:T(8,128)(2,1)}, ...), condition=%wide.region_3.0_spmd.clone, body=%wide.region_2.0_spmd.clone.sunk | while | flops 761167872 | bytes 24425796 | solution.py:106
  120.5 2.2 collective-permute-start.2
  123.6 5.0 %collective-permute-start = (bf16[384,256]{0,1:T(8,128)(2,1)S(1)}, bf16[384,256]{0,1:T(8,128)(2,1)}, u32[]{:S(2)}, u32[]{:S(2)}) collective-permute-start(bf16[384,256]{0,1:T(8,128)(2,1)S(1)} %copy.72), channel_id=1, source_target_pairs={{0,1},{1,2},{2,3},{3,4},{4,5},{5,6},{6,7},{7,0},{8,9},{9,10},{10,1... | collective-permute-start | bytes 589832 | tf_op jit(solution)/shard_map/while/body/eval_jaxpr/ppermute | solution.py:13
  129.5 2.0 collective-permute-start.1
  131.5 3.4 collective-permute-start.3
  138.6 3.4 collective-permute-start.4
  144.6 6.7 %collective-permute-done.4 = f32[384,256]{0,1:T(8,128)S(1)} collective-permute-done((f32[384,256]{0,1:T(8,128)}, f32[384,256]{0,1:T(8,128)S(1)}, u32[]{:S(2)}, u32[]{:S(2)}) %collective-permute-start.4) | collective-permute-done | bytes 393248 | tf_op jit(solution)/shard_map/while/body/eval_jaxpr/ppermute | solution.py:13
  151.3 2.5 collective-permute-start.2
  154.7 5.5 %collective-permute-start = (bf16[384,256]{0,1:T(8,128)(2,1)S(1)}, bf16[384,256]{0,1:T(8,128)(2,1)}, u32[]{:S(2)}, u32[]{:S(2)}) collective-permute-start(bf16[384,256]{0,1:T(8,128)(2,1)S(1)} %copy.72), channel_id=1, source_target_pairs={{0,1},{1,2},{2,3},{3,4},{4,5},{5,6},{6,7},{7,0},{8,9},{9,10},{10,1... | collective-permute-start | bytes 589832 | tf_op jit(solution)/shard_map/while/body/eval_jaxpr/ppermute | solution.py:13
  163.1 3.4 collective-permute-start.3
  173.1 2.6 bitcast_add_fusion.6
  175.8 5.1 %collective-permute-done.4 = f32[384,256]{0,1:T(8,128)S(1)} collective-permute-done((f32[384,256]{0,1:T(8,128)}, f32[384,256]{0,1:T(8,128)S(1)}, u32[]{:S(2)}, u32[]{:S(2)}) %collective-permute-start.4) | collective-permute-done | bytes 393248 | tf_op jit(solution)/shard_map/while/body/eval_jaxpr/ppermute | solution.py:13
  183.8 6.2 %collective-permute-start = (bf16[384,256]{0,1:T(8,128)(2,1)S(1)}, bf16[384,256]{0,1:T(8,128)(2,1)}, u32[]{:S(2)}, u32[]{:S(2)}) collective-permute-start(bf16[384,256]{0,1:T(8,128)(2,1)S(1)} %copy.72), channel_id=1, source_target_pairs={{0,1},{1,2},{2,3},{3,4},{4,5},{5,6},{6,7},{7,0},{8,9},{9,10},{10,1... | collective-permute-start | bytes 589832 | tf_op jit(solution)/shard_map/while/body/eval_jaxpr/ppermute | solution.py:13
  192.8 2.5 collective-permute-start.3
  199.0 2.8 collective-permute-start.4
  202.9 2.6 bitcast_add_fusion.6
  205.5 4.3 %collective-permute-done.4 = f32[384,256]{0,1:T(8,128)S(1)} collective-permute-done((f32[384,256]{0,1:T(8,128)}, f32[384,256]{0,1:T(8,128)S(1)}, u32[]{:S(2)}, u32[]{:S(2)}) %collective-permute-start.4) | collective-permute-done | bytes 393248 | tf_op jit(solution)/shard_map/while/body/eval_jaxpr/ppermute | solution.py:13
  209.8 2.8 collective-permute-start.2
  213.5 6.4 %collective-permute-start = (bf16[384,256]{0,1:T(8,128)(2,1)S(1)}, bf16[384,256]{0,1:T(8,128)(2,1)}, u32[]{:S(2)}, u32[]{:S(2)}) collective-permute-start(bf16[384,256]{0,1:T(8,128)(2,1)S(1)} %copy.72), channel_id=1, source_target_pairs={{0,1},{1,2},{2,3},{3,4},{4,5},{5,6},{6,7},{7,0},{8,9},{9,10},{10,1... | collective-permute-start | bytes 589832 | tf_op jit(solution)/shard_map/while/body/eval_jaxpr/ppermute | solution.py:13
  222.8 2.1 collective-permute-start.3
  228.6 2.9 collective-permute-start.4
  232.6 2.6 bitcast_add_fusion.6
  235.3 4.1 %collective-permute-done.4 = f32[384,256]{0,1:T(8,128)S(1)} collective-permute-done((f32[384,256]{0,1:T(8,128)}, f32[384,256]{0,1:T(8,128)S(1)}, u32[]{:S(2)}, u32[]{:S(2)}) %collective-permute-start.4) | collective-permute-done | bytes 393248 | tf_op jit(solution)/shard_map/while/body/eval_jaxpr/ppermute | solution.py:13
  239.4 2.9 collective-permute-start.2
  243.3 6.4 %collective-permute-start = (bf16[384,256]{0,1:T(8,128)(2,1)S(1)}, bf16[384,256]{0,1:T(8,128)(2,1)}, u32[]{:S(2)}, u32[]{:S(2)}) collective-permute-start(bf16[384,256]{0,1:T(8,128)(2,1)S(1)} %copy.72), channel_id=1, source_target_pairs={{0,1},{1,2},{2,3},{3,4},{4,5},{5,6},{6,7},{7,0},{8,9},{9,10},{10,1... | collective-permute-start | bytes 589832 | tf_op jit(solution)/shard_map/while/body/eval_jaxpr/ppermute | solution.py:13
  258.2 4.1 %collective-permute-start.4 = (f32[384,256]{0,1:T(8,128)}, f32[384,256]{0,1:T(8,128)S(1)}, u32[]{:S(2)}, u32[]{:S(2)}) collective-permute-start(f32[384,256]{0,1:T(8,128)} %bitcast_add_fusion.5), channel_id=1, source_target_pairs={{0,1},{1,2},{2,3},{3,4},{4,5},{5,6},{6,7},{7,0},{8,9},{9,10},{10,1... | collective-permute-start | bytes 1179656 | tf_op jit(solution)/shard_map/while/body/eval_jaxpr/ppermute | solution.py:13
  263.4 2.6 bitcast_add_fusion.6
  266.0 2.9 collective-permute-done.4
  269.0 5.9 %collective-permute-start.2 = (f32[2,384]{1,0:T(2,128)S(1)}, f32[2,384]{1,0:T(2,128)S(1)}, u32[]{:S(2)}, u32[]{:S(2)}) collective-permute-start(f32[2,384]{1,0:T(2,128)S(1)} %copy.74), channel_id=1, source_target_pairs={{0,1},{1,2},{2,3},{3,4},{4,5},{5,6},{6,7},{7,0},{8,9},{9,10},{10,1... | collective-permute-start | bytes 9224 | tf_op jit(solution)/shard_map/while/body/eval_jaxpr/ppermute | solution.py:13
  275.8 6.4 %collective-permute-start = (bf16[384,256]{0,1:T(8,128)(2,1)S(1)}, bf16[384,256]{0,1:T(8,128)(2,1)}, u32[]{:S(2)}, u32[]{:S(2)}) collective-permute-start(bf16[384,256]{0,1:T(8,128)(2,1)S(1)} %copy.72), channel_id=1, source_target_pairs={{0,1},{1,2},{2,3},{3,4},{4,5},{5,6},{6,7},{7,0},{8,9},{9,10},{10,1... | collective-permute-start | bytes 589832 | tf_op jit(solution)/shard_map/while/body/eval_jaxpr/ppermute | solution.py:13
  290.7 2.7 collective-permute-start.4
  294.4 2.6 bitcast_add_fusion.6
  297.1 6.5 %collective-permute-done.4 = f32[384,256]{0,1:T(8,128)S(1)} collective-permute-done((f32[384,256]{0,1:T(8,128)}, f32[384,256]{0,1:T(8,128)S(1)}, u32[]{:S(2)}, u32[]{:S(2)}) %collective-permute-start.4) | collective-permute-done | bytes 393248 | tf_op jit(solution)/shard_map/while/body/eval_jaxpr/ppermute | solution.py:13
  306.4 6.4 %collective-permute-start = (bf16[384,256]{0,1:T(8,128)(2,1)S(1)}, bf16[384,256]{0,1:T(8,128)(2,1)}, u32[]{:S(2)}, u32[]{:S(2)}) collective-permute-start(bf16[384,256]{0,1:T(8,128)(2,1)S(1)} %copy.72), channel_id=1, source_target_pairs={{0,1},{1,2},{2,3},{3,4},{4,5},{5,6},{6,7},{7,0},{8,9},{9,10},{10,1... | collective-permute-start | bytes 589832 | tf_op jit(solution)/shard_map/while/body/eval_jaxpr/ppermute | solution.py:13
  321.3 6.2 %collective-permute-start.4 = (f32[384,256]{0,1:T(8,128)}, f32[384,256]{0,1:T(8,128)S(1)}, u32[]{:S(2)}, u32[]{:S(2)}) collective-permute-start(f32[384,256]{0,1:T(8,128)} %bitcast_add_fusion.5), channel_id=1, source_target_pairs={{0,1},{1,2},{2,3},{3,4},{4,5},{5,6},{6,7},{7,0},{8,9},{9,10},{10,1... | collective-permute-start | bytes 1179656 | tf_op jit(solution)/shard_map/while/body/eval_jaxpr/ppermute | solution.py:13
  328.6 2.6 bitcast_add_fusion.6
  331.2 4.2 %collective-permute-done.4 = f32[384,256]{0,1:T(8,128)S(1)} collective-permute-done((f32[384,256]{0,1:T(8,128)}, f32[384,256]{0,1:T(8,128)S(1)}, u32[]{:S(2)}, u32[]{:S(2)}) %collective-permute-start.4) | collective-permute-done | bytes 393248 | tf_op jit(solution)/shard_map/while/body/eval_jaxpr/ppermute | solution.py:13
  335.5 5.8 %collective-permute-start.2 = (f32[2,384]{1,0:T(2,128)S(1)}, f32[2,384]{1,0:T(2,128)S(1)}, u32[]{:S(2)}, u32[]{:S(2)}) collective-permute-start(f32[2,384]{1,0:T(2,128)S(1)} %copy.74), channel_id=1, source_target_pairs={{0,1},{1,2},{2,3},{3,4},{4,5},{5,6},{6,7},{7,0},{8,9},{9,10},{10,1... | collective-permute-start | bytes 9224 | tf_op jit(solution)/shard_map/while/body/eval_jaxpr/ppermute | solution.py:13
  342.2 6.4 %collective-permute-start = (bf16[384,256]{0,1:T(8,128)(2,1)S(1)}, bf16[384,256]{0,1:T(8,128)(2,1)}, u32[]{:S(2)}, u32[]{:S(2)}) collective-permute-start(bf16[384,256]{0,1:T(8,128)(2,1)S(1)} %copy.72), channel_id=1, source_target_pairs={{0,1},{1,2},{2,3},{3,4},{4,5},{5,6},{6,7},{7,0},{8,9},{9,10},{10,1... | collective-permute-start | bytes 589832 | tf_op jit(solution)/shard_map/while/body/eval_jaxpr/ppermute | solution.py:13
  360.1 2.6 bitcast_add_fusion.6
  362.8 5.1 %collective-permute-done.4 = f32[384,256]{0,1:T(8,128)S(1)} collective-permute-done((f32[384,256]{0,1:T(8,128)}, f32[384,256]{0,1:T(8,128)S(1)}, u32[]{:S(2)}, u32[]{:S(2)}) %collective-permute-start.4) | collective-permute-done | bytes 393248 | tf_op jit(solution)/shard_map/while/body/eval_jaxpr/ppermute | solution.py:13
  371.6 8.2 %collective-permute-start.7 = (bf16[384,256]{1,0:T(8,128)(2,1)S(1)}, bf16[384,256]{1,0:T(8,128)(2,1)S(1)}, u32[]{:S(2)}, u32[]{:S(2)}) collective-permute-start(bf16[384,256]{1,0:T(8,128)(2,1)S(1)} %slice.31), channel_id=1, source_target_pairs={{0,504},{8,0},{16,8},{24,16},{32,24},{40,32},{48,40},{56,48},{64,5... | collective-permute-start | bytes 589832 | tf_op jit(solution)/shard_map/ppermute | solution.py:13
  (163 shorter events, 99.7 us)
Async XLA Ops:
  7.2 29.6 %copy-start.3 = (bf16[384,256]{1,0:T(8,128)(2,1)S(1)}, bf16[384,256]{1,0:T(8,128)(2,1)}, u32[]{:S(2)}) copy-start(bf16[384,256]{1,0:T(8,128)(2,1)} %param.9) | copy-start | bytes 589828
  7.2 23.4 %copy-start.2 = (bf16[384,256]{1,0:T(8,128)(2,1)S(1)}, bf16[384,256]{1,0:T(8,128)(2,1)}, u32[]{:S(2)}) copy-start(bf16[384,256]{1,0:T(8,128)(2,1)} %param.10) | copy-start | bytes 589828
  7.2 24.1 %copy-start.1 = (bf16[384,256]{1,0:T(8,128)(2,1)S(1)}, bf16[384,256]{1,0:T(8,128)(2,1)}, u32[]{:S(2)}) copy-start(bf16[384,256]{1,0:T(8,128)(2,1)} %param.7) | copy-start | bytes 589828
  7.2 92.3 %all-gather.2.cloned.1.call-start = ((), (), s32[]{:S(2)}) async-start(), calls=%async_computation | async-start | bytes 3538944 | tf_op jit(solution)/shard_map/all_gather | solution.py:69
  8.4 16.6 %collective-permute-start.5 = (bf16[384,256]{0,1:T(8,128)(2,1)S(1)}, bf16[384,256]{0,1:T(8,128)(2,1)S(1)}, u32[]{:S(2)}, u32[]{:S(2)}) collective-permute-start(bf16[384,256]{0,1:T(8,128)(2,1)S(1)} %copy.27), channel_id=1, source_target_pairs={{0,8},{8,16},{16,24},{24,32},{32,40},{40,48},{48,56},{56,64},{64,7... | collective-permute-start | bytes 589832 | tf_op jit(solution)/shard_map/ppermute | solution.py:13
  25.9 10.8 %collective-permute-start.6 = (bf16[384,256]{1,0:T(8,128)(2,1)}, bf16[384,256]{1,0:T(8,128)(2,1)S(1)}, u32[]{:S(2)}, u32[]{:S(2)}) collective-permute-start(bf16[384,256]{1,0:T(8,128)(2,1)} %param.9), channel_id=1, source_target_pairs={{0,8},{8,16},{16,24},{24,32},{32,40},{40,48},{48,56},{56,64},{64,7... | collective-permute-start | bytes 589832 | tf_op jit(solution)/shard_map/ppermute | solution.py:13
  120.5 24.1 %collective-permute-start.2 = (f32[2,384]{1,0:T(2,128)S(1)}, f32[2,384]{1,0:T(2,128)S(1)}, u32[]{:S(2)}, u32[]{:S(2)}) collective-permute-start(f32[2,384]{1,0:T(2,128)S(1)} %copy.74), channel_id=1, source_target_pairs={{0,1},{1,2},{2,3},{3,4},{4,5},{5,6},{6,7},{7,0},{8,9},{9,10},{10,1... | collective-permute-start | bytes 9224 | tf_op jit(solution)/shard_map/while/body/eval_jaxpr/ppermute | solution.py:13
  123.6 21.0 %collective-permute-start = (bf16[384,256]{0,1:T(8,128)(2,1)S(1)}, bf16[384,256]{0,1:T(8,128)(2,1)}, u32[]{:S(2)}, u32[]{:S(2)}) collective-permute-start(bf16[384,256]{0,1:T(8,128)(2,1)S(1)} %copy.72), channel_id=1, source_target_pairs={{0,1},{1,2},{2,3},{3,4},{4,5},{5,6},{6,7},{7,0},{8,9},{9,10},{10,1... | collective-permute-start | bytes 589832 | tf_op jit(solution)/shard_map/while/body/eval_jaxpr/ppermute | solution.py:13
  129.5 15.1 %collective-permute-start.1 = (bf16[384,256]{0,1:T(8,128)(2,1)S(1)}, bf16[384,256]{0,1:T(8,128)(2,1)}, u32[]{:S(2)}, u32[]{:S(2)}) collective-permute-start(bf16[384,256]{0,1:T(8,128)(2,1)S(1)} %copy.73), channel_id=1, source_target_pairs={{0,1},{1,2},{2,3},{3,4},{4,5},{5,6},{6,7},{7,0},{8,9},{9,10},{10,1... | collective-permute-start | bytes 589832 | tf_op jit(solution)/shard_map/while/body/eval_jaxpr/ppermute | solution.py:13
  131.5 13.1 %collective-permute-start.3 = (f32[2,384]{1,0:T(2,128)S(1)}, f32[2,384]{1,0:T(2,128)S(1)}, u32[]{:S(2)}, u32[]{:S(2)}) collective-permute-start(f32[2,384]{1,0:T(2,128)S(1)} %copy.75), channel_id=1, source_target_pairs={{0,1},{1,2},{2,3},{3,4},{4,5},{5,6},{6,7},{7,0},{8,9},{9,10},{10,1... | collective-permute-start | bytes 9224 | tf_op jit(solution)/shard_map/while/body/eval_jaxpr/ppermute | solution.py:13
  138.6 12.7 %collective-permute-start.4 = (f32[384,256]{0,1:T(8,128)}, f32[384,256]{0,1:T(8,128)S(1)}, u32[]{:S(2)}, u32[]{:S(2)}) collective-permute-start(f32[384,256]{0,1:T(8,128)} %bitcast_add_fusion.5), channel_id=1, source_target_pairs={{0,1},{1,2},{2,3},{3,4},{4,5},{5,6},{6,7},{7,0},{8,9},{9,10},{10,1... | collective-permute-start | bytes 1179656 | tf_op jit(solution)/shard_map/while/body/eval_jaxpr/ppermute | solution.py:13
  151.3 24.4 %collective-permute-start.2 = (f32[2,384]{1,0:T(2,128)S(1)}, f32[2,384]{1,0:T(2,128)S(1)}, u32[]{:S(2)}, u32[]{:S(2)}) collective-permute-start(f32[2,384]{1,0:T(2,128)S(1)} %copy.74), channel_id=1, source_target_pairs={{0,1},{1,2},{2,3},{3,4},{4,5},{5,6},{6,7},{7,0},{8,9},{9,10},{10,1... | collective-permute-start | bytes 9224 | tf_op jit(solution)/shard_map/while/body/eval_jaxpr/ppermute | solution.py:13
  154.7 21.0 %collective-permute-start = (bf16[384,256]{0,1:T(8,128)(2,1)S(1)}, bf16[384,256]{0,1:T(8,128)(2,1)}, u32[]{:S(2)}, u32[]{:S(2)}) collective-permute-start(bf16[384,256]{0,1:T(8,128)(2,1)S(1)} %copy.72), channel_id=1, source_target_pairs={{0,1},{1,2},{2,3},{3,4},{4,5},{5,6},{6,7},{7,0},{8,9},{9,10},{10,1... | collective-permute-start | bytes 589832 | tf_op jit(solution)/shard_map/while/body/eval_jaxpr/ppermute | solution.py:13
  161.1 14.6 %collective-permute-start.1 = (bf16[384,256]{0,1:T(8,128)(2,1)S(1)}, bf16[384,256]{0,1:T(8,128)(2,1)}, u32[]{:S(2)}, u32[]{:S(2)}) collective-permute-start(bf16[384,256]{0,1:T(8,128)(2,1)S(1)} %copy.73), channel_id=1, source_target_pairs={{0,1},{1,2},{2,3},{3,4},{4,5},{5,6},{6,7},{7,0},{8,9},{9,10},{10,1... | collective-permute-start | bytes 589832 | tf_op jit(solution)/shard_map/while/body/eval_jaxpr/ppermute | solution.py:13
  163.1 12.7 %collective-permute-start.3 = (f32[2,384]{1,0:T(2,128)S(1)}, f32[2,384]{1,0:T(2,128)S(1)}, u32[]{:S(2)}, u32[]{:S(2)}) collective-permute-start(f32[2,384]{1,0:T(2,128)S(1)} %copy.75), channel_id=1, source_target_pairs={{0,1},{1,2},{2,3},{3,4},{4,5},{5,6},{6,7},{7,0},{8,9},{9,10},{10,1... | collective-permute-start | bytes 9224 | tf_op jit(solution)/shard_map/while/body/eval_jaxpr/ppermute | solution.py:13
  170.1 10.8 %collective-permute-start.4 = (f32[384,256]{0,1:T(8,128)}, f32[384,256]{0,1:T(8,128)S(1)}, u32[]{:S(2)}, u32[]{:S(2)}) collective-permute-start(f32[384,256]{0,1:T(8,128)} %bitcast_add_fusion.5), channel_id=1, source_target_pairs={{0,1},{1,2},{2,3},{3,4},{4,5},{5,6},{6,7},{7,0},{8,9},{9,10},{10,1... | collective-permute-start | bytes 1179656 | tf_op jit(solution)/shard_map/while/body/eval_jaxpr/ppermute | solution.py:13
  180.9 24.6 %collective-permute-start.2 = (f32[2,384]{1,0:T(2,128)S(1)}, f32[2,384]{1,0:T(2,128)S(1)}, u32[]{:S(2)}, u32[]{:S(2)}) collective-permute-start(f32[2,384]{1,0:T(2,128)S(1)} %copy.74), channel_id=1, source_target_pairs={{0,1},{1,2},{2,3},{3,4},{4,5},{5,6},{6,7},{7,0},{8,9},{9,10},{10,1... | collective-permute-start | bytes 9224 | tf_op jit(solution)/shard_map/while/body/eval_jaxpr/ppermute | solution.py:13
  183.8 21.7 %collective-permute-start = (bf16[384,256]{0,1:T(8,128)(2,1)S(1)}, bf16[384,256]{0,1:T(8,128)(2,1)}, u32[]{:S(2)}, u32[]{:S(2)}) collective-permute-start(bf16[384,256]{0,1:T(8,128)(2,1)S(1)} %copy.72), channel_id=1, source_target_pairs={{0,1},{1,2},{2,3},{3,4},{4,5},{5,6},{6,7},{7,0},{8,9},{9,10},{10,1... | collective-permute-start | bytes 589832 | tf_op jit(solution)/shard_map/while/body/eval_jaxpr/ppermute | solution.py:13
  190.9 14.6 %collective-permute-start.1 = (bf16[384,256]{0,1:T(8,128)(2,1)S(1)}, bf16[384,256]{0,1:T(8,128)(2,1)}, u32[]{:S(2)}, u32[]{:S(2)}) collective-permute-start(bf16[384,256]{0,1:T(8,128)(2,1)S(1)} %copy.73), channel_id=1, source_target_pairs={{0,1},{1,2},{2,3},{3,4},{4,5},{5,6},{6,7},{7,0},{8,9},{9,10},{10,1... | collective-permute-start | bytes 589832 | tf_op jit(solution)/shard_map/while/body/eval_jaxpr/ppermute | solution.py:13
  192.8 12.7 %collective-permute-start.3 = (f32[2,384]{1,0:T(2,128)S(1)}, f32[2,384]{1,0:T(2,128)S(1)}, u32[]{:S(2)}, u32[]{:S(2)}) collective-permute-start(f32[2,384]{1,0:T(2,128)S(1)} %copy.75), channel_id=1, source_target_pairs={{0,1},{1,2},{2,3},{3,4},{4,5},{5,6},{6,7},{7,0},{8,9},{9,10},{10,1... | collective-permute-start | bytes 9224 | tf_op jit(solution)/shard_map/while/body/eval_jaxpr/ppermute | solution.py:13
  199.0 10.8 %collective-permute-start.4 = (f32[384,256]{0,1:T(8,128)}, f32[384,256]{0,1:T(8,128)S(1)}, u32[]{:S(2)}, u32[]{:S(2)}) collective-permute-start(f32[384,256]{0,1:T(8,128)} %bitcast_add_fusion.5), channel_id=1, source_target_pairs={{0,1},{1,2},{2,3},{3,4},{4,5},{5,6},{6,7},{7,0},{8,9},{9,10},{10,1... | collective-permute-start | bytes 1179656 | tf_op jit(solution)/shard_map/while/body/eval_jaxpr/ppermute | solution.py:13
  209.8 25.5 %collective-permute-start.2 = (f32[2,384]{1,0:T(2,128)S(1)}, f32[2,384]{1,0:T(2,128)S(1)}, u32[]{:S(2)}, u32[]{:S(2)}) collective-permute-start(f32[2,384]{1,0:T(2,128)S(1)} %copy.74), channel_id=1, source_target_pairs={{0,1},{1,2},{2,3},{3,4},{4,5},{5,6},{6,7},{7,0},{8,9},{9,10},{10,1... | collective-permute-start | bytes 9224 | tf_op jit(solution)/shard_map/while/body/eval_jaxpr/ppermute | solution.py:13
  213.5 21.7 %collective-permute-start = (bf16[384,256]{0,1:T(8,128)(2,1)S(1)}, bf16[384,256]{0,1:T(8,128)(2,1)}, u32[]{:S(2)}, u32[]{:S(2)}) collective-permute-start(bf16[384,256]{0,1:T(8,128)(2,1)S(1)} %copy.72), channel_id=1, source_target_pairs={{0,1},{1,2},{2,3},{3,4},{4,5},{5,6},{6,7},{7,0},{8,9},{9,10},{10,1... | collective-permute-start | bytes 589832 | tf_op jit(solution)/shard_map/while/body/eval_jaxpr/ppermute | solution.py:13
  220.8 14.4 %collective-permute-start.1 = (bf16[384,256]{0,1:T(8,128)(2,1)S(1)}, bf16[384,256]{0,1:T(8,128)(2,1)}, u32[]{:S(2)}, u32[]{:S(2)}) collective-permute-start(bf16[384,256]{0,1:T(8,128)(2,1)S(1)} %copy.73), channel_id=1, source_target_pairs={{0,1},{1,2},{2,3},{3,4},{4,5},{5,6},{6,7},{7,0},{8,9},{9,10},{10,1... | collective-permute-start | bytes 589832 | tf_op jit(solution)/shard_map/while/body/eval_jaxpr/ppermute | solution.py:13
  222.8 12.5 %collective-permute-start.3 = (f32[2,384]{1,0:T(2,128)S(1)}, f32[2,384]{1,0:T(2,128)S(1)}, u32[]{:S(2)}, u32[]{:S(2)}) collective-permute-start(f32[2,384]{1,0:T(2,128)S(1)} %copy.75), channel_id=1, source_target_pairs={{0,1},{1,2},{2,3},{3,4},{4,5},{5,6},{6,7},{7,0},{8,9},{9,10},{10,1... | collective-permute-start | bytes 9224 | tf_op jit(solution)/shard_map/while/body/eval_jaxpr/ppermute | solution.py:13
  228.6 10.8 %collective-permute-start.4 = (f32[384,256]{0,1:T(8,128)}, f32[384,256]{0,1:T(8,128)S(1)}, u32[]{:S(2)}, u32[]{:S(2)}) collective-permute-start(f32[384,256]{0,1:T(8,128)} %bitcast_add_fusion.5), channel_id=1, source_target_pairs={{0,1},{1,2},{2,3},{3,4},{4,5},{5,6},{6,7},{7,0},{8,9},{9,10},{10,1... | collective-permute-start | bytes 1179656 | tf_op jit(solution)/shard_map/while/body/eval_jaxpr/ppermute | solution.py:13
  239.4 26.6 %collective-permute-start.2 = (f32[2,384]{1,0:T(2,128)S(1)}, f32[2,384]{1,0:T(2,128)S(1)}, u32[]{:S(2)}, u32[]{:S(2)}) collective-permute-start(f32[2,384]{1,0:T(2,128)S(1)} %copy.74), channel_id=1, source_target_pairs={{0,1},{1,2},{2,3},{3,4},{4,5},{5,6},{6,7},{7,0},{8,9},{9,10},{10,1... | collective-permute-start | bytes 9224 | tf_op jit(solution)/shard_map/while/body/eval_jaxpr/ppermute | solution.py:13
  243.3 22.7 %collective-permute-start = (bf16[384,256]{0,1:T(8,128)(2,1)S(1)}, bf16[384,256]{0,1:T(8,128)(2,1)}, u32[]{:S(2)}, u32[]{:S(2)}) collective-permute-start(bf16[384,256]{0,1:T(8,128)(2,1)S(1)} %copy.72), channel_id=1, source_target_pairs={{0,1},{1,2},{2,3},{3,4},{4,5},{5,6},{6,7},{7,0},{8,9},{9,10},{10,1... | collective-permute-start | bytes 589832 | tf_op jit(solution)/shard_map/while/body/eval_jaxpr/ppermute | solution.py:13
  250.6 15.4 %collective-permute-start.1 = (bf16[384,256]{0,1:T(8,128)(2,1)S(1)}, bf16[384,256]{0,1:T(8,128)(2,1)}, u32[]{:S(2)}, u32[]{:S(2)}) collective-permute-start(bf16[384,256]{0,1:T(8,128)(2,1)S(1)} %copy.73), channel_id=1, source_target_pairs={{0,1},{1,2},{2,3},{3,4},{4,5},{5,6},{6,7},{7,0},{8,9},{9,10},{10,1... | collective-permute-start | bytes 589832 | tf_op jit(solution)/shard_map/while/body/eval_jaxpr/ppermute | solution.py:13
  252.5 13.5 %collective-permute-start.3 = (f32[2,384]{1,0:T(2,128)S(1)}, f32[2,384]{1,0:T(2,128)S(1)}, u32[]{:S(2)}, u32[]{:S(2)}) collective-permute-start(f32[2,384]{1,0:T(2,128)S(1)} %copy.75), channel_id=1, source_target_pairs={{0,1},{1,2},{2,3},{3,4},{4,5},{5,6},{6,7},{7,0},{8,9},{9,10},{10,1... | collective-permute-start | bytes 9224 | tf_op jit(solution)/shard_map/while/body/eval_jaxpr/ppermute | solution.py:13
  258.2 10.8 %collective-permute-start.4 = (f32[384,256]{0,1:T(8,128)}, f32[384,256]{0,1:T(8,128)S(1)}, u32[]{:S(2)}, u32[]{:S(2)}) collective-permute-start(f32[384,256]{0,1:T(8,128)} %bitcast_add_fusion.5), channel_id=1, source_target_pairs={{0,1},{1,2},{2,3},{3,4},{4,5},{5,6},{6,7},{7,0},{8,9},{9,10},{10,1... | collective-permute-start | bytes 1179656 | tf_op jit(solution)/shard_map/while/body/eval_jaxpr/ppermute | solution.py:13
  269.0 28.1 %collective-permute-start.2 = (f32[2,384]{1,0:T(2,128)S(1)}, f32[2,384]{1,0:T(2,128)S(1)}, u32[]{:S(2)}, u32[]{:S(2)}) collective-permute-start(f32[2,384]{1,0:T(2,128)S(1)} %copy.74), channel_id=1, source_target_pairs={{0,1},{1,2},{2,3},{3,4},{4,5},{5,6},{6,7},{7,0},{8,9},{9,10},{10,1... | collective-permute-start | bytes 9224 | tf_op jit(solution)/shard_map/while/body/eval_jaxpr/ppermute | solution.py:13
  275.8 21.3 %collective-permute-start = (bf16[384,256]{0,1:T(8,128)(2,1)S(1)}, bf16[384,256]{0,1:T(8,128)(2,1)}, u32[]{:S(2)}, u32[]{:S(2)}) collective-permute-start(bf16[384,256]{0,1:T(8,128)(2,1)S(1)} %copy.72), channel_id=1, source_target_pairs={{0,1},{1,2},{2,3},{3,4},{4,5},{5,6},{6,7},{7,0},{8,9},{9,10},{10,1... | collective-permute-start | bytes 589832 | tf_op jit(solution)/shard_map/while/body/eval_jaxpr/ppermute | solution.py:13
  283.1 13.9 %collective-permute-start.1 = (bf16[384,256]{0,1:T(8,128)(2,1)S(1)}, bf16[384,256]{0,1:T(8,128)(2,1)}, u32[]{:S(2)}, u32[]{:S(2)}) collective-permute-start(bf16[384,256]{0,1:T(8,128)(2,1)S(1)} %copy.73), channel_id=1, source_target_pairs={{0,1},{1,2},{2,3},{3,4},{4,5},{5,6},{6,7},{7,0},{8,9},{9,10},{10,1... | collective-permute-start | bytes 589832 | tf_op jit(solution)/shard_map/while/body/eval_jaxpr/ppermute | solution.py:13
  285.0 12.0 %collective-permute-start.3 = (f32[2,384]{1,0:T(2,128)S(1)}, f32[2,384]{1,0:T(2,128)S(1)}, u32[]{:S(2)}, u32[]{:S(2)}) collective-permute-start(f32[2,384]{1,0:T(2,128)S(1)} %copy.75), channel_id=1, source_target_pairs={{0,1},{1,2},{2,3},{3,4},{4,5},{5,6},{6,7},{7,0},{8,9},{9,10},{10,1... | collective-permute-start | bytes 9224 | tf_op jit(solution)/shard_map/while/body/eval_jaxpr/ppermute | solution.py:13
  290.7 12.9 %collective-permute-start.4 = (f32[384,256]{0,1:T(8,128)}, f32[384,256]{0,1:T(8,128)S(1)}, u32[]{:S(2)}, u32[]{:S(2)}) collective-permute-start(f32[384,256]{0,1:T(8,128)} %bitcast_add_fusion.5), channel_id=1, source_target_pairs={{0,1},{1,2},{2,3},{3,4},{4,5},{5,6},{6,7},{7,0},{8,9},{9,10},{10,1... | collective-permute-start | bytes 1179656 | tf_op jit(solution)/shard_map/while/body/eval_jaxpr/ppermute | solution.py:13
  303.6 27.7 %collective-permute-start.2 = (f32[2,384]{1,0:T(2,128)S(1)}, f32[2,384]{1,0:T(2,128)S(1)}, u32[]{:S(2)}, u32[]{:S(2)}) collective-permute-start(f32[2,384]{1,0:T(2,128)S(1)} %copy.74), channel_id=1, source_target_pairs={{0,1},{1,2},{2,3},{3,4},{4,5},{5,6},{6,7},{7,0},{8,9},{9,10},{10,1... | collective-permute-start | bytes 9224 | tf_op jit(solution)/shard_map/while/body/eval_jaxpr/ppermute | solution.py:13
  306.4 24.8 %collective-permute-start = (bf16[384,256]{0,1:T(8,128)(2,1)S(1)}, bf16[384,256]{0,1:T(8,128)(2,1)}, u32[]{:S(2)}, u32[]{:S(2)}) collective-permute-start(bf16[384,256]{0,1:T(8,128)(2,1)S(1)} %copy.72), channel_id=1, source_target_pairs={{0,1},{1,2},{2,3},{3,4},{4,5},{5,6},{6,7},{7,0},{8,9},{9,10},{10,1... | collective-permute-start | bytes 589832 | tf_op jit(solution)/shard_map/while/body/eval_jaxpr/ppermute | solution.py:13
  313.7 17.5 %collective-permute-start.1 = (bf16[384,256]{0,1:T(8,128)(2,1)S(1)}, bf16[384,256]{0,1:T(8,128)(2,1)}, u32[]{:S(2)}, u32[]{:S(2)}) collective-permute-start(bf16[384,256]{0,1:T(8,128)(2,1)S(1)} %copy.73), channel_id=1, source_target_pairs={{0,1},{1,2},{2,3},{3,4},{4,5},{5,6},{6,7},{7,0},{8,9},{9,10},{10,1... | collective-permute-start | bytes 589832 | tf_op jit(solution)/shard_map/while/body/eval_jaxpr/ppermute | solution.py:13
  315.6 15.6 %collective-permute-start.3 = (f32[2,384]{1,0:T(2,128)S(1)}, f32[2,384]{1,0:T(2,128)S(1)}, u32[]{:S(2)}, u32[]{:S(2)}) collective-permute-start(f32[2,384]{1,0:T(2,128)S(1)} %copy.75), channel_id=1, source_target_pairs={{0,1},{1,2},{2,3},{3,4},{4,5},{5,6},{6,7},{7,0},{8,9},{9,10},{10,1... | collective-permute-start | bytes 9224 | tf_op jit(solution)/shard_map/while/body/eval_jaxpr/ppermute | solution.py:13
  321.3 14.2 %collective-permute-start.4 = (f32[384,256]{0,1:T(8,128)}, f32[384,256]{0,1:T(8,128)S(1)}, u32[]{:S(2)}, u32[]{:S(2)}) collective-permute-start(f32[384,256]{0,1:T(8,128)} %bitcast_add_fusion.5), channel_id=1, source_target_pairs={{0,1},{1,2},{2,3},{3,4},{4,5},{5,6},{6,7},{7,0},{8,9},{9,10},{10,1... | collective-permute-start | bytes 1179656 | tf_op jit(solution)/shard_map/while/body/eval_jaxpr/ppermute | solution.py:13
  335.5 27.3 %collective-permute-start.2 = (f32[2,384]{1,0:T(2,128)S(1)}, f32[2,384]{1,0:T(2,128)S(1)}, u32[]{:S(2)}, u32[]{:S(2)}) collective-permute-start(f32[2,384]{1,0:T(2,128)S(1)} %copy.74), channel_id=1, source_target_pairs={{0,1},{1,2},{2,3},{3,4},{4,5},{5,6},{6,7},{7,0},{8,9},{9,10},{10,1... | collective-permute-start | bytes 9224 | tf_op jit(solution)/shard_map/while/body/eval_jaxpr/ppermute | solution.py:13
  342.2 20.5 %collective-permute-start = (bf16[384,256]{0,1:T(8,128)(2,1)S(1)}, bf16[384,256]{0,1:T(8,128)(2,1)}, u32[]{:S(2)}, u32[]{:S(2)}) collective-permute-start(bf16[384,256]{0,1:T(8,128)(2,1)S(1)} %copy.72), channel_id=1, source_target_pairs={{0,1},{1,2},{2,3},{3,4},{4,5},{5,6},{6,7},{7,0},{8,9},{9,10},{10,1... | collective-permute-start | bytes 589832 | tf_op jit(solution)/shard_map/while/body/eval_jaxpr/ppermute | solution.py:13
  349.6 13.2 %collective-permute-start.1 = (bf16[384,256]{0,1:T(8,128)(2,1)S(1)}, bf16[384,256]{0,1:T(8,128)(2,1)}, u32[]{:S(2)}, u32[]{:S(2)}) collective-permute-start(bf16[384,256]{0,1:T(8,128)(2,1)S(1)} %copy.73), channel_id=1, source_target_pairs={{0,1},{1,2},{2,3},{3,4},{4,5},{5,6},{6,7},{7,0},{8,9},{9,10},{10,1... | collective-permute-start | bytes 589832 | tf_op jit(solution)/shard_map/while/body/eval_jaxpr/ppermute | solution.py:13
  351.5 11.3 %collective-permute-start.3 = (f32[2,384]{1,0:T(2,128)S(1)}, f32[2,384]{1,0:T(2,128)S(1)}, u32[]{:S(2)}, u32[]{:S(2)}) collective-permute-start(f32[2,384]{1,0:T(2,128)S(1)} %copy.75), channel_id=1, source_target_pairs={{0,1},{1,2},{2,3},{3,4},{4,5},{5,6},{6,7},{7,0},{8,9},{9,10},{10,1... | collective-permute-start | bytes 9224 | tf_op jit(solution)/shard_map/while/body/eval_jaxpr/ppermute | solution.py:13
  357.1 10.8 %collective-permute-start.4 = (f32[384,256]{0,1:T(8,128)}, f32[384,256]{0,1:T(8,128)S(1)}, u32[]{:S(2)}, u32[]{:S(2)}) collective-permute-start(f32[384,256]{0,1:T(8,128)} %bitcast_add_fusion.5), channel_id=1, source_target_pairs={{0,1},{1,2},{2,3},{3,4},{4,5},{5,6},{6,7},{7,0},{8,9},{9,10},{10,1... | collective-permute-start | bytes 1179656 | tf_op jit(solution)/shard_map/while/body/eval_jaxpr/ppermute | solution.py:13
  369.3 11.3 %collective-permute-start.8 = (bf16[384,256]{1,0:T(8,128)(2,1)S(1)}, bf16[384,256]{1,0:T(8,128)(2,1)S(1)}, u32[]{:S(2)}, u32[]{:S(2)}) collective-permute-start(bf16[384,256]{1,0:T(8,128)(2,1)S(1)} %slice.30), channel_id=1, source_target_pairs={{0,504},{8,0},{16,8},{24,16},{32,24},{40,32},{48,40},{56,48},{64,5... | collective-permute-start | bytes 589832 | tf_op jit(solution)/shard_map/ppermute | solution.py:13
  371.6 11.4 %collective-permute-start.7 = (bf16[384,256]{1,0:T(8,128)(2,1)S(1)}, bf16[384,256]{1,0:T(8,128)(2,1)S(1)}, u32[]{:S(2)}, u32[]{:S(2)}) collective-permute-start(bf16[384,256]{1,0:T(8,128)(2,1)S(1)} %slice.31), channel_id=1, source_target_pairs={{0,504},{8,0},{16,8},{24,16},{32,24},{40,32},{48,40},{56,48},{64,5... | collective-permute-start | bytes 589832 | tf_op jit(solution)/shard_map/ppermute | solution.py:13
  (1 other events, 9.5 us)
Sparse Core Ops, SparseCore 0:
  26.0 73.4 all-gather.1
where the time goes:
time: 396 us; the launch traced here: 391 us
  starting transfers between devices  149 us (38%)
  waiting for transfers between devices  122 us (31%)
  matrix products  43 us (11%)
  other arithmetic  39.3 us (10%)
  local copies, waits for them, and re-layouts  22.3 us (6%)
  between operations  14.2 us (4%)
    ppermute x44, starting transfers between devices, passed_along(): return lax.ppermute(value, axis, pairs)  149 us
    all_gather x1, waiting for transfers between devices, on_device(): lax.all_gather(window_keys, 'inner', axis=0, tiled=True)  62 us
    ppermute x44, waiting for transfers between devices, passed_along(): return lax.ppermute(value, axis, pairs)  60.1 us
    add x8, other arithmetic, query_turn(): value_acc + grad_value  19.9 us
    dot_general x9, matrix products, scores_of(): jnp.einsum('qhd,khd->hqk', query_heads, split_heads(key_block), preferred...  15.4 us
    dot_general x8, matrix products, tile_grads(): jnp.einsum('qhd,khd->hqk', grad_heads, split_heads(value_block), preferre...  15.3 us
    while x32, local copies, waits for them, and re-layouts  14.9 us
    reduce_sum x1, other arithmetic, on_device(): total = jnp.sum(jnp.exp(scores - newest[:, :, None]), axis=2)  9.48 us
  transfers between devices with their start and end apart: 45, of which 12 were waited for; matrix products, arithmetic and copies ran while one was open for 20% of the time, Pallas kernels for 0%

commit v1 on v0

v1 whole, which is shorter than its diff:
```python
import functools

import jax
import jax.numpy as jnp
from jax import lax
from jax.experimental import pallas as pl
from jax.experimental.pallas import tpu as pltpu
from jax.sharding import PartitionSpec as P

R = 384
D = 128
SCALE = D ** -0.5
C = SCALE * 1.4426950408889634
NK = 1536
F32 = jnp.float32
BF = jnp.bfloat16
MB = 1024 * 1024
VM = pl.BlockSpec(memory_space=pltpu.VMEM)


def dot(a, b, ca, cb):
    return lax.dot_general(a, b, (((ca,), (cb,)), ((), ())), preferred_element_type=F32)


def params(mb):
    return pltpu.CompilerParams(vmem_limit_bytes=mb * MB)


def prep_body(q, k, v, o, g, qg, kv):
    def t(x):
        return x[...].astype(F32).T
    gt = t(g)
    qg[0:256] = t(q).astype(BF)
    qg[256:512] = gt.astype(BF)
    kv[0:256] = t(k).astype(BF)
    kv[256:512] = t(v).astype(BF)
    prod = gt * t(o)
    parts = []
    for h in range(2):
        d = jnp.sum(prod[h * D:(h + 1) * D], axis=0, keepdims=True)
        hi = d.astype(BF).astype(F32)
        mid = (d - hi).astype(BF).astype(F32)
        parts += [hi, mid, d - hi - mid]
    qg[512:528] = jnp.concatenate(parts + [jnp.zeros((10, R), F32)], axis=0).astype(BF)


def prep(q, k, v, o, g):
    return pl.pallas_call(
        prep_body,
        out_shape=[jax.ShapeDtypeStruct((528, R), BF), jax.ShapeDtypeStruct((512, R), BF)],
        name="pack",
    )(q, k, v, o, g)


def gather_keys(dst, refs, h, base):
    for n, ref in enumerate(refs):
        dst[h, 0:D, n * R:(n + 1) * R] = ref[base + h * D:base + (h + 1) * D, :]


def k1_body(*refs):
    qg, kv = refs[0:4], refs[4:8]
    p_ref, st_ref, ks, st = refs[8:]
    for h in range(2):
        gather_keys(ks, kv, h, 0)
    for n in range(4):
        for h in range(2):
            s = dot(qg[n][h * D:(h + 1) * D, :], ks[h], 0, 0)
            m = jnp.max(s, axis=1, keepdims=True) * C
            p = jnp.exp2(s * C - m)
            st[n * R:(n + 1) * R, 2 * h:2 * h + 1] = m
            st[n * R:(n + 1) * R, 2 * h + 1:2 * h + 2] = jnp.sum(p, axis=1, keepdims=True)
            p_ref[h, n * R:(n + 1) * R, :] = p.astype(BF)
    st_ref[...] = st[...].T[0:8, :]


BIG = pltpu.VMEM((2, 1536, NK), BF)


def stage1(qg, kv):
    return pl.pallas_call(
        k1_body,
        in_specs=[VM] * 8,
        out_specs=[VM, VM],
        out_shape=[BIG, jax.ShapeDtypeStruct((8, 1536), F32)],
        scratch_shapes=[pltpu.VMEM((2, D, NK), BF), pltpu.VMEM((1536, D), F32)],
        compiler_params=params(30),
        name="scores",
    )(*qg, *kv)


def k2_body(*refs):
    qg, kv, p_ref, ds_ref = refs[0:4], refs[4:8], refs[8], refs[9]
    out = refs[10:14]
    ks, vs, gs = refs[14:]
    row = lax.broadcasted_iota(jnp.int32, (16, NK), 0)
    for h in range(2):
        gather_keys(ks, kv, h, 0)
        gather_keys(vs, kv, h, 256)
        vs[h, D:D + 16, :] = jnp.where((row >= 3 * h) & (row < 3 * h + 3), -1.0, 0.0).astype(BF)
    for n in range(4):
        for h in range(2):
            gs[n, h, 0:D, :] = qg[n][256 + h * D:256 + (h + 1) * D, :]
            gs[n, h, D:D + 16, :] = qg[n][512:528, :]
            pg = dot(gs[n, h], vs[h], 0, 0)
            ds = (p_ref[h, n * R:(n + 1) * R, :].astype(F32) * pg).astype(BF)
            ds_ref[h, n * R:(n + 1) * R, :] = ds
            out[n][:, h * D:(h + 1) * D] = dot(ds, ks[h], 1, 1).astype(BF)


def stage2(qg, kv, p):
    return pl.pallas_call(
        k2_body,
        in_specs=[VM] * 9,
        out_specs=[VM] * 5,
        out_shape=[BIG] + [jax.ShapeDtypeStruct((R, 2 * D), BF)] * 4,
        scratch_shapes=[pltpu.VMEM((2, D, NK), BF), pltpu.VMEM((2, D + 16, NK), BF), pltpu.VMEM((4, 2, D + 16, R), BF)],
        compiler_params=params(30),
        name="score_grads",
    )(*qg, *kv, p)


REL = (0, 1, 3, 2)


def chunk_of(sender, n):
    return REL.index((REL[n] - REL[sender]) % 4)


def factors(stats, h, n):
    ms, ls = [], []
    for sender, ref in enumerate(stats):
        c = chunk_of(sender, n)
        ms.append(ref[2 * h:2 * h + 1, c * R:(c + 1) * R])
        ls.append(ref[2 * h + 1:2 * h + 2, c * R:(c + 1) * R])
    top = functools.reduce(jnp.maximum, ms)
    scaled = [jnp.exp2(m - top) for m in ms]
    total = sum(l * e for l, e in zip(ls, scaled))
    return [e / total for e in scaled]


def k3_body(*refs):
    qg, st, p_ref, ds_ref = refs[0:4], refs[4:8], refs[8], refs[9]
    prior, own = refs[10:12]
    xs = refs[12]
    for h in range(2):
        for n in range(4):
            fn = factors(st, h, n)[0]
            xs[h, 0, :, n * R:(n + 1) * R] = (qg[n][h * D:(h + 1) * D, :].astype(F32) * (fn * SCALE)).astype(BF)
            xs[h, 1, :, n * R:(n + 1) * R] = (qg[n][256 + h * D:256 + (h + 1) * D, :].astype(F32) * fn).astype(BF)
    for out, cols in ((prior, slice(768, 1536)), (own, slice(0, 768))):
        for h in range(2):
            out[h * D:(h + 1) * D, :] = dot(xs[h, 0], ds_ref[h, :, cols], 1, 0).astype(out.dtype)
            out[256 + h * D:256 + (h + 1) * D, :] = dot(xs[h, 1], p_ref[h, :, cols], 1, 0).astype(out.dtype)


def stage3(qg, stats, p, ds):
    return pl.pallas_call(
        k3_body,
        in_specs=[VM] * 10,
        out_specs=[VM] * 2,
        out_shape=[jax.ShapeDtypeStruct((512, 768), BF), jax.ShapeDtypeStruct((512, 768), F32)],
        scratch_shapes=[pltpu.VMEM((2, 2, D, 1536), BF)],
        compiler_params=params(30),
        name="key_grads",
    )(*qg, *stats, p, ds)


def query_sum_body(a0, a1, a2, a3, s0, s1, s2, s3, out):
    parts = (a0, a1, a2, a3)
    rows = []
    for h in range(2):
        rows += factors((s0, s1, s2, s3), h, 0)
    cols = jnp.concatenate(rows, axis=0).T
    for h in range(2):
        cut = slice(h * D, (h + 1) * D)
        total = sum(parts[n][:, cut].astype(F32) * cols[:, 4 * h + n:4 * h + n + 1] for n in range(4))
        out[:, cut] = (total * SCALE).astype(BF)


def query_sum(parts, stats):
    return pl.pallas_call(
        query_sum_body,
        out_shape=jax.ShapeDtypeStruct((R, 2 * D), BF),
        name="query_sum",
    )(*parts, *stats)


def partner_sum_body(own, back, out):
    out[...] = (own[:, R:] + back[:, R:].astype(F32)).astype(BF)


def partner_sum(own, back):
    return pl.pallas_call(
        partner_sum_body,
        out_shape=jax.ShapeDtypeStruct((512, R), BF),
        name="partner_sum",
    )(own, back)


def key_sum_body(own, back, other, dk, dv):
    total = own[:, :R] + back[:, :R].astype(F32) + other[...].astype(F32)
    dk[...] = total[0:256].T.astype(BF)
    dv[...] = total[256:512].T.astype(BF)


def key_sum(own, back, other):
    return pl.pallas_call(
        key_sum_body,
        out_shape=[jax.ShapeDtypeStruct((R, 2 * D), BF)] * 2,
        name="key_sum",
    )(own, back, other)


def along_y(value, steps):
    pairs = [(2 * y + x, 2 * ((y + steps) % 4) + x) for y in range(4) for x in range(2)]
    return lax.ppermute(value, "inner", pairs)


def along_x(value):
    return lax.ppermute(value, "inner", [(i, i ^ 1) for i in range(8)])


def along_outer(value, steps):
    n = lax.axis_size("outer")
    return lax.ppermute(value, "outer", [(i, (i + steps) % n) for i in range(n)])


def from_peers(value):
    return [along_y(value, -REL[n]) for n in (1, 2, 3)]


def on_device(queries, key_rows, value_rows, outputs, out_grad):
    qg_own, kv_own = prep(queries, key_rows, value_rows, outputs, out_grad)
    kv_other = along_x(kv_own)
    qg = [qg_own] + from_peers(qg_own)
    kv = [kv_own, kv_other, along_outer(kv_own, 1), along_outer(kv_other, 1)]
    p, st = stage1(qg, kv)
    stats = [st] + from_peers(st)
    ds, *parts = stage2(qg, kv, p)
    parts = [parts[0]] + [along_y(parts[REL.index(-REL[n] % 4)], -REL[n]) for n in (1, 2, 3)]
    prior, own = stage3(qg, stats, p, ds)
    back = along_outer(prior, -1)
    other = along_x(partner_sum(own, back))
    query_grad = query_sum(parts, stats)
    key_grad, value_grad = key_sum(own, back, other)
    return query_grad, key_grad, value_grad


def solution(mesh):
    spec = P(("outer", "inner"), None)
    return jax.shard_map(
        on_device, mesh=mesh, in_specs=(spec,) * 5, out_specs=(spec,) * 3, check_vma=False
    )
```

time: 396 us -> 109 us (0.28)
  starting transfers between devices: 149 us -> 44.5 us
  waiting for transfers between devices: 122 us -> 31.6 us
  matrix products: 43 us -> 0 us
  other arithmetic: 39.3 us -> 0 us
  Pallas kernels: 0 us -> 23.8 us
  local copies, waits for them, and re-layouts: 22.3 us -> 6.21 us
  between operations: 14.2 us -> 0.86 us
    ppermute x44 -> x14, starting transfers between devices: 149 us -> 44.5 us  [the longest x9 32.3 us: along_y(): return lax.ppermute(value, 'inner', pairs)]
    all_gather x1 -> x0, waiting for transfers between devices: 62 us -> none  [on_device(): lax.all_gather(window_keys, 'inner', axis=0, tiled=True)]
    dot_general x41 -> x0, matrix products: 43 us -> none  [the longest x9 15.4 us: scores_of(): jnp.einsum('qhd,khd->hqk', query_heads, split_heads(key_block), preferred...]
    ppermute x44 -> x14, waiting for transfers between devices: 60.1 us -> 31.6 us  [the longest x3 25.3 us: along_outer(): lax.ppermute(value, 'outer', [(i, (i + steps) % n) for i in range(n)])]
    add x17 -> x0, other arithmetic: 26.3 us -> none  [the longest x8 19.9 us: query_turn(): value_acc + grad_value]
    pallas_call x0 -> x7, Pallas kernels: none -> 23.8 us  [the longest x1 5.54 us: stage1(): pl.pallas_call(k1_body, in_specs=[VM] * 8, out_specs=[VM, VM], out_shape=...]
    while x35 -> x0, local copies, waits for them, and re-layouts: 17.4 us -> none
    reduce_sum x1 -> x0, other arithmetic: 9.48 us -> none  [on_device(): total = jnp.sum(jnp.exp(scores - newest[:, :, None]), axis=2)]
  transfers between devices with their start and end apart: 45 -> 14, of which waited for: 12 -> 5; matrix products, arithmetic and copies ran while one was open for 20% -> 0% of each run, Pallas kernels for 0% -> 7%
where the time goes in v1:
time: 109 us; the launch traced here: 107 us
  starting transfers between devices  44.5 us (41%)
  waiting for transfers between devices  31.6 us (29%)
  Pallas kernels  23.8 us (22%)
  local copies, waits for them, and re-layouts  6.21 us (6%)
    ppermute x9, starting transfers between devices, along_y(): return lax.ppermute(value, 'inner', pairs)  32.3 us
    ppermute x3, waiting for transfers between devices, along_outer(): lax.ppermute(value, 'outer', [(i, (i + steps) % n) for i in range(n)])  25.3 us
    ppermute x3, starting transfers between devices, along_outer(): lax.ppermute(value, 'outer', [(i, (i + steps) % n) for i in range(n)])  6.7 us
    ppermute x9, waiting for transfers between devices, along_y(): return lax.ppermute(value, 'inner', pairs)  6.31 us
    unnamed x26, local copies, waits for them, and re-layouts  6.21 us
    pallas_call x1, Pallas kernels, stage1(): pl.pallas_call(k1_body, in_specs=[VM] * 8, out_specs=[VM, VM], out_shape=...  5.54 us
    ppermute x2, starting transfers between devices, along_x(): return lax.ppermute(value, 'inner', [(i, i ^ 1) for i in range(8)])  5.52 us
    pallas_call x1, Pallas kernels, stage2(): pl.pallas_call(k2_body, in_specs=[VM] * 9, out_specs=[VM] * 5, out_shape=...  5.42 us
  transfers between devices with their start and end apart: 14, of which 5 were waited for; matrix products, arithmetic and copies ran while one was open for 0% of the time, Pallas kernels for 7%

profile of v1, /device:TPU:24, one launch (start us, length us, event | category | flops | bytes accessed | tf_op | source)
XLA Modules:
  0.0 107.0 jit_solution(18159165884306359530)
XLA Ops:
  0.6 2.5 %pack.1 = (bf16[528,384]{1,0:T(8,128)(2,1)}, bf16[512,384]{1,0:T(8,128)(2,1)}) custom-call(bf16[384,256]{1,0:T(8,128)(2,1)} %q.1, bf16[384,256]{1,0:T(8,128)(2,1)} %k.1, bf16[384,256]{1,0:T(8,128)(2,1)} %v.1, bf16[384,256]{1,0:T(8,128)(2,1)} %o.1, bf16[384,256]{1,0:T(8,128)(2,1)} %g.1), custom_call_target="tpu_custom_call" | custom-call | tf_op jit(solution)/shard_map/pack/pallas_call | solution.py:48
  3.1 3.4 %collective-permute-start.3 = (bf16[512,384]{1,0:T(8,128)(2,1)}, bf16[512,384]{1,0:T(8,128)(2,1)S(1)}, u32[]{:S(2)}, u32[]{:S(2)}) collective-permute-start(bf16[512,384]{1,0:T(8,128)(2,1)} %get-tuple-element.17.refs_4_), channel_id=1, source_target_pairs={{0,1},{1,0},{2,3},{3,2},{4,5},{5,4},{6,7},{7,6},{8,9},{9,8},{10,11... | collective-permute-start | bytes 1179656 | tf_op jit(solution)/shard_map/ppermute | solution.py:220
  6.5 2.7 %collective-permute-start = (bf16[528,384]{1,0:T(8,128)(2,1)}, bf16[528,384]{1,0:T(8,128)(2,1)S(1)}, u32[]{:S(2)}, u32[]{:S(2)}) collective-permute-start(bf16[528,384]{1,0:T(8,128)(2,1)} %get-tuple-element.16.refs_0_), channel_id=1, source_target_pairs={{0,6},{1,7},{2,0},{3,1},{4,2},{5,3},{6,4},{7,5},{8,14},{9,15},{10,... | collective-permute-start | bytes 1216520 | tf_op jit(solution)/shard_map/ppermute | solution.py:216
  9.2 5.3 %collective-permute-start.1 = (bf16[528,384]{1,0:T(8,128)(2,1)}, bf16[528,384]{1,0:T(8,128)(2,1)S(1)}, u32[]{:S(2)}, u32[]{:S(2)}) collective-permute-start(bf16[528,384]{1,0:T(8,128)(2,1)} %get-tuple-element.16.refs_0_), channel_id=1, source_target_pairs={{0,2},{1,3},{2,4},{3,5},{4,6},{5,7},{6,0},{7,1},{8,10},{9,11},{10,... | collective-permute-start | bytes 1216520 | tf_op jit(solution)/shard_map/ppermute | solution.py:216
  14.5 3.4 %collective-permute-start.2 = (bf16[528,384]{1,0:T(8,128)(2,1)}, bf16[528,384]{1,0:T(8,128)(2,1)S(1)}, u32[]{:S(2)}, u32[]{:S(2)}) collective-permute-start(bf16[528,384]{1,0:T(8,128)(2,1)} %get-tuple-element.16.refs_0_), channel_id=1, source_target_pairs={{0,4},{1,5},{2,6},{3,7},{4,0},{5,1},{6,2},{7,3},{8,12},{9,13},{10,... | collective-permute-start | bytes 1216520 | tf_op jit(solution)/shard_map/ppermute | solution.py:216
  17.8 1.9 %collective-permute-start.4 = (bf16[512,384]{1,0:T(8,128)(2,1)}, bf16[512,384]{1,0:T(8,128)(2,1)S(1)}, u32[]{:S(2)}, u32[]{:S(2)}) collective-permute-start(bf16[512,384]{1,0:T(8,128)(2,1)} %get-tuple-element.17.refs_4_), channel_id=1, source_target_pairs={{0,8},{8,16},{16,24},{24,32},{32,40},{40,48},{48,56},{56,64},{64,7... | collective-permute-start | bytes 1179656 | tf_op jit(solution)/shard_map/ppermute | solution.py:225
  19.8 0.0 collective-permute-done.3.refs_5_
  19.8 1.9 %collective-permute-start.5 = (bf16[512,384]{1,0:T(8,128)(2,1)S(1)}, bf16[512,384]{1,0:T(8,128)(2,1)S(1)}, u32[]{:S(2)}, u32[]{:S(2)}) collective-permute-start(bf16[512,384]{1,0:T(8,128)(2,1)S(1)} %collective-permute-done.3.refs_5_), channel_id=1, source_target_pairs={{0,8},{8,16},{16,24},{24,32},{32,40},{40,48},{48,56},{56,64},{64,7... | collective-permute-start | bytes 1179656 | tf_op jit(solution)/shard_map/ppermute | solution.py:225
  21.7 11.6 %collective-permute-done.4.refs_6_ = bf16[512,384]{1,0:T(8,128)(2,1)S(1)} collective-permute-done((bf16[512,384]{1,0:T(8,128)(2,1)}, bf16[512,384]{1,0:T(8,128)(2,1)S(1)}, u32[]{:S(2)}, u32[]{:S(2)}) %collective-permute-start.4) | collective-permute-done | bytes 393248 | tf_op jit(solution)/shard_map/ppermute | solution.py:225
  33.3 0.0 collective-permute-done.refs_1_
  33.3 0.0 collective-permute-done.1.refs_2_
  33.3 0.0 collective-permute-done.2.refs_3_
  33.3 4.2 %collective-permute-done.5.refs_7_ = bf16[512,384]{1,0:T(8,128)(2,1)S(1)} collective-permute-done((bf16[512,384]{1,0:T(8,128)(2,1)S(1)}, bf16[512,384]{1,0:T(8,128)(2,1)S(1)}, u32[]{:S(2)}, u32[]{:S(2)}) %collective-permute-start.5) | collective-permute-done | bytes 393248 | tf_op jit(solution)/shard_map/ppermute | solution.py:225
  37.5 1.0 copy-done.1
  38.5 1.0 copy-done.2
  39.5 5.5 %scores.1 = (bf16[2,1536,1536]{2,1,0:T(8,128)(2,1)S(1)}, f32[8,1536]{1,0:T(8,128)S(1)}) custom-call(bf16[528,384]{1,0:T(8,128)(2,1)S(1)} %copy-done.1, bf16[528,384]{1,0:T(8,128)(2,1)S(1)} %collective-permute-done.refs_1_, bf16[528,384]{1,0:T(8,128)(2,1)S(1)} %collective-permute-done.1.refs_2_, bf16[528,384]{1,0:T(8,128)(2,1)S(1)} %collective-permute-done.2.refs_3_, ...), custom_call_target="tpu_custom_call" | custom-call | tf_op jit(solution)/shard_map/scores/pallas_call | solution.py:80
  45.1 2.8 %collective-permute-start.9 = (f32[8,1536]{1,0:T(8,128)S(1)}, f32[8,1536]{1,0:T(8,128)S(1)}, u32[]{:S(2)}, u32[]{:S(2)}) collective-permute-start(f32[8,1536]{1,0:T(8,128)S(1)} %get-tuple-element.23.s0.refs_4_), channel_id=1, source_target_pairs={{0,6},{1,7},{2,0},{3,1},{4,2},{5,3},{6,4},{7,5},{8,14},{9,15},{10,... | collective-permute-start | bytes 147464 | tf_op jit(solution)/shard_map/ppermute | solution.py:216
  47.9 4.3 %collective-permute-start.10 = (f32[8,1536]{1,0:T(8,128)S(1)}, f32[8,1536]{1,0:T(8,128)S(1)}, u32[]{:S(2)}, u32[]{:S(2)}) collective-permute-start(f32[8,1536]{1,0:T(8,128)S(1)} %get-tuple-element.23.s0.refs_4_), channel_id=1, source_target_pairs={{0,2},{1,3},{2,4},{3,5},{4,6},{5,7},{6,0},{7,1},{8,10},{9,11},{10,... | collective-permute-start | bytes 147464 | tf_op jit(solution)/shard_map/ppermute | solution.py:216
  52.2 4.1 %collective-permute-start.11 = (f32[8,1536]{1,0:T(8,128)S(1)}, f32[8,1536]{1,0:T(8,128)S(1)}, u32[]{:S(2)}, u32[]{:S(2)}) collective-permute-start(f32[8,1536]{1,0:T(8,128)S(1)} %get-tuple-element.23.s0.refs_4_), channel_id=1, source_target_pairs={{0,4},{1,5},{2,6},{3,7},{4,0},{5,1},{6,2},{7,3},{8,12},{9,13},{10,... | collective-permute-start | bytes 147464 | tf_op jit(solution)/shard_map/ppermute | solution.py:216
  56.3 5.4 %score_grads.1 = (bf16[2,1536,1536]{2,1,0:T(8,128)(2,1)S(1)}, bf16[384,256]{1,0:T(8,128)(2,1)S(1)}, bf16[384,256]{1,0:T(8,128)(2,1)S(1)}, bf16[384,256]{1,0:T(8,128)(2,1)S(1)}, bf16[384,256]{1,0:T(8,128)(2,1)S(1)}) custom-call(bf16[528,384]{1,0:T(8,128)(2,1)S(1)} %copy-done.1, bf16[528,384]{1,0:T(8,128)(2,1)S(1)} %collective-permute-done.refs_1_, ...), custom_call_target="tpu_custom_call" | custom-call | tf_op jit(solution)/shard_map/score_grads/pallas_call | solution.py:111
  61.7 0.0 copy-start.3
  61.7 0.7 copy-done.3
  62.4 0.0 collective-permute-done.9.s1.refs_5_
  62.4 0.0 collective-permute-done.10.s2.refs_6_
  62.4 0.0 copy-start.6
  62.4 0.0 collective-permute-done.11.s3.refs_7_
  62.4 0.0 copy-start.7
  62.4 2.7 %key_grads.1 = (bf16[512,768]{1,0:T(8,128)(2,1)S(1)}, f32[512,768]{1,0:T(8,128)S(1)}) custom-call(bf16[528,384]{1,0:T(8,128)(2,1)S(1)} %copy-done.1, bf16[528,384]{1,0:T(8,128)(2,1)S(1)} %collective-permute-done.refs_1_, bf16[528,384]{1,0:T(8,128)(2,1)S(1)} %collective-permute-done.1.refs_2_, bf16[528,384]{1,0:T(8,128)(2,1)S(1)} %collective-permute-done.2.refs_3_, ...), custom_call_target="tpu_custom_call" | custom-call | tf_op jit(solution)/shard_map/key_grads/pallas_call | solution.py:157
  65.1 0.0 copy-done.4
  65.2 0.0 copy-done.5
  65.2 0.0 copy-done.6
  65.2 1.2 %copy-done = f32[512,768]{1,0:T(8,128)} copy-done((f32[512,768]{1,0:T(8,128)}, f32[512,768]{1,0:T(8,128)S(1)}, u32[]{:S(2)}) %copy-start) | copy-done | bytes 1572888
  66.4 2.9 %collective-permute-start.12 = (bf16[512,768]{1,0:T(8,128)(2,1)S(1)}, bf16[512,768]{1,0:T(8,128)(2,1)S(1)}, u32[]{:S(2)}, u32[]{:S(2)}) collective-permute-start(bf16[512,768]{1,0:T(8,128)(2,1)S(1)} %get-tuple-element.26), channel_id=1, source_target_pairs={{0,504},{8,0},{16,8},{24,16},{32,24},{40,32},{48,40},{56,48},{64,5... | collective-permute-start | bytes 2359304 | tf_op jit(solution)/shard_map/ppermute | solution.py:225
  69.2 9.5 %collective-permute-done.12.back = bf16[512,768]{1,0:T(8,128)(2,1)S(1)} collective-permute-done((bf16[512,768]{1,0:T(8,128)(2,1)S(1)}, bf16[512,768]{1,0:T(8,128)(2,1)S(1)}, u32[]{:S(2)}, u32[]{:S(2)}) %collective-permute-start.12) | collective-permute-done | bytes 786464 | tf_op jit(solution)/shard_map/ppermute | solution.py:225
  78.7 0.9 copy-done.8
  79.6 2.4 %partner_sum.1 = bf16[512,384]{1,0:T(8,128)(2,1)} custom-call(f32[512,768]{1,0:T(8,128)} %copy-done, bf16[512,768]{1,0:T(8,128)(2,1)} %copy-done.8), custom_call_target="tpu_custom_call" | custom-call | tf_op jit(solution)/shard_map/partner_sum/pallas_call | solution.py:193
  82.1 2.1 %collective-permute-start.13 = (bf16[512,384]{1,0:T(8,128)(2,1)}, bf16[512,384]{1,0:T(8,128)(2,1)S(1)}, u32[]{:S(2)}, u32[]{:S(2)}) collective-permute-start(bf16[512,384]{1,0:T(8,128)(2,1)} %partner_sum.1), channel_id=1, source_target_pairs={{0,1},{1,0},{2,3},{3,2},{4,5},{5,4},{6,7},{7,6},{8,9},{9,8},{10,11... | collective-permute-start | bytes 1179656 | tf_op jit(solution)/shard_map/ppermute | solution.py:220
  84.2 3.0 %collective-permute-start.6 = (bf16[384,256]{1,0:T(8,128)(2,1)S(1)}, bf16[384,256]{1,0:T(8,128)(2,1)S(1)}, u32[]{:S(2)}, u32[]{:S(2)}) collective-permute-start(bf16[384,256]{1,0:T(8,128)(2,1)S(1)} %get-tuple-element.20), channel_id=1, source_target_pairs={{0,6},{1,7},{2,0},{3,1},{4,2},{5,3},{6,4},{7,5},{8,14},{9,15},{10,... | collective-permute-start | bytes 589832 | tf_op jit(solution)/shard_map/ppermute | solution.py:216
  87.2 4.0 %collective-permute-start.7 = (bf16[384,256]{1,0:T(8,128)(2,1)S(1)}, bf16[384,256]{1,0:T(8,128)(2,1)S(1)}, u32[]{:S(2)}, u32[]{:S(2)}) collective-permute-start(bf16[384,256]{1,0:T(8,128)(2,1)S(1)} %get-tuple-element.21), channel_id=1, source_target_pairs={{0,2},{1,3},{2,4},{3,5},{4,6},{5,7},{6,0},{7,1},{8,10},{9,11},{10,... | collective-permute-start | bytes 589832 | tf_op jit(solution)/shard_map/ppermute | solution.py:216
  91.3 2.8 %collective-permute-start.8 = (bf16[384,256]{1,0:T(8,128)(2,1)S(1)}, bf16[384,256]{1,0:T(8,128)(2,1)S(1)}, u32[]{:S(2)}, u32[]{:S(2)}) collective-permute-start(bf16[384,256]{1,0:T(8,128)(2,1)S(1)} %get-tuple-element.22), channel_id=1, source_target_pairs={{0,4},{1,5},{2,6},{3,7},{4,0},{5,1},{6,2},{7,3},{8,12},{9,13},{10,... | collective-permute-start | bytes 589832 | tf_op jit(solution)/shard_map/ppermute | solution.py:216
  94.1 1.0 collective-permute-done.6.a1
  95.1 0.0 collective-permute-done.7.a2
  95.1 5.3 %collective-permute-done.8.a3 = bf16[384,256]{1,0:T(8,128)(2,1)S(1)} collective-permute-done((bf16[384,256]{1,0:T(8,128)(2,1)S(1)}, bf16[384,256]{1,0:T(8,128)(2,1)S(1)}, u32[]{:S(2)}, u32[]{:S(2)}) %collective-permute-start.8) | collective-permute-done | bytes 196640 | tf_op jit(solution)/shard_map/ppermute | solution.py:216
  100.4 0.7 copy-done.12
  101.0 2.6 %query_sum.1 = bf16[384,256]{1,0:T(8,128)(2,1)} custom-call(bf16[384,256]{1,0:T(8,128)(2,1)} %copy-done.3, bf16[384,256]{1,0:T(8,128)(2,1)} %copy-done.10, bf16[384,256]{1,0:T(8,128)(2,1)} %copy-done.11, bf16[384,256]{1,0:T(8,128)(2,1)} %copy-done.12, f32[8,1536]{1,0:T(8,128)} %copy-done.4, f32[8,1536]{1,0:T(8,128)} %copy-done.5, f32[8,1536]{1,0:T(8,128)} %copy-done.6, ...), custom_call_target="tpu_custom_call" | custom-call | tf_op jit(solution)/shard_map/query_sum/pallas_call | solution.py:181
  103.6 0.0 collective-permute-done.13.other
  103.6 0.8 copy-done.9
  104.4 2.6 %key_sum.1 = (bf16[384,256]{1,0:T(8,128)(2,1)}, bf16[384,256]{1,0:T(8,128)(2,1)}) custom-call(f32[512,768]{1,0:T(8,128)} %copy-done, bf16[512,768]{1,0:T(8,128)(2,1)} %copy-done.8, bf16[512,384]{1,0:T(8,128)(2,1)} %copy-done.9), custom_call_target="tpu_custom_call" | custom-call | tf_op jit(solution)/shard_map/key_sum/pallas_call | solution.py:207
  (13 shorter events, 0.0 us)
Async XLA Ops:
  3.1 16.7 %collective-permute-start.3 = (bf16[512,384]{1,0:T(8,128)(2,1)}, bf16[512,384]{1,0:T(8,128)(2,1)S(1)}, u32[]{:S(2)}, u32[]{:S(2)}) collective-permute-start(bf16[512,384]{1,0:T(8,128)(2,1)} %get-tuple-element.17.refs_4_), channel_id=1, source_target_pairs={{0,1},{1,0},{2,3},{3,2},{4,5},{5,4},{6,7},{7,6},{8,9},{9,8},{10,11... | collective-permute-start | bytes 1179656 | tf_op jit(solution)/shard_map/ppermute | solution.py:220
  6.5 26.8 %collective-permute-start = (bf16[528,384]{1,0:T(8,128)(2,1)}, bf16[528,384]{1,0:T(8,128)(2,1)S(1)}, u32[]{:S(2)}, u32[]{:S(2)}) collective-permute-start(bf16[528,384]{1,0:T(8,128)(2,1)} %get-tuple-element.16.refs_0_), channel_id=1, source_target_pairs={{0,6},{1,7},{2,0},{3,1},{4,2},{5,3},{6,4},{7,5},{8,14},{9,15},{10,... | collective-permute-start | bytes 1216520 | tf_op jit(solution)/shard_map/ppermute | solution.py:216
  9.2 24.2 %collective-permute-start.1 = (bf16[528,384]{1,0:T(8,128)(2,1)}, bf16[528,384]{1,0:T(8,128)(2,1)S(1)}, u32[]{:S(2)}, u32[]{:S(2)}) collective-permute-start(bf16[528,384]{1,0:T(8,128)(2,1)} %get-tuple-element.16.refs_0_), channel_id=1, source_target_pairs={{0,2},{1,3},{2,4},{3,5},{4,6},{5,7},{6,0},{7,1},{8,10},{9,11},{10,... | collective-permute-start | bytes 1216520 | tf_op jit(solution)/shard_map/ppermute | solution.py:216
  14.5 18.9 %collective-permute-start.2 = (bf16[528,384]{1,0:T(8,128)(2,1)}, bf16[528,384]{1,0:T(8,128)(2,1)S(1)}, u32[]{:S(2)}, u32[]{:S(2)}) collective-permute-start(bf16[528,384]{1,0:T(8,128)(2,1)} %get-tuple-element.16.refs_0_), channel_id=1, source_target_pairs={{0,4},{1,5},{2,6},{3,7},{4,0},{5,1},{6,2},{7,3},{8,12},{9,13},{10,... | collective-permute-start | bytes 1216520 | tf_op jit(solution)/shard_map/ppermute | solution.py:216
  17.8 15.5 %collective-permute-start.4 = (bf16[512,384]{1,0:T(8,128)(2,1)}, bf16[512,384]{1,0:T(8,128)(2,1)S(1)}, u32[]{:S(2)}, u32[]{:S(2)}) collective-permute-start(bf16[512,384]{1,0:T(8,128)(2,1)} %get-tuple-element.17.refs_4_), channel_id=1, source_target_pairs={{0,8},{8,16},{16,24},{24,32},{32,40},{40,48},{48,56},{56,64},{64,7... | collective-permute-start | bytes 1179656 | tf_op jit(solution)/shard_map/ppermute | solution.py:225
  19.8 17.8 %collective-permute-start.5 = (bf16[512,384]{1,0:T(8,128)(2,1)S(1)}, bf16[512,384]{1,0:T(8,128)(2,1)S(1)}, u32[]{:S(2)}, u32[]{:S(2)}) collective-permute-start(bf16[512,384]{1,0:T(8,128)(2,1)S(1)} %collective-permute-done.3.refs_5_), channel_id=1, source_target_pairs={{0,8},{8,16},{16,24},{24,32},{32,40},{40,48},{48,56},{56,64},{64,7... | collective-permute-start | bytes 1179656 | tf_op jit(solution)/shard_map/ppermute | solution.py:225
  37.5 1.0 copy-start.1
  38.5 1.0 copy-start.2
  45.1 20.1 %copy-start.4 = (f32[8,1536]{1,0:T(8,128)}, f32[8,1536]{1,0:T(8,128)S(1)}, u32[]{:S(2)}) copy-start(f32[8,1536]{1,0:T(8,128)S(1)} %get-tuple-element.23.s0.refs_4_) | copy-start | bytes 147460
  45.1 17.3 %collective-permute-start.9 = (f32[8,1536]{1,0:T(8,128)S(1)}, f32[8,1536]{1,0:T(8,128)S(1)}, u32[]{:S(2)}, u32[]{:S(2)}) collective-permute-start(f32[8,1536]{1,0:T(8,128)S(1)} %get-tuple-element.23.s0.refs_4_), channel_id=1, source_target_pairs={{0,6},{1,7},{2,0},{3,1},{4,2},{5,3},{6,4},{7,5},{8,14},{9,15},{10,... | collective-permute-start | bytes 147464 | tf_op jit(solution)/shard_map/ppermute | solution.py:216
  47.9 14.5 %collective-permute-start.10 = (f32[8,1536]{1,0:T(8,128)S(1)}, f32[8,1536]{1,0:T(8,128)S(1)}, u32[]{:S(2)}, u32[]{:S(2)}) collective-permute-start(f32[8,1536]{1,0:T(8,128)S(1)} %get-tuple-element.23.s0.refs_4_), channel_id=1, source_target_pairs={{0,2},{1,3},{2,4},{3,5},{4,6},{5,7},{6,0},{7,1},{8,10},{9,11},{10,... | collective-permute-start | bytes 147464 | tf_op jit(solution)/shard_map/ppermute | solution.py:216
  52.2 10.3 %collective-permute-start.11 = (f32[8,1536]{1,0:T(8,128)S(1)}, f32[8,1536]{1,0:T(8,128)S(1)}, u32[]{:S(2)}, u32[]{:S(2)}) collective-permute-start(f32[8,1536]{1,0:T(8,128)S(1)} %get-tuple-element.23.s0.refs_4_), channel_id=1, source_target_pairs={{0,4},{1,5},{2,6},{3,7},{4,0},{5,1},{6,2},{7,3},{8,12},{9,13},{10,... | collective-permute-start | bytes 147464 | tf_op jit(solution)/shard_map/ppermute | solution.py:216
  61.7 0.7 copy-start.3
  62.4 2.8 %copy-start.5 = (f32[8,1536]{1,0:T(8,128)}, f32[8,1536]{1,0:T(8,128)S(1)}, u32[]{:S(2)}) copy-start(f32[8,1536]{1,0:T(8,128)S(1)} %collective-permute-done.9.s1.refs_5_) | copy-start | bytes 147460
  62.4 2.8 %copy-start.6 = (f32[8,1536]{1,0:T(8,128)}, f32[8,1536]{1,0:T(8,128)S(1)}, u32[]{:S(2)}) copy-start(f32[8,1536]{1,0:T(8,128)S(1)} %collective-permute-done.10.s2.refs_6_) | copy-start | bytes 147460
  62.4 2.8 %copy-start.7 = (f32[8,1536]{1,0:T(8,128)}, f32[8,1536]{1,0:T(8,128)S(1)}, u32[]{:S(2)}) copy-start(f32[8,1536]{1,0:T(8,128)S(1)} %collective-permute-done.11.s3.refs_7_) | copy-start | bytes 147460
  65.2 1.2 %copy-start = (f32[512,768]{1,0:T(8,128)}, f32[512,768]{1,0:T(8,128)S(1)}, u32[]{:S(2)}) copy-start(f32[512,768]{1,0:T(8,128)S(1)} %get-tuple-element.25.own) | copy-start | bytes 4718596
  66.4 12.4 %collective-permute-start.12 = (bf16[512,768]{1,0:T(8,128)(2,1)S(1)}, bf16[512,768]{1,0:T(8,128)(2,1)S(1)}, u32[]{:S(2)}, u32[]{:S(2)}) collective-permute-start(bf16[512,768]{1,0:T(8,128)(2,1)S(1)} %get-tuple-element.26), channel_id=1, source_target_pairs={{0,504},{8,0},{16,8},{24,16},{32,24},{40,32},{48,40},{56,48},{64,5... | collective-permute-start | bytes 2359304 | tf_op jit(solution)/shard_map/ppermute | solution.py:225
  78.7 0.9 copy-start.8
  82.1 21.6 %collective-permute-start.13 = (bf16[512,384]{1,0:T(8,128)(2,1)}, bf16[512,384]{1,0:T(8,128)(2,1)S(1)}, u32[]{:S(2)}, u32[]{:S(2)}) collective-permute-start(bf16[512,384]{1,0:T(8,128)(2,1)} %partner_sum.1), channel_id=1, source_target_pairs={{0,1},{1,0},{2,3},{3,2},{4,5},{5,4},{6,7},{7,6},{8,9},{9,8},{10,11... | collective-permute-start | bytes 1179656 | tf_op jit(solution)/shard_map/ppermute | solution.py:220
  84.2 10.9 %collective-permute-start.6 = (bf16[384,256]{1,0:T(8,128)(2,1)S(1)}, bf16[384,256]{1,0:T(8,128)(2,1)S(1)}, u32[]{:S(2)}, u32[]{:S(2)}) collective-permute-start(bf16[384,256]{1,0:T(8,128)(2,1)S(1)} %get-tuple-element.20), channel_id=1, source_target_pairs={{0,6},{1,7},{2,0},{3,1},{4,2},{5,3},{6,4},{7,5},{8,14},{9,15},{10,... | collective-permute-start | bytes 589832 | tf_op jit(solution)/shard_map/ppermute | solution.py:216
  87.2 7.8 %collective-permute-start.7 = (bf16[384,256]{1,0:T(8,128)(2,1)S(1)}, bf16[384,256]{1,0:T(8,128)(2,1)S(1)}, u32[]{:S(2)}, u32[]{:S(2)}) collective-permute-start(bf16[384,256]{1,0:T(8,128)(2,1)S(1)} %get-tuple-element.21), channel_id=1, source_target_pairs={{0,2},{1,3},{2,4},{3,5},{4,6},{5,7},{6,0},{7,1},{8,10},{9,11},{10,... | collective-permute-start | bytes 589832 | tf_op jit(solution)/shard_map/ppermute | solution.py:216
  91.3 9.1 %collective-permute-start.8 = (bf16[384,256]{1,0:T(8,128)(2,1)S(1)}, bf16[384,256]{1,0:T(8,128)(2,1)S(1)}, u32[]{:S(2)}, u32[]{:S(2)}) collective-permute-start(bf16[384,256]{1,0:T(8,128)(2,1)S(1)} %get-tuple-element.22), channel_id=1, source_target_pairs={{0,4},{1,5},{2,6},{3,7},{4,0},{5,1},{6,2},{7,3},{8,12},{9,13},{10,... | collective-permute-start | bytes 589832 | tf_op jit(solution)/shard_map/ppermute | solution.py:216
  95.1 5.3 %copy-start.10 = (bf16[384,256]{1,0:T(8,128)(2,1)}, bf16[384,256]{1,0:T(8,128)(2,1)S(1)}, u32[]{:S(2)}) copy-start(bf16[384,256]{1,0:T(8,128)(2,1)S(1)} %collective-permute-done.6.a1) | copy-start | bytes 589828
  95.1 5.3 %copy-start.11 = (bf16[384,256]{1,0:T(8,128)(2,1)}, bf16[384,256]{1,0:T(8,128)(2,1)S(1)}, u32[]{:S(2)}) copy-start(bf16[384,256]{1,0:T(8,128)(2,1)S(1)} %collective-permute-done.7.a2) | copy-start | bytes 589828
  100.4 0.7 copy-start.12
  103.6 0.8 copy-start.9

commit v2 on v1

v2 whole, which is shorter than its diff:
```python
import jax
import jax.numpy as jnp
from jax import lax
from jax.experimental import pallas as pl
from jax.experimental.pallas import tpu as pltpu
from jax.sharding import PartitionSpec as P

R = 384
D = 128
SCALE = D ** -0.5
C = SCALE * 1.4426950408889634
NQ = 4 * R
NK = 4 * R
F32 = jnp.float32
BF = jnp.bfloat16
VM = pl.BlockSpec(memory_space=pltpu.VMEM)
HBM = pl.BlockSpec(memory_space=pltpu.HBM)
PARAMS = pltpu.CompilerParams(vmem_limit_bytes=16 * 1024 * 1024)
ALONE = pltpu.CompilerParams(vmem_limit_bytes=60 * 1024 * 1024)


def dot(a, b, ca, cb):
    return lax.dot_general(a, b, (((ca,), (cb,)), ((), ())), preferred_element_type=F32)


def chunk(n):
    return slice(n * R, (n + 1) * R)


def head(h, base=0):
    return slice(base + h * D, base + (h + 1) * D)


def turned(copies, refs, n):
    copies[n].wait()
    return refs[n][...].astype(F32).T


def started(refs, held, sems):
    copies = [pltpu.make_async_copy(ref, held[n], sems.at[n]) for n, ref in enumerate(refs)]
    for copy in copies:
        copy.start()
    return copies


def pack_keys_body(k, v, kv, ks, vs, sems):
    held = (ks, vs)
    copies = started((k, v), held, sems)
    kv[0:256] = turned(copies, held, 0).astype(BF)
    kv[256:512] = turned(copies, held, 1).astype(BF)
    kv[512:544] = jnp.zeros((32, R), BF)


def pack_queries_body(q, o, g, qg, qs, os, gs, sems):
    held = (qs, os, gs)
    copies = started((q, o, g), held, sems)
    qg[0:256] = turned(copies, held, 0).astype(BF)
    outs = turned(copies, held, 1)
    grads = turned(copies, held, 2)
    qg[256:512] = grads.astype(BF)
    prod = grads * outs
    rows = []
    for h in range(2):
        d = jnp.sum(prod[head(h)], axis=0, keepdims=True)
        hi = d.astype(BF).astype(F32)
        mid = (d - hi).astype(BF).astype(F32)
        rows += [hi, mid, d - hi - mid]
    qg[512:528] = jnp.concatenate(rows + [jnp.zeros((10, R), F32)], axis=0).astype(BF)


def pack_keys(k, v):
    return pl.pallas_call(
        pack_keys_body,
        in_specs=[HBM] * 2,
        out_specs=VM,
        out_shape=pltpu.VMEM((544, R), BF),
        scratch_shapes=[pltpu.VMEM((R, 2 * D), BF)] * 2 + [pltpu.SemaphoreType.DMA((2,))],
        compiler_params=ALONE,
        name="pack_keys",
    )(k, v)


def pack_queries(q, o, g):
    return pl.pallas_call(
        pack_queries_body,
        in_specs=[HBM] * 3,
        out_specs=VM,
        out_shape=pltpu.VMEM((528, R), BF),
        scratch_shapes=[pltpu.VMEM((R, 2 * D), BF)] * 3 + [pltpu.SemaphoreType.DMA((3,))],
        compiler_params=ALONE,
        name="pack_queries",
    )(q, o, g)


def scores_body(*refs):
    qg, kv = refs[0:4], refs[4:8]
    p_ref, st_ref, ks, st = refs[8:]
    for h in range(2):
        for n in range(4):
            ks[h, :, chunk(n)] = kv[n][head(h), :]
    for n in range(4):
        for h in range(2):
            s = dot(qg[n][head(h), :], ks[h], 0, 0)
            m = jnp.max(s, axis=1, keepdims=True) * C
            p = jnp.exp2(s * C - m)
            st[chunk(n), h:h + 1] = m
            st[chunk(n), 2 + h:3 + h] = jnp.sum(p, axis=1, keepdims=True)
            p_ref[h, chunk(n), :] = p.astype(BF)
    st_ref[...] = st[...].T[0:8, :]


def scores(qg, kv):
    return pl.pallas_call(
        scores_body,
        in_specs=[VM] * 8,
        out_specs=[VM] * 2,
        out_shape=[pltpu.VMEM((2, NQ, NK), BF), pltpu.VMEM((8, NQ), F32)],
        scratch_shapes=[pltpu.VMEM((2, D, NK), BF), pltpu.VMEM((NQ, D), F32)],
        compiler_params=PARAMS,
        name="scores",
    )(*qg, *kv)


def merged(a, b, m):
    b = jnp.concatenate([b[0:4, chunk(n ^ m)] for n in range(4)], axis=1)
    top = jnp.maximum(a[0:2], b[0:2])
    total = a[2:4] * jnp.exp2(a[0:2] - top) + b[2:4] * jnp.exp2(b[0:2] - top)
    return top, total


def merge_body(a, b, after, out):
    top, total = merged(a[...], b[...], 1)
    out[0:2] = top
    out[2:4] = total
    out[4:8] = jnp.zeros((4, NQ), F32)


def merge(a, b, after):
    return pl.pallas_call(
        merge_body,
        in_specs=[VM] * 3,
        out_specs=VM,
        out_shape=pltpu.VMEM((8, NQ), F32),
        compiler_params=PARAMS,
        name="merge",
    )(a, b, after)


def score_grads_body(h, *refs):
    qg, kv, p_ref = refs[0:4], refs[4:8], refs[8]
    ds_ref, dq_ref, ks, vs, gs = refs[9:]
    row = lax.broadcasted_iota(jnp.int32, (16, NK), 0)
    for n in range(4):
        ks[:, chunk(n)] = kv[n][head(h), :]
        vs[0:D, chunk(n)] = kv[n][head(h, 256), :]
        gs[n, 0:D, :] = qg[n][head(h, 256), :]
        gs[n, D:D + 16, :] = qg[n][512:528, :]
    vs[D:D + 16, :] = jnp.where((row >= 3 * h) & (row < 3 * h + 3), -1.0, 0.0).astype(BF)
    for n in range(4):
        pg = dot(gs[n], vs[...], 0, 0)
        ds = (p_ref[h, chunk(n), :].astype(F32) * pg).astype(BF)
        ds_ref[chunk(n), :] = ds
        dq_ref[chunk(n), :] = dot(ds, ks[...], 1, 1)


def score_grads(h, qg, kv, p):
    return pl.pallas_call(
        lambda *refs: score_grads_body(h, *refs),
        in_specs=[VM] * 9,
        out_specs=[VM] * 2,
        out_shape=[pltpu.VMEM((NQ, NK), BF), pltpu.VMEM((NQ, D), F32)],
        scratch_shapes=[
            pltpu.VMEM((D, NK), BF),
            pltpu.VMEM((D + 16, NK), BF),
            pltpu.VMEM((4, D + 16, R), BF),
        ],
        compiler_params=PARAMS,
        name="score_grads",
    )(*qg, *kv, p)


def key_part(out, xs, ds, p_ref, cols):
    for h in range(2):
        out[head(h), :] = dot(xs[h, 0], ds[h][:, cols], 1, 0).astype(out.dtype)
        out[head(h, 256), :] = dot(xs[h, 1], p_ref[h, :, cols], 1, 0).astype(out.dtype)


def prior_partner_body(*refs):
    qg, own, pair, other, p_ref, ds, dqs = refs[0:4], refs[4], refs[5], refs[6], refs[7], refs[8:10], refs[10:12]
    out, xs, near, far = refs[12:]
    top, total = merged(pair[...], other[...], 3)
    f = jnp.exp2(own[0:2] - top) / total
    cols = jnp.concatenate([f * SCALE, jnp.zeros((6, NQ), F32)], axis=0).T
    for place, n in ((0, 0), (1, 1)):
        for h, dq in enumerate(dqs):
            near[chunk(place), head(h)] = dq[chunk(n), :] * cols[chunk(n), h:h + 1]
    for place, n in ((0, 3), (1, 2)):
        for h, dq in enumerate(dqs):
            far[chunk(place), head(h)] = (dq[chunk(n), :] * cols[chunk(n), h:h + 1]).astype(BF)
    for h in range(2):
        for n in range(4):
            fn = f[h:h + 1, chunk(n)]
            xs[h, 0, :, chunk(n)] = (qg[n][head(h), :].astype(F32) * (fn * SCALE)).astype(BF)
            xs[h, 1, :, chunk(n)] = (qg[n][head(h, 256), :].astype(F32) * fn).astype(BF)
    key_part(out, xs, ds, p_ref, chunk(3))


def prior_partner(qg, own, pair, other, p, ds, dq):
    return pl.pallas_call(
        prior_partner_body,
        in_specs=[VM] * 12,
        out_specs=[VM] * 4,
        out_shape=[
            pltpu.VMEM((512, R), BF),
            pltpu.VMEM((2, 2, D, NQ), BF),
            pltpu.VMEM((2 * R, 2 * D), F32),
            pltpu.VMEM((2 * R, 2 * D), BF),
        ],
        compiler_params=PARAMS,
        name="prior_partner",
    )(*qg, own, pair, other, p, *ds, *dq)


def key_grads_body(xs, p_ref, ds0, ds1, own_partner, prior, own):
    ds = (ds0, ds1)
    key_part(own_partner, xs, ds, p_ref, chunk(1))
    key_part(prior, xs, ds, p_ref, chunk(2))
    key_part(own, xs, ds, p_ref, chunk(0))


def key_grads(xs, p, ds):
    part = pltpu.VMEM((512, R), F32)
    return pl.pallas_call(
        key_grads_body,
        in_specs=[VM] * 4,
        out_specs=[VM] * 3,
        out_shape=[pltpu.VMEM((512, R), BF), part, part],
        compiler_params=PARAMS,
        name="key_grads",
    )(xs, p, *ds)


def prior_sum_body(a, b, out):
    out[...] = (a[...] + b[...].astype(F32)).astype(BF)


def prior_sum(a, b):
    return pl.pallas_call(
        prior_sum_body,
        in_specs=[VM] * 2,
        out_specs=VM,
        out_shape=pltpu.VMEM((512, R), BF),
        compiler_params=PARAMS,
        name="prior_sum",
    )(a, b)


def query_mid_body(near, far, own, pair):
    own[...] = near[chunk(0), :] + far[chunk(0), :].astype(F32)
    pair[...] = (near[chunk(1), :] + far[chunk(1), :].astype(F32)).astype(BF)


def query_mid(near, far):
    return pl.pallas_call(
        query_mid_body,
        in_specs=[VM] * 2,
        out_specs=[VM] * 2,
        out_shape=[pltpu.VMEM((R, 2 * D), F32), pltpu.VMEM((R, 2 * D), BF)],
        compiler_params=PARAMS,
        name="query_mid",
    )(near, far)


def query_sum_body(own, pair, out):
    out[...] = (own[...] + pair[...].astype(F32)).astype(BF)


def query_sum(own, pair):
    return pl.pallas_call(
        query_sum_body,
        in_specs=[VM] * 2,
        out_shape=jax.ShapeDtypeStruct((R, 2 * D), BF),
        compiler_params=PARAMS,
        name="query_sum",
    )(own, pair)


def key_sum_body(own, other, back, dk, dv):
    total = own[...] + other[...].astype(F32) + back[...].astype(F32)
    dk[...] = total[0:256].T.astype(BF)
    dv[...] = total[256:512].T.astype(BF)


def key_sum(own, other, back):
    return pl.pallas_call(
        key_sum_body,
        in_specs=[VM] * 3,
        out_shape=[jax.ShapeDtypeStruct((R, 2 * D), BF)] * 2,
        compiler_params=PARAMS,
        name="key_sum",
    )(own, other, back)


def along_y(value, m):
    return lax.ppermute(value, "inner", [(i, i ^ (2 * m)) for i in range(8)])


def passed_on(one, three):
    outer, inner = lax.axis_size("outer"), lax.axis_size("inner")
    pairs = [
        (o * inner + i, o * inner + (i ^ (2 if o % 2 == 0 else 6))) for o in range(outer) for i in range(inner)
    ]
    value = jnp.where(lax.axis_index("outer") % 2 == 0, three, one)
    return lax.ppermute(value, ("outer", "inner"), pairs)


def along_x(value):
    return lax.ppermute(value, "inner", [(i, i ^ 1) for i in range(8)])


def window_pairs():
    outer, inner = lax.axis_size("outer"), lax.axis_size("inner")
    turn = outer // 2
    return [
        (o * inner + i, (o + 1) % outer * inner + (i ^ 1 if o % turn == turn - 1 else i))
        for o in range(outer)
        for i in range(inner)
    ]


def to_next(value):
    return lax.ppermute(value, ("outer", "inner"), window_pairs())


def to_prior(value):
    return lax.ppermute(value, ("outer", "inner"), [(b, a) for a, b in window_pairs()])


def on_device(queries, key_rows, value_rows, outputs, out_grad):
    kv_own = pack_keys(key_rows, value_rows)
    qg_own = pack_queries(queries, outputs, out_grad)
    kv_prior = to_next(kv_own)
    kv_partner = along_x(kv_own)
    kv = [kv_own, kv_partner, kv_prior, to_next(kv_partner)]
    qg_1, qg_3 = along_y(qg_own, 1), along_y(qg_own, 3)
    qg = [qg_own, qg_1, passed_on(qg_1, qg_3), qg_3]
    p, st = scores(qg, kv)
    st_pair = along_y(st, 1)
    ds0, dq0 = score_grads(0, qg, kv, p)
    pair = merge(st, st_pair, dq0)
    pair_other = along_y(pair, 3)
    ds1, dq1 = score_grads(1, qg, kv, p)
    ds, dq = (ds0, ds1), (dq0, dq1)
    part, xs, near, far = prior_partner(qg, st, pair, pair_other, p, ds, dq)
    part = along_x(part)
    far = along_y(far, 3)
    own_partner, prior, own = key_grads(xs, p, ds)
    other = along_x(own_partner)
    back = to_prior(prior_sum(prior, part))
    near, pair = query_mid(near, far)
    query_grad = query_sum(near, along_y(pair, 1))
    key_grad, value_grad = key_sum(own, other, back)
    return query_grad, key_grad, value_grad


def solution(mesh):
    spec = P(("outer", "inner"), None)
    return jax.shard_map(
        on_device, mesh=mesh, in_specs=(spec,) * 5, out_specs=(spec,) * 3, check_vma=False
    )
```

time: 109 us -> 82.8 us (0.76)
  waiting for transfers between devices: 31.6 us -> 18.7 us
  local copies, waits for them, and re-layouts: 6.21 us -> 0 us
  Pallas kernels: 23.8 us -> 19.3 us
  starting transfers between devices: 44.5 us -> 42.7 us
    ppermute x12 -> x10, waiting for transfers between devices: 31.6 us -> 18.7 us  [the longest x6 9.73 us: along_y(): return lax.ppermute(value, 'inner', [(i, i ^ 2 * m) for i in range(8)])]
    unnamed x26 -> x0, local copies, waits for them, and re-layouts: 6.21 us -> none
    ppermute x12 -> x10, starting transfers between devices: 39 us -> 33.4 us  [the longest x6 22 us: along_y(): return lax.ppermute(value, 'inner', [(i, i ^ 2 * m) for i in range(8)])]
    pallas_call x7 -> x12, Pallas kernels: 23.8 us -> 19.3 us  [the longest x2 5.67 us: score_grads(): pl.pallas_call(lambda *refs: score_grads_body(h, *refs), in_specs=[VM] *...]
    ppermute x2 -> x3, starting transfers between devices: 5.52 us -> 9.24 us  [along_x(): return lax.ppermute(value, 'inner', [(i, i ^ 1) for i in range(8)])]
  transfers between devices with their start and end apart: 14 -> 13, of which waited for: 5 -> 7; matrix products, arithmetic and copies ran while one was open for 0% -> 0% of each run, Pallas kernels for 7% -> 13%
where the time goes in v2:
time: 82.8 us; the launch traced here: 81.6 us
  starting transfers between devices  42.7 us (52%)
  Pallas kernels  19.3 us (23%)
  waiting for transfers between devices  18.7 us (23%)
  between operations  0.84 us (1%)
    ppermute x6, starting transfers between devices, along_y(): return lax.ppermute(value, 'inner', [(i, i ^ 2 * m) for i in range(8)])  22 us
    ppermute x6, waiting for transfers between devices, along_y(): return lax.ppermute(value, 'inner', [(i, i ^ 2 * m) for i in range(8)])  9.73 us
    ppermute x3, starting transfers between devices, along_x(): return lax.ppermute(value, 'inner', [(i, i ^ 1) for i in range(8)])  9.24 us
    ppermute x1, starting transfers between devices, to_prior(): lax.ppermute(value, ('outer', 'inner'), [(b, a) for a, b in window_pairs()])  5.68 us
    pallas_call x2, Pallas kernels, score_grads(): pl.pallas_call(lambda *refs: score_grads_body(h, *refs), in_specs=[VM] *...  5.67 us
    ppermute x2, waiting for transfers between devices, to_next(): return lax.ppermute(value, ('outer', 'inner'), window_pairs())  5.52 us
    pallas_call x1, Pallas kernels, scores(): pl.pallas_call(scores_body, in_specs=[VM] * 8, out_specs=[VM] * 2, out_sh...  5.52 us
    ppermute x2, starting transfers between devices, to_next(): return lax.ppermute(value, ('outer', 'inner'), window_pairs())  3.84 us
  transfers between devices with their start and end apart: 13, of which 7 were waited for; matrix products, arithmetic and copies ran while one was open for 0% of the time, Pallas kernels for 13%

profile of v2, /device:TPU:24, one launch (start us, length us, event | category | flops | bytes accessed | tf_op | source)
XLA Modules:
  0.0 81.6 jit_solution(6982772710370603299)
XLA Ops:
  0.6 1.2 %pack_keys.1.refs_4_ = bf16[544,384]{1,0:T(8,128)(2,1)S(1)} custom-call(bf16[384,256]{1,0:T(8,128)(2,1)} %k.1, bf16[384,256]{1,0:T(8,128)(2,1)} %v.1), custom_call_target="tpu_custom_call" | custom-call | tf_op jit(solution)/shard_map/pack_keys/pallas_call | solution.py:72
  1.9 3.4 %collective-permute-start.3 = (bf16[544,384]{1,0:T(8,128)(2,1)S(1)}, bf16[544,384]{1,0:T(8,128)(2,1)S(1)}, u32[]{:S(2)}, u32[]{:S(2)}) collective-permute-start(bf16[544,384]{1,0:T(8,128)(2,1)S(1)} %pack_keys.1.refs_4_), channel_id=1, source_target_pairs={{0,1},{1,0},{2,3},{3,2},{4,5},{5,4},{6,7},{7,6},{8,9},{9,8},{10,11... | collective-permute-start | bytes 1253384 | tf_op jit(solution)/shard_map/ppermute | solution.py:318
  5.3 1.4 %pack_queries.1.refs_0_ = bf16[528,384]{1,0:T(8,128)(2,1)S(1)} custom-call(bf16[384,256]{1,0:T(8,128)(2,1)} %q.1, bf16[384,256]{1,0:T(8,128)(2,1)} %o.1, bf16[384,256]{1,0:T(8,128)(2,1)} %g.1), custom_call_target="tpu_custom_call" | custom-call | tf_op jit(solution)/shard_map/pack_queries/pallas_call | solution.py:84
  6.7 6.0 %collective-permute-start.1 = (bf16[528,384]{1,0:T(8,128)(2,1)S(1)}, bf16[528,384]{1,0:T(8,128)(2,1)S(1)}, u32[]{:S(2)}, u32[]{:S(2)}) collective-permute-start(bf16[528,384]{1,0:T(8,128)(2,1)S(1)} %pack_queries.1.refs_0_), channel_id=1, source_target_pairs={{0,6},{1,7},{2,4},{3,5},{4,2},{5,3},{6,0},{7,1},{8,14},{9,15},{10,... | collective-permute-start | bytes 1216520 | tf_op jit(solution)/shard_map/ppermute | solution.py:305
  12.7 1.9 %collective-permute-start = (bf16[528,384]{1,0:T(8,128)(2,1)S(1)}, bf16[528,384]{1,0:T(8,128)(2,1)S(1)}, u32[]{:S(2)}, u32[]{:S(2)}) collective-permute-start(bf16[528,384]{1,0:T(8,128)(2,1)S(1)} %pack_queries.1.refs_0_), channel_id=1, source_target_pairs={{0,2},{1,3},{2,0},{3,1},{4,6},{5,7},{6,4},{7,5},{8,10},{9,11},{10,... | collective-permute-start | bytes 1216520 | tf_op jit(solution)/shard_map/ppermute | solution.py:305
  14.6 1.9 %collective-permute-start.4 = (bf16[544,384]{1,0:T(8,128)(2,1)S(1)}, bf16[544,384]{1,0:T(8,128)(2,1)S(1)}, u32[]{:S(2)}, u32[]{:S(2)}) collective-permute-start(bf16[544,384]{1,0:T(8,128)(2,1)S(1)} %pack_keys.1.refs_4_), channel_id=1, source_target_pairs={{0,8},{1,9},{2,10},{3,11},{4,12},{5,13},{6,14},{7,15},{8,16},{9,17... | collective-permute-start | bytes 1253384 | tf_op jit(solution)/shard_map/ppermute | solution.py:332
  16.6 0.0 collective-permute-done.3.refs_5_
  16.6 1.9 %collective-permute-start.5 = (bf16[544,384]{1,0:T(8,128)(2,1)S(1)}, bf16[544,384]{1,0:T(8,128)(2,1)S(1)}, u32[]{:S(2)}, u32[]{:S(2)}) collective-permute-start(bf16[544,384]{1,0:T(8,128)(2,1)S(1)} %collective-permute-done.3.refs_5_), channel_id=1, source_target_pairs={{0,8},{1,9},{2,10},{3,11},{4,12},{5,13},{6,14},{7,15},{8,16},{9,17... | collective-permute-start | bytes 1253384 | tf_op jit(solution)/shard_map/ppermute | solution.py:332
  18.5 2.1 %collective-permute-done.1.refs_3_ = bf16[528,384]{1,0:T(8,128)(2,1)S(1)} collective-permute-done((bf16[528,384]{1,0:T(8,128)(2,1)S(1)}, bf16[528,384]{1,0:T(8,128)(2,1)S(1)}, u32[]{:S(2)}, u32[]{:S(2)}) %collective-permute-start.1) | collective-permute-done | bytes 405536 | tf_op jit(solution)/shard_map/ppermute | solution.py:305
  20.6 1.9 %collective-permute-done.refs_1_ = bf16[528,384]{1,0:T(8,128)(2,1)S(1)} collective-permute-done((bf16[528,384]{1,0:T(8,128)(2,1)S(1)}, bf16[528,384]{1,0:T(8,128)(2,1)S(1)}, u32[]{:S(2)}, u32[]{:S(2)}) %collective-permute-start) | collective-permute-done | bytes 405536 | tf_op jit(solution)/shard_map/ppermute | solution.py:305
  22.5 0.1 broadcast_select_fusion
  22.6 1.9 %collective-permute-start.2 = (bf16[528,384]{1,0:T(8,128)(2,1)S(1)}, bf16[528,384]{1,0:T(8,128)(2,1)S(1)}, u32[]{:S(2)}, u32[]{:S(2)}) collective-permute-start(bf16[528,384]{1,0:T(8,128)(2,1)S(1)} %broadcast_select_fusion), channel_id=1, source_target_pairs={{0,2},{1,3},{2,0},{3,1},{4,6},{5,7},{6,4},{7,5},{8,14},{9,15},{10,... | collective-permute-start | bytes 1216520 | tf_op jit(solution)/shard_map/ppermute | solution.py:314
  24.5 4.5 %collective-permute-done.4.refs_6_ = bf16[544,384]{1,0:T(8,128)(2,1)S(1)} collective-permute-done((bf16[544,384]{1,0:T(8,128)(2,1)S(1)}, bf16[544,384]{1,0:T(8,128)(2,1)S(1)}, u32[]{:S(2)}, u32[]{:S(2)}) %collective-permute-start.4) | collective-permute-done | bytes 417824 | tf_op jit(solution)/shard_map/ppermute | solution.py:332
  28.9 3.4 %collective-permute-done.2.refs_2_ = bf16[528,384]{1,0:T(8,128)(2,1)S(1)} collective-permute-done((bf16[528,384]{1,0:T(8,128)(2,1)S(1)}, bf16[528,384]{1,0:T(8,128)(2,1)S(1)}, u32[]{:S(2)}, u32[]{:S(2)}) %collective-permute-start.2) | collective-permute-done | bytes 405536 | tf_op jit(solution)/shard_map/ppermute | solution.py:314
  32.4 1.1 %collective-permute-done.5.refs_7_ = bf16[544,384]{1,0:T(8,128)(2,1)S(1)} collective-permute-done((bf16[544,384]{1,0:T(8,128)(2,1)S(1)}, bf16[544,384]{1,0:T(8,128)(2,1)S(1)}, u32[]{:S(2)}, u32[]{:S(2)}) %collective-permute-start.5) | collective-permute-done | bytes 417824 | tf_op jit(solution)/shard_map/ppermute | solution.py:332
  33.4 5.5 %scores.1 = (bf16[2,1536,1536]{2,1,0:T(8,128)(2,1)S(1)}, f32[8,1536]{1,0:T(8,128)S(1)}) custom-call(bf16[528,384]{1,0:T(8,128)(2,1)S(1)} %pack_queries.1.refs_0_, bf16[528,384]{1,0:T(8,128)(2,1)S(1)} %collective-permute-done.refs_1_, bf16[528,384]{1,0:T(8,128)(2,1)S(1)} %collective-permute-done.2.refs_2_, ...), custom_call_target="tpu_custom_call" | custom-call | tf_op jit(solution)/shard_map/scores/pallas_call | solution.py:113
  38.9 3.0 %collective-permute-start.6 = (f32[8,1536]{1,0:T(8,128)S(1)}, f32[8,1536]{1,0:T(8,128)S(1)}, u32[]{:S(2)}, u32[]{:S(2)}) collective-permute-start(f32[8,1536]{1,0:T(8,128)S(1)} %get-tuple-element.20.a.refs_4_), channel_id=1, source_target_pairs={{0,2},{1,3},{2,0},{3,1},{4,6},{5,7},{6,4},{7,5},{8,10},{9,11},{10,... | collective-permute-start | bytes 147464 | tf_op jit(solution)/shard_map/ppermute | solution.py:305
  42.0 2.8 %score_grads.2 = (bf16[1536,1536]{1,0:T(8,128)(2,1)S(1)}, f32[1536,128]{1,0:T(8,128)S(1)}) custom-call(bf16[528,384]{1,0:T(8,128)(2,1)S(1)} %pack_queries.1.refs_0_, bf16[528,384]{1,0:T(8,128)(2,1)S(1)} %collective-permute-done.refs_1_, bf16[528,384]{1,0:T(8,128)(2,1)S(1)} %collective-permute-done.2.refs_2_, ...), custom_call_target="tpu_custom_call" | custom-call | tf_op jit(solution)/shard_map/score_grads/pallas_call | solution.py:167
  44.8 0.1 collective-permute-done.6.b
  45.0 4.9 %collective-permute-start.7 = (f32[8,1536]{1,0:T(8,128)S(1)}, f32[8,1536]{1,0:T(8,128)S(1)}, u32[]{:S(2)}, u32[]{:S(2)}) collective-permute-start(f32[8,1536]{1,0:T(8,128)S(1)} %merge.1.refs_5_), channel_id=1, source_target_pairs={{0,6},{1,7},{2,4},{3,5},{4,2},{5,3},{6,0},{7,1},{8,14},{9,15},{10,... | collective-permute-start | bytes 147464 | tf_op jit(solution)/shard_map/ppermute | solution.py:305
  49.9 2.8 %score_grads.3 = (bf16[1536,1536]{1,0:T(8,128)(2,1)S(1)}, f32[1536,128]{1,0:T(8,128)S(1)}) custom-call(bf16[528,384]{1,0:T(8,128)(2,1)S(1)} %pack_queries.1.refs_0_, bf16[528,384]{1,0:T(8,128)(2,1)S(1)} %collective-permute-done.refs_1_, bf16[528,384]{1,0:T(8,128)(2,1)S(1)} %collective-permute-done.2.refs_2_, ...), custom_call_target="tpu_custom_call" | custom-call | tf_op jit(solution)/shard_map/score_grads/pallas_call | solution.py:167
  52.7 0.0 collective-permute-done.7.refs_6_
  52.8 1.2 %prior_partner.1 = (bf16[512,384]{1,0:T(8,128)(2,1)S(1)}, bf16[2,2,128,1536]{3,2,1,0:T(8,128)(2,1)S(1)}, f32[768,256]{1,0:T(8,128)S(1)}, bf16[768,256]{1,0:T(8,128)(2,1)S(1)}) custom-call(bf16[528,384]{1,0:T(8,128)(2,1)S(1)} %pack_queries.1.refs_0_, bf16[528,384]{1,0:T(8,128)(2,1)S(1)} %collective-permute-done.refs_1_, ...), custom_call_target="tpu_custom_call" | custom-call | tf_op jit(solution)/shard_map/prior_partner/pallas_call | solution.py:209
  53.9 2.5 %collective-permute-start.11 = (bf16[512,384]{1,0:T(8,128)(2,1)S(1)}, bf16[512,384]{1,0:T(8,128)(2,1)S(1)}, u32[]{:S(2)}, u32[]{:S(2)}) collective-permute-start(bf16[512,384]{1,0:T(8,128)(2,1)S(1)} %get-tuple-element.34), channel_id=1, source_target_pairs={{0,1},{1,0},{2,3},{3,2},{4,5},{5,4},{6,7},{7,6},{8,9},{9,8},{10,11... | collective-permute-start | bytes 1179656 | tf_op jit(solution)/shard_map/ppermute | solution.py:318
  56.4 4.2 %collective-permute-start.8 = (bf16[768,256]{1,0:T(8,128)(2,1)S(1)}, bf16[768,256]{1,0:T(8,128)(2,1)S(1)}, u32[]{:S(2)}, u32[]{:S(2)}) collective-permute-start(bf16[768,256]{1,0:T(8,128)(2,1)S(1)} %get-tuple-element.27), channel_id=1, source_target_pairs={{0,6},{1,7},{2,4},{3,5},{4,2},{5,3},{6,0},{7,1},{8,14},{9,15},{10,... | collective-permute-start | bytes 1179656 | tf_op jit(solution)/shard_map/ppermute | solution.py:305
  60.6 2.6 %key_grads.1 = (bf16[512,384]{1,0:T(8,128)(2,1)S(1)}, f32[512,384]{1,0:T(8,128)S(1)}, f32[512,384]{1,0:T(8,128)S(1)}) custom-call(bf16[2,2,128,1536]{3,2,1,0:T(8,128)(2,1)S(1)} %get-tuple-element.30.xs, bf16[2,1536,1536]{2,1,0:T(8,128)(2,1)S(1)} %get-tuple-element.21.refs_8_.refs_7_.p_ref, bf16[1536,1536]{1,0:T(8,128)(2,1)S(1)} %get-tuple-element.23.refs_8_.ds0, ...), custom_call_target="tpu_custom_call" | custom-call | tf_op jit(solution)/shard_map/key_grads/pallas_call | solution.py:233
  63.2 3.3 %collective-permute-start.10 = (bf16[512,384]{1,0:T(8,128)(2,1)S(1)}, bf16[512,384]{1,0:T(8,128)(2,1)S(1)}, u32[]{:S(2)}, u32[]{:S(2)}) collective-permute-start(bf16[512,384]{1,0:T(8,128)(2,1)S(1)} %get-tuple-element.32), channel_id=1, source_target_pairs={{0,1},{1,0},{2,3},{3,2},{4,5},{5,4},{6,7},{7,6},{8,9},{9,8},{10,11... | collective-permute-start | bytes 1179656 | tf_op jit(solution)/shard_map/ppermute | solution.py:318
  66.6 0.0 collective-permute-done.11.b
  66.6 0.1 prior_sum.1
  66.7 5.7 %collective-permute-start.12 = (bf16[512,384]{1,0:T(8,128)(2,1)S(1)}, bf16[512,384]{1,0:T(8,128)(2,1)S(1)}, u32[]{:S(2)}, u32[]{:S(2)}) collective-permute-start(bf16[512,384]{1,0:T(8,128)(2,1)S(1)} %prior_sum.1), channel_id=1, source_target_pairs={{8,0},{9,1},{10,2},{11,3},{12,4},{13,5},{14,6},{15,7},{16,8},{17,9... | collective-permute-start | bytes 1179656 | tf_op jit(solution)/shard_map/ppermute | solution.py:336
  72.3 0.0 collective-permute-done.8.far
  72.3 0.1 query_mid.1
  72.4 1.9 %collective-permute-start.9 = (bf16[384,256]{1,0:T(8,128)(2,1)S(1)}, bf16[384,256]{1,0:T(8,128)(2,1)S(1)}, u32[]{:S(2)}, u32[]{:S(2)}) collective-permute-start(bf16[384,256]{1,0:T(8,128)(2,1)S(1)} %get-tuple-element.29), channel_id=1, source_target_pairs={{0,2},{1,3},{2,0},{3,1},{4,6},{5,7},{6,4},{7,5},{8,10},{9,11},{10,... | collective-permute-start | bytes 589832 | tf_op jit(solution)/shard_map/ppermute | solution.py:305
  74.4 5.6 %collective-permute-done.9.pair = bf16[384,256]{1,0:T(8,128)(2,1)S(1)} collective-permute-done((bf16[384,256]{1,0:T(8,128)(2,1)S(1)}, bf16[384,256]{1,0:T(8,128)(2,1)S(1)}, u32[]{:S(2)}, u32[]{:S(2)}) %collective-permute-start.9) | collective-permute-done | bytes 196640 | tf_op jit(solution)/shard_map/ppermute | solution.py:305
  80.0 0.7 query_sum.1
  80.7 0.0 collective-permute-done.10.other
  80.7 0.0 collective-permute-done.12.back
  80.7 0.9 %key_sum.1 = (bf16[384,256]{1,0:T(8,128)(2,1)}, bf16[384,256]{1,0:T(8,128)(2,1)}) custom-call(f32[512,384]{1,0:T(8,128)S(1)} %get-tuple-element.31.own, bf16[512,384]{1,0:T(8,128)(2,1)S(1)} %collective-permute-done.10.other, bf16[512,384]{1,0:T(8,128)(2,1)S(1)} %collective-permute-done.12.back), custom_call_target="tpu_custom_call" | custom-call | tf_op jit(solution)/shard_map/key_sum/pallas_call | solution.py:295
  (1 shorter events, 0.0 us)
Async XLA Ops:
  1.9 14.7 %collective-permute-start.3 = (bf16[544,384]{1,0:T(8,128)(2,1)S(1)}, bf16[544,384]{1,0:T(8,128)(2,1)S(1)}, u32[]{:S(2)}, u32[]{:S(2)}) collective-permute-start(bf16[544,384]{1,0:T(8,128)(2,1)S(1)} %pack_keys.1.refs_4_), channel_id=1, source_target_pairs={{0,1},{1,0},{2,3},{3,2},{4,5},{5,4},{6,7},{7,6},{8,9},{9,8},{10,11... | collective-permute-start | bytes 1253384 | tf_op jit(solution)/shard_map/ppermute | solution.py:318
  6.7 13.9 %collective-permute-start.1 = (bf16[528,384]{1,0:T(8,128)(2,1)S(1)}, bf16[528,384]{1,0:T(8,128)(2,1)S(1)}, u32[]{:S(2)}, u32[]{:S(2)}) collective-permute-start(bf16[528,384]{1,0:T(8,128)(2,1)S(1)} %pack_queries.1.refs_0_), channel_id=1, source_target_pairs={{0,6},{1,7},{2,4},{3,5},{4,2},{5,3},{6,0},{7,1},{8,14},{9,15},{10,... | collective-permute-start | bytes 1216520 | tf_op jit(solution)/shard_map/ppermute | solution.py:305
  12.7 9.8 %collective-permute-start = (bf16[528,384]{1,0:T(8,128)(2,1)S(1)}, bf16[528,384]{1,0:T(8,128)(2,1)S(1)}, u32[]{:S(2)}, u32[]{:S(2)}) collective-permute-start(bf16[528,384]{1,0:T(8,128)(2,1)S(1)} %pack_queries.1.refs_0_), channel_id=1, source_target_pairs={{0,2},{1,3},{2,0},{3,1},{4,6},{5,7},{6,4},{7,5},{8,10},{9,11},{10,... | collective-permute-start | bytes 1216520 | tf_op jit(solution)/shard_map/ppermute | solution.py:305
  14.6 14.3 %collective-permute-start.4 = (bf16[544,384]{1,0:T(8,128)(2,1)S(1)}, bf16[544,384]{1,0:T(8,128)(2,1)S(1)}, u32[]{:S(2)}, u32[]{:S(2)}) collective-permute-start(bf16[544,384]{1,0:T(8,128)(2,1)S(1)} %pack_keys.1.refs_4_), channel_id=1, source_target_pairs={{0,8},{1,9},{2,10},{3,11},{4,12},{5,13},{6,14},{7,15},{8,16},{9,17... | collective-permute-start | bytes 1253384 | tf_op jit(solution)/shard_map/ppermute | solution.py:332
  16.6 16.8 %collective-permute-start.5 = (bf16[544,384]{1,0:T(8,128)(2,1)S(1)}, bf16[544,384]{1,0:T(8,128)(2,1)S(1)}, u32[]{:S(2)}, u32[]{:S(2)}) collective-permute-start(bf16[544,384]{1,0:T(8,128)(2,1)S(1)} %collective-permute-done.3.refs_5_), channel_id=1, source_target_pairs={{0,8},{1,9},{2,10},{3,11},{4,12},{5,13},{6,14},{7,15},{8,16},{9,17... | collective-permute-start | bytes 1253384 | tf_op jit(solution)/shard_map/ppermute | solution.py:332
  22.6 9.8 %collective-permute-start.2 = (bf16[528,384]{1,0:T(8,128)(2,1)S(1)}, bf16[528,384]{1,0:T(8,128)(2,1)S(1)}, u32[]{:S(2)}, u32[]{:S(2)}) collective-permute-start(bf16[528,384]{1,0:T(8,128)(2,1)S(1)} %broadcast_select_fusion), channel_id=1, source_target_pairs={{0,2},{1,3},{2,0},{3,1},{4,6},{5,7},{6,4},{7,5},{8,14},{9,15},{10,... | collective-permute-start | bytes 1216520 | tf_op jit(solution)/shard_map/ppermute | solution.py:314
  38.9 6.0 %collective-permute-start.6 = (f32[8,1536]{1,0:T(8,128)S(1)}, f32[8,1536]{1,0:T(8,128)S(1)}, u32[]{:S(2)}, u32[]{:S(2)}) collective-permute-start(f32[8,1536]{1,0:T(8,128)S(1)} %get-tuple-element.20.a.refs_4_), channel_id=1, source_target_pairs={{0,2},{1,3},{2,0},{3,1},{4,6},{5,7},{6,4},{7,5},{8,10},{9,11},{10,... | collective-permute-start | bytes 147464 | tf_op jit(solution)/shard_map/ppermute | solution.py:305
  45.0 7.8 %collective-permute-start.7 = (f32[8,1536]{1,0:T(8,128)S(1)}, f32[8,1536]{1,0:T(8,128)S(1)}, u32[]{:S(2)}, u32[]{:S(2)}) collective-permute-start(f32[8,1536]{1,0:T(8,128)S(1)} %merge.1.refs_5_), channel_id=1, source_target_pairs={{0,6},{1,7},{2,4},{3,5},{4,2},{5,3},{6,0},{7,1},{8,14},{9,15},{10,... | collective-permute-start | bytes 147464 | tf_op jit(solution)/shard_map/ppermute | solution.py:305
  53.9 12.6 %collective-permute-start.11 = (bf16[512,384]{1,0:T(8,128)(2,1)S(1)}, bf16[512,384]{1,0:T(8,128)(2,1)S(1)}, u32[]{:S(2)}, u32[]{:S(2)}) collective-permute-start(bf16[512,384]{1,0:T(8,128)(2,1)S(1)} %get-tuple-element.34), channel_id=1, source_target_pairs={{0,1},{1,0},{2,3},{3,2},{4,5},{5,4},{6,7},{7,6},{8,9},{9,8},{10,11... | collective-permute-start | bytes 1179656 | tf_op jit(solution)/shard_map/ppermute | solution.py:318
  56.4 15.9 %collective-permute-start.8 = (bf16[768,256]{1,0:T(8,128)(2,1)S(1)}, bf16[768,256]{1,0:T(8,128)(2,1)S(1)}, u32[]{:S(2)}, u32[]{:S(2)}) collective-permute-start(bf16[768,256]{1,0:T(8,128)(2,1)S(1)} %get-tuple-element.27), channel_id=1, source_target_pairs={{0,6},{1,7},{2,4},{3,5},{4,2},{5,3},{6,0},{7,1},{8,14},{9,15},{10,... | collective-permute-start | bytes 1179656 | tf_op jit(solution)/shard_map/ppermute | solution.py:305
  63.2 17.5 %collective-permute-start.10 = (bf16[512,384]{1,0:T(8,128)(2,1)S(1)}, bf16[512,384]{1,0:T(8,128)(2,1)S(1)}, u32[]{:S(2)}, u32[]{:S(2)}) collective-permute-start(bf16[512,384]{1,0:T(8,128)(2,1)S(1)} %get-tuple-element.32), channel_id=1, source_target_pairs={{0,1},{1,0},{2,3},{3,2},{4,5},{5,4},{6,7},{7,6},{8,9},{9,8},{10,11... | collective-permute-start | bytes 1179656 | tf_op jit(solution)/shard_map/ppermute | solution.py:318
  66.7 14.1 %collective-permute-start.12 = (bf16[512,384]{1,0:T(8,128)(2,1)S(1)}, bf16[512,384]{1,0:T(8,128)(2,1)S(1)}, u32[]{:S(2)}, u32[]{:S(2)}) collective-permute-start(bf16[512,384]{1,0:T(8,128)(2,1)S(1)} %prior_sum.1), channel_id=1, source_target_pairs={{8,0},{9,1},{10,2},{11,3},{12,4},{13,5},{14,6},{15,7},{16,8},{17,9... | collective-permute-start | bytes 1179656 | tf_op jit(solution)/shard_map/ppermute | solution.py:336
  72.4 7.6 %collective-permute-start.9 = (bf16[384,256]{1,0:T(8,128)(2,1)S(1)}, bf16[384,256]{1,0:T(8,128)(2,1)S(1)}, u32[]{:S(2)}, u32[]{:S(2)}) collective-permute-start(bf16[384,256]{1,0:T(8,128)(2,1)S(1)} %get-tuple-element.29), channel_id=1, source_target_pairs={{0,2},{1,3},{2,0},{3,1},{4,6},{5,7},{6,4},{7,5},{8,10},{9,11},{10,... | collective-permute-start | bytes 589832 | tf_op jit(solution)/shard_map/ppermute | solution.py:305

commit v3 on v2

--- a/solution.py
+++ b/solution.py
@@ -48,7 +48,6 @@
     copies = started((k, v), held, sems)
     kv[0:256] = turned(copies, held, 0).astype(BF)
     kv[256:512] = turned(copies, held, 1).astype(BF)
-    kv[512:544] = jnp.zeros((32, R), BF)
 
 
 def pack_queries_body(q, o, g, qg, qs, os, gs, sems):
@@ -73,7 +72,7 @@
         pack_keys_body,
         in_specs=[HBM] * 2,
         out_specs=VM,
-        out_shape=pltpu.VMEM((544, R), BF),
+        out_shape=pltpu.VMEM((512, R), BF),
         scratch_shapes=[pltpu.VMEM((R, 2 * D), BF)] * 2 + [pltpu.SemaphoreType.DMA((2,))],
         compiler_params=ALONE,
         name="pack_keys",
@@ -92,33 +91,63 @@
     )(q, o, g)
 
 
-def scores_body(*refs):
-    qg, kv = refs[0:4], refs[4:8]
-    p_ref, st_ref, ks, st = refs[8:]
-    for h in range(2):
-        for n in range(4):
-            ks[h, :, chunk(n)] = kv[n][head(h), :]
-    for n in range(4):
+def score_chunk(n, h, q, keys, p_ref, st):
+    scaled = q[head(h), :].astype(F32) * C
+    high = scaled.astype(BF)
+    low = (scaled - high.astype(F32)).astype(BF)
+    s = dot(jnp.concatenate([high, low], axis=0), keys, 0, 0)
+    m = jnp.max(s, axis=1, keepdims=True)
+    p = jnp.exp2(s - m)
+    st[:, h:h + 1] = m
+    st[:, 2 + h:3 + h] = jnp.sum(p, axis=1, keepdims=True)
+    p_ref[h, chunk(n), :] = p.astype(BF)
+
+
+def first_scores_body(own, first, k0, k1, k2, k3, p_ref, st_ref, ks, st):
+    for n, ref in enumerate((k0, k1, k2, k3)):
         for h in range(2):
-            s = dot(qg[n][head(h), :], ks[h], 0, 0)
-            m = jnp.max(s, axis=1, keepdims=True) * C
-            p = jnp.exp2(s * C - m)
-            st[chunk(n), h:h + 1] = m
-            st[chunk(n), 2 + h:3 + h] = jnp.sum(p, axis=1, keepdims=True)
-            p_ref[h, chunk(n), :] = p.astype(BF)
-    st_ref[...] = st[...].T[0:8, :]
-
-
-def scores(qg, kv):
-    return pl.pallas_call(
-        scores_body,
-        in_specs=[VM] * 8,
+            ks[h, 0:D, chunk(n)] = ref[head(h), :]
+            ks[h, D:2 * D, chunk(n)] = ref[head(h), :]
+    for n, q in enumerate((own, first)):
+        for h in range(2):
+            score_chunk(n, h, q, ks[h], p_ref, st.at[n])
+        st_ref[:, chunk(n)] = st[n].T[0:8, :]
+    st_ref[:, 2 * R:4 * R] = jnp.zeros((8, 2 * R), F32)
+
+
+def first_scores(qg, kv):
+    return pl.pallas_call(
+        first_scores_body,
+        in_specs=[VM] * 6,
+        out_specs=[VM] * 3,
+        out_shape=[pltpu.VMEM((2, NQ, NK), BF), pltpu.VMEM((8, NQ), F32), pltpu.VMEM((2, 2 * D, NK), BF)],
+        scratch_shapes=[pltpu.VMEM((2, R, D), F32)],
+        compiler_params=PARAMS,
+        cost_estimate=pl.CostEstimate(flops=9 * 10 ** 9, bytes_accessed=0, transcendentals=0),
+        name="first_scores",
+    )(qg[0], qg[1], *kv)
+
+
+def last_scores_body(second, third, ks, p_in, st_in, p_ref, st_ref, st):
+    st_ref[...] = st_in[...]
+    for n, q in ((2, second), (3, third)):
+        for h in range(2):
+            score_chunk(n, h, q, ks[h], p_ref, st.at[n - 2])
+        st_ref[:, chunk(n)] = st[n - 2].T[0:8, :]
+
+
+def last_scores(qg, ks, p, st):
+    return pl.pallas_call(
+        last_scores_body,
+        in_specs=[VM] * 5,
         out_specs=[VM] * 2,
         out_shape=[pltpu.VMEM((2, NQ, NK), BF), pltpu.VMEM((8, NQ), F32)],
-        scratch_shapes=[pltpu.VMEM((2, D, NK), BF), pltpu.VMEM((NQ, D), F32)],
-        compiler_params=PARAMS,
-        name="scores",
-    )(*qg, *kv)
+        scratch_shapes=[pltpu.VMEM((2, R, D), F32)],
+        input_output_aliases={3: 0},
+        compiler_params=PARAMS,
+        cost_estimate=pl.CostEstimate(flops=3 * 10 ** 9, bytes_accessed=0, transcendentals=0),
+        name="last_scores",
+    )(qg[2], qg[3], ks, p, st)
 
 
 def merged(a, b, m):
@@ -147,11 +176,10 @@
 
 
 def score_grads_body(h, *refs):
-    qg, kv, p_ref = refs[0:4], refs[4:8], refs[8]
-    ds_ref, dq_ref, ks, vs, gs = refs[9:]
+    qg, kv, ks, p_ref = refs[0:4], refs[4:8], refs[8], refs[9]
+    ds_ref, dq_ref, vs, gs = refs[10:]
     row = lax.broadcasted_iota(jnp.int32, (16, NK), 0)
     for n in range(4):
-        ks[:, chunk(n)] = kv[n][head(h), :]
         vs[0:D, chunk(n)] = kv[n][head(h, 256), :]
         gs[n, 0:D, :] = qg[n][head(h, 256), :]
         gs[n, D:D + 16, :] = qg[n][512:528, :]
@@ -160,23 +188,22 @@
         pg = dot(gs[n], vs[...], 0, 0)
         ds = (p_ref[h, chunk(n), :].astype(F32) * pg).astype(BF)
         ds_ref[chunk(n), :] = ds
-        dq_ref[chunk(n), :] = dot(ds, ks[...], 1, 1)
-
-
-def score_grads(h, qg, kv, p):
+        dq_ref[chunk(n), :] = dot(ds, ks[h, 0:D], 1, 1)
+
+
+def score_grads(h, qg, kv, ks, p):
     return pl.pallas_call(
         lambda *refs: score_grads_body(h, *refs),
-        in_specs=[VM] * 9,
+        in_specs=[VM] * 10,
         out_specs=[VM] * 2,
         out_shape=[pltpu.VMEM((NQ, NK), BF), pltpu.VMEM((NQ, D), F32)],
         scratch_shapes=[
-            pltpu.VMEM((D, NK), BF),
             pltpu.VMEM((D + 16, NK), BF),
             pltpu.VMEM((4, D + 16, R), BF),
         ],
         compiler_params=PARAMS,
         name="score_grads",
-    )(*qg, *kv, p)
+    )(*qg, *kv, ks, p)
 
 
 def key_part(out, xs, ds, p_ref, cols):
@@ -186,15 +213,15 @@
 
 
 def prior_partner_body(*refs):
-    qg, own, pair, other, p_ref, ds, dqs = refs[0:4], refs[4], refs[5], refs[6], refs[7], refs[8:10], refs[10:12]
+    qg, own, pair, other, p_ref, ds, dqs = refs[0:4], *refs[4:8], refs[8:10], refs[10:12]
     out, xs, near, far = refs[12:]
-    top, total = merged(pair[...], other[...], 3)
+    top, total = merged(pair[...], other[...], 2)
     f = jnp.exp2(own[0:2] - top) / total
     cols = jnp.concatenate([f * SCALE, jnp.zeros((6, NQ), F32)], axis=0).T
     for place, n in ((0, 0), (1, 1)):
         for h, dq in enumerate(dqs):
             near[chunk(place), head(h)] = dq[chunk(n), :] * cols[chunk(n), h:h + 1]
-    for place, n in ((0, 3), (1, 2)):
+    for place, n in ((0, 2), (1, 3)):
         for h, dq in enumerate(dqs):
             far[chunk(place), head(h)] = (dq[chunk(n), :] * cols[chunk(n), h:h + 1]).astype(BF)
     for h in range(2):
@@ -240,35 +267,35 @@
     )(xs, p, *ds)
 
 
-def prior_sum_body(a, b, out):
+def prior_sum_body(a, b, after, out):
     out[...] = (a[...] + b[...].astype(F32)).astype(BF)
 
 
-def prior_sum(a, b):
+def prior_sum(a, b, after):
     return pl.pallas_call(
         prior_sum_body,
-        in_specs=[VM] * 2,
+        in_specs=[VM] * 3,
         out_specs=VM,
         out_shape=pltpu.VMEM((512, R), BF),
         compiler_params=PARAMS,
         name="prior_sum",
-    )(a, b)
-
-
-def query_mid_body(near, far, own, pair):
+    )(a, b, after)
+
+
+def query_mid_body(near, far, after, own, pair):
     own[...] = near[chunk(0), :] + far[chunk(0), :].astype(F32)
     pair[...] = (near[chunk(1), :] + far[chunk(1), :].astype(F32)).astype(BF)
 
 
-def query_mid(near, far):
+def query_mid(near, far, after):
     return pl.pallas_call(
         query_mid_body,
-        in_specs=[VM] * 2,
+        in_specs=[VM] * 3,
         out_specs=[VM] * 2,
         out_shape=[pltpu.VMEM((R, 2 * D), F32), pltpu.VMEM((R, 2 * D), BF)],
         compiler_params=PARAMS,
         name="query_mid",
-    )(near, far)
+    )(near, far, after)
 
 
 def query_sum_body(own, pair, out):
@@ -281,36 +308,48 @@
         in_specs=[VM] * 2,
         out_shape=jax.ShapeDtypeStruct((R, 2 * D), BF),
         compiler_params=PARAMS,
+        cost_estimate=pl.CostEstimate(flops=6 * 10 ** 9, bytes_accessed=0, transcendentals=0),
         name="query_sum",
     )(own, pair)
 
 
-def key_sum_body(own, other, back, dk, dv):
-    total = own[...] + other[...].astype(F32) + back[...].astype(F32)
+def own_sum_body(own, other, out):
+    out[...] = own[...] + other[...].astype(F32)
+
+
+def own_sum(own, other):
+    return pl.pallas_call(
+        own_sum_body,
+        in_specs=[VM] * 2,
+        out_specs=VM,
+        out_shape=pltpu.VMEM((512, R), F32),
+        compiler_params=PARAMS,
+        cost_estimate=pl.CostEstimate(flops=8 * 10 ** 9, bytes_accessed=0, transcendentals=0),
+        name="own_sum",
+    )(own, other)
+
+
+def key_sum_body(own, back, dk, dv):
+    total = own[...] + back[...].astype(F32)
     dk[...] = total[0:256].T.astype(BF)
     dv[...] = total[256:512].T.astype(BF)
 
 
-def key_sum(own, other, back):
+def key_sum(own, back):
     return pl.pallas_call(
         key_sum_body,
-        in_specs=[VM] * 3,
+        in_specs=[VM] * 2,
         out_shape=[jax.ShapeDtypeStruct((R, 2 * D), BF)] * 2,
         compiler_params=PARAMS,
         name="key_sum",
-    )(own, other, back)
-
-
-def along_y(value, m):
-    return lax.ppermute(value, "inner", [(i, i ^ (2 * m)) for i in range(8)])
-
-
-def passed_on(one, three):
+    )(own, back)
+
+
+def along_y(value, turn):
     outer, inner = lax.axis_size("outer"), lax.axis_size("inner")
     pairs = [
-        (o * inner + i, o * inner + (i ^ (2 if o % 2 == 0 else 6))) for o in range(outer) for i in range(inner)
+        (o * inner + i, o * inner + (i ^ (6 if o % 2 == turn else 2))) for o in range(outer) for i in range(inner)
     ]
-    value = jnp.where(lax.axis_index("outer") % 2 == 0, three, one)
     return lax.ppermute(value, ("outer", "inner"), pairs)
 
 
@@ -342,24 +381,25 @@
     kv_prior = to_next(kv_own)
     kv_partner = along_x(kv_own)
     kv = [kv_own, kv_partner, kv_prior, to_next(kv_partner)]
-    qg_1, qg_3 = along_y(qg_own, 1), along_y(qg_own, 3)
-    qg = [qg_own, qg_1, passed_on(qg_1, qg_3), qg_3]
-    p, st = scores(qg, kv)
-    st_pair = along_y(st, 1)
-    ds0, dq0 = score_grads(0, qg, kv, p)
+    qg_first = along_y(qg_own, 0)
+    qg = [qg_own, qg_first, along_y(qg_own, 1), along_y(qg_first, 1)]
+    p, st, ks = first_scores(qg, kv)
+    p, st = last_scores(qg, ks, p, st)
+    st_pair = along_y(st, 0)
+    ds0, dq0 = score_grads(0, qg, kv, ks, p)
     pair = merge(st, st_pair, dq0)
-    pair_other = along_y(pair, 3)
-    ds1, dq1 = score_grads(1, qg, kv, p)
+    pair_other = along_y(pair, 1)
+    ds1, dq1 = score_grads(1, qg, kv, ks, p)
     ds, dq = (ds0, ds1), (dq0, dq1)
     part, xs, near, far = prior_partner(qg, st, pair, pair_other, p, ds, dq)
     part = along_x(part)
-    far = along_y(far, 3)
+    far = along_y(far, 1)
     own_partner, prior, own = key_grads(xs, p, ds)
     other = along_x(own_partner)
-    back = to_prior(prior_sum(prior, part))
-    near, pair = query_mid(near, far)
-    query_grad = query_sum(near, along_y(pair, 1))
-    key_grad, value_grad = key_sum(own, other, back)
+    near, pair = query_mid(near, far, own_partner)
+    query_grad = query_sum(near, along_y(pair, 0))
+    back = to_prior(prior_sum(prior, part, pair))
+    key_grad, value_grad = key_sum(own_sum(own, other), back)
     return query_grad, key_grad, value_grad
 
 

time: 82.8 us -> 78.9 us (0.953)
  the two profiles are of different devices: /device:TPU:24 before, /device:TPU:8 now
where the time goes in v3:
time: 78.9 us; the launch traced here: 78.4 us
  starting transfers between devices  42.3 us (54%)
  Pallas kernels  18.9 us (24%)
  waiting for transfers between devices  16.3 us (21%)
  between operations  0.84 us (1%)
    ppermute x7, starting transfers between devices, along_y(): return lax.ppermute(value, ('outer', 'inner'), pairs)  25 us
    ppermute x3, starting transfers between devices, along_x(): return lax.ppermute(value, 'inner', [(i, i ^ 1) for i in range(8)])  9.24 us
    ppermute x2, waiting for transfers between devices, to_next(): return lax.ppermute(value, ('outer', 'inner'), window_pairs())  8.29 us
    pallas_call x2, Pallas kernels, score_grads(): pl.pallas_call(lambda *refs: score_grads_body(h, *refs), in_specs=[VM] *...  5.63 us
    ppermute x1, starting transfers between devices, to_prior(): lax.ppermute(value, ('outer', 'inner'), [(b, a) for a, b in window_pairs()])  4.24 us
    ppermute x1, waiting for transfers between devices, to_prior(): lax.ppermute(value, ('outer', 'inner'), [(b, a) for a, b in window_pairs()])  4.07 us
    ppermute x3, waiting for transfers between devices, along_x(): return lax.ppermute(value, 'inner', [(i, i ^ 1) for i in range(8)])  3.96 us
    ppermute x2, starting transfers between devices, to_next(): return lax.ppermute(value, ('outer', 'inner'), window_pairs())  3.83 us
  transfers between devices with their start and end apart: 13, of which 6 were waited for; matrix products, arithmetic and copies ran while one was open for 0% of the time, Pallas kernels for 17%

profile of v3, /device:TPU:8, one launch (start us, length us, event | category | flops | bytes accessed | tf_op | source)
XLA Modules:
  0.0 78.4 jit_solution(7000421856291781688)
XLA Ops:
  0.6 1.2 %pack_keys.1.k0.refs_4_ = bf16[512,384]{1,0:T(8,128)(2,1)S(1)} custom-call(bf16[384,256]{1,0:T(8,128)(2,1)} %k.1, bf16[384,256]{1,0:T(8,128)(2,1)} %v.1), custom_call_target="tpu_custom_call" | custom-call | tf_op jit(solution)/shard_map/pack_keys/pallas_call | solution.py:71
  1.9 3.4 %collective-permute-start.3 = (bf16[512,384]{1,0:T(8,128)(2,1)S(1)}, bf16[512,384]{1,0:T(8,128)(2,1)S(1)}, u32[]{:S(2)}, u32[]{:S(2)}) collective-permute-start(bf16[512,384]{1,0:T(8,128)(2,1)S(1)} %pack_keys.1.k0.refs_4_), channel_id=1, source_target_pairs={{0,1},{1,0},{2,3},{3,2},{4,5},{5,4},{6,7},{7,6},{8,9},{9,8},{10,11... | collective-permute-start | bytes 1179656 | tf_op jit(solution)/shard_map/ppermute | solution.py:357
  5.3 1.4 %pack_queries.1.own.refs_0_ = bf16[528,384]{1,0:T(8,128)(2,1)S(1)} custom-call(bf16[384,256]{1,0:T(8,128)(2,1)} %q.1, bf16[384,256]{1,0:T(8,128)(2,1)} %o.1, bf16[384,256]{1,0:T(8,128)(2,1)} %g.1), custom_call_target="tpu_custom_call" | custom-call | tf_op jit(solution)/shard_map/pack_queries/pallas_call | solution.py:83
  6.7 3.5 %collective-permute-start = (bf16[528,384]{1,0:T(8,128)(2,1)S(1)}, bf16[528,384]{1,0:T(8,128)(2,1)S(1)}, u32[]{:S(2)}, u32[]{:S(2)}) collective-permute-start(bf16[528,384]{1,0:T(8,128)(2,1)S(1)} %pack_queries.1.own.refs_0_), channel_id=1, source_target_pairs={{0,6},{1,7},{2,4},{3,5},{4,2},{5,3},{6,0},{7,1},{8,10},{9,11},{10,... | collective-permute-start | bytes 1216520 | tf_op jit(solution)/shard_map/ppermute | solution.py:353
  10.2 1.9 %collective-permute-start.4 = (bf16[512,384]{1,0:T(8,128)(2,1)S(1)}, bf16[512,384]{1,0:T(8,128)(2,1)S(1)}, u32[]{:S(2)}, u32[]{:S(2)}) collective-permute-start(bf16[512,384]{1,0:T(8,128)(2,1)S(1)} %pack_keys.1.k0.refs_4_), channel_id=1, source_target_pairs={{0,8},{1,9},{2,10},{3,11},{4,12},{5,13},{6,14},{7,15},{8,16},{9,17... | collective-permute-start | bytes 1179656 | tf_op jit(solution)/shard_map/ppermute | solution.py:371
  12.1 2.5 %collective-permute-done.3.k1.refs_5_ = bf16[512,384]{1,0:T(8,128)(2,1)S(1)} collective-permute-done((bf16[512,384]{1,0:T(8,128)(2,1)S(1)}, bf16[512,384]{1,0:T(8,128)(2,1)S(1)}, u32[]{:S(2)}, u32[]{:S(2)}) %collective-permute-start.3) | collective-permute-done | bytes 393248 | tf_op jit(solution)/shard_map/ppermute | solution.py:357
  14.6 1.9 %collective-permute-start.5 = (bf16[512,384]{1,0:T(8,128)(2,1)S(1)}, bf16[512,384]{1,0:T(8,128)(2,1)S(1)}, u32[]{:S(2)}, u32[]{:S(2)}) collective-permute-start(bf16[512,384]{1,0:T(8,128)(2,1)S(1)} %collective-permute-done.3.k1.refs_5_), channel_id=1, source_target_pairs={{0,8},{1,9},{2,10},{3,11},{4,12},{5,13},{6,14},{7,15},{8,16},{9,17... | collective-permute-start | bytes 1179656 | tf_op jit(solution)/shard_map/ppermute | solution.py:371
  16.5 4.7 %collective-permute-start.1 = (bf16[528,384]{1,0:T(8,128)(2,1)S(1)}, bf16[528,384]{1,0:T(8,128)(2,1)S(1)}, u32[]{:S(2)}, u32[]{:S(2)}) collective-permute-start(bf16[528,384]{1,0:T(8,128)(2,1)S(1)} %pack_queries.1.own.refs_0_), channel_id=1, source_target_pairs={{0,2},{1,3},{2,0},{3,1},{4,6},{5,7},{6,4},{7,5},{8,14},{9,15},{10,... | collective-permute-start | bytes 1216520 | tf_op jit(solution)/shard_map/ppermute | solution.py:353
  21.2 0.0 collective-permute-done.first.refs_1_
  21.2 2.7 %collective-permute-start.2 = (bf16[528,384]{1,0:T(8,128)(2,1)S(1)}, bf16[528,384]{1,0:T(8,128)(2,1)S(1)}, u32[]{:S(2)}, u32[]{:S(2)}) collective-permute-start(bf16[528,384]{1,0:T(8,128)(2,1)S(1)} %collective-permute-done.first.refs_1_), channel_id=1, source_target_pairs={{0,2},{1,3},{2,0},{3,1},{4,6},{5,7},{6,4},{7,5},{8,14},{9,15},{10,... | collective-permute-start | bytes 1216520 | tf_op jit(solution)/shard_map/ppermute | solution.py:353
  23.9 2.4 %collective-permute-done.4.k2.refs_6_ = bf16[512,384]{1,0:T(8,128)(2,1)S(1)} collective-permute-done((bf16[512,384]{1,0:T(8,128)(2,1)S(1)}, bf16[512,384]{1,0:T(8,128)(2,1)S(1)}, u32[]{:S(2)}, u32[]{:S(2)}) %collective-permute-start.4) | collective-permute-done | bytes 393248 | tf_op jit(solution)/shard_map/ppermute | solution.py:371
  26.3 5.9 %collective-permute-done.5.k3.refs_7_ = bf16[512,384]{1,0:T(8,128)(2,1)S(1)} collective-permute-done((bf16[512,384]{1,0:T(8,128)(2,1)S(1)}, bf16[512,384]{1,0:T(8,128)(2,1)S(1)}, u32[]{:S(2)}, u32[]{:S(2)}) %collective-permute-start.5) | collective-permute-done | bytes 393248 | tf_op jit(solution)/shard_map/ppermute | solution.py:371
  32.2 2.6 %first_scores.1 = (bf16[2,1536,1536]{2,1,0:T(8,128)(2,1)S(1)}, f32[8,1536]{1,0:T(8,128)S(1)}, bf16[2,256,1536]{2,1,0:T(8,128)(2,1)S(1)}) custom-call(bf16[528,384]{1,0:T(8,128)(2,1)S(1)} %pack_queries.1.own.refs_0_, bf16[528,384]{1,0:T(8,128)(2,1)S(1)} %collective-permute-done.first.refs_1_, bf16[512,384]{1,0:T(8,128)(2,1)S(1)} %pack_keys.1.k0.refs_4_, ...), custom_call_target="tpu_custom_call" | custom-call | flops 8999999488 | tf_op jit(solution)/shard_map/first_scores/pallas_call | solution.py:119
  34.8 0.0 collective-permute-done.1.second.refs_2_
  34.8 0.0 collective-permute-done.2.third.refs_3_
  34.8 2.5 %last_scores.1 = (bf16[2,1536,1536]{2,1,0:T(8,128)(2,1)S(1)}, f32[8,1536]{1,0:T(8,128)S(1)}) custom-call(bf16[528,384]{1,0:T(8,128)(2,1)S(1)} %collective-permute-done.1.second.refs_2_, bf16[528,384]{1,0:T(8,128)(2,1)S(1)} %collective-permute-done.2.third.refs_3_, ...), custom_call_target="tpu_custom_call", output_to_operand_aliasing={{0}: (3, {})} | custom-call | flops 3000000000 | tf_op jit(solution)/shard_map/last_scores/pallas_call | solution.py:140
  37.3 3.5 %collective-permute-start.6 = (f32[8,1536]{1,0:T(8,128)S(1)}, f32[8,1536]{1,0:T(8,128)S(1)}, u32[]{:S(2)}, u32[]{:S(2)}) collective-permute-start(f32[8,1536]{1,0:T(8,128)S(1)} %get-tuple-element.26.a.refs_4_), channel_id=1, source_target_pairs={{0,6},{1,7},{2,4},{3,5},{4,2},{5,3},{6,0},{7,1},{8,10},{9,11},{10,... | collective-permute-start | bytes 147464 | tf_op jit(solution)/shard_map/ppermute | solution.py:353
  40.8 2.8 %score_grads.2 = (bf16[1536,1536]{1,0:T(8,128)(2,1)S(1)}, f32[1536,128]{1,0:T(8,128)S(1)}) custom-call(bf16[528,384]{1,0:T(8,128)(2,1)S(1)} %pack_queries.1.own.refs_0_, bf16[528,384]{1,0:T(8,128)(2,1)S(1)} %collective-permute-done.first.refs_1_, bf16[528,384]{1,0:T(8,128)(2,1)S(1)} %collective-permute-done.1.second.refs_2_, ...), custom_call_target="tpu_custom_call" | custom-call | tf_op jit(solution)/shard_map/score_grads/pallas_call | solution.py:195
  43.6 0.0 collective-permute-done.6.b
  43.6 4.0 %collective-permute-start.7 = (f32[8,1536]{1,0:T(8,128)S(1)}, f32[8,1536]{1,0:T(8,128)S(1)}, u32[]{:S(2)}, u32[]{:S(2)}) collective-permute-start(f32[8,1536]{1,0:T(8,128)S(1)} %merge.1.refs_5_), channel_id=1, source_target_pairs={{0,2},{1,3},{2,0},{3,1},{4,6},{5,7},{6,4},{7,5},{8,14},{9,15},{10,... | collective-permute-start | bytes 147464 | tf_op jit(solution)/shard_map/ppermute | solution.py:353
  47.6 2.8 %score_grads.3 = (bf16[1536,1536]{1,0:T(8,128)(2,1)S(1)}, f32[1536,128]{1,0:T(8,128)S(1)}) custom-call(bf16[528,384]{1,0:T(8,128)(2,1)S(1)} %pack_queries.1.own.refs_0_, bf16[528,384]{1,0:T(8,128)(2,1)S(1)} %collective-permute-done.first.refs_1_, bf16[528,384]{1,0:T(8,128)(2,1)S(1)} %collective-permute-done.1.second.refs_2_, ...), custom_call_target="tpu_custom_call" | custom-call | tf_op jit(solution)/shard_map/score_grads/pallas_call | solution.py:195
  50.4 0.0 collective-permute-done.7.refs_6_
  50.5 1.1 %prior_partner.1 = (bf16[512,384]{1,0:T(8,128)(2,1)S(1)}, bf16[2,2,128,1536]{3,2,1,0:T(8,128)(2,1)S(1)}, f32[768,256]{1,0:T(8,128)S(1)}, bf16[768,256]{1,0:T(8,128)(2,1)S(1)}) custom-call(bf16[528,384]{1,0:T(8,128)(2,1)S(1)} %pack_queries.1.own.refs_0_, bf16[528,384]{1,0:T(8,128)(2,1)S(1)} %collective-permute-done.first.refs_1_, ...), custom_call_target="tpu_custom_call" | custom-call | tf_op jit(solution)/shard_map/prior_partner/pallas_call | solution.py:236
  51.6 3.0 %collective-permute-start.8 = (bf16[768,256]{1,0:T(8,128)(2,1)S(1)}, bf16[768,256]{1,0:T(8,128)(2,1)S(1)}, u32[]{:S(2)}, u32[]{:S(2)}) collective-permute-start(bf16[768,256]{1,0:T(8,128)(2,1)S(1)} %get-tuple-element.33), channel_id=1, source_target_pairs={{0,2},{1,3},{2,0},{3,1},{4,6},{5,7},{6,4},{7,5},{8,14},{9,15},{10,... | collective-permute-start | bytes 1179656 | tf_op jit(solution)/shard_map/ppermute | solution.py:353
  54.6 2.1 %collective-permute-start.11 = (bf16[512,384]{1,0:T(8,128)(2,1)S(1)}, bf16[512,384]{1,0:T(8,128)(2,1)S(1)}, u32[]{:S(2)}, u32[]{:S(2)}) collective-permute-start(bf16[512,384]{1,0:T(8,128)(2,1)S(1)} %get-tuple-element.40), channel_id=1, source_target_pairs={{0,1},{1,0},{2,3},{3,2},{4,5},{5,4},{6,7},{7,6},{8,9},{9,8},{10,11... | collective-permute-start | bytes 1179656 | tf_op jit(solution)/shard_map/ppermute | solution.py:357
  56.7 2.6 %key_grads.1 = (bf16[512,384]{1,0:T(8,128)(2,1)S(1)}, f32[512,384]{1,0:T(8,128)S(1)}, f32[512,384]{1,0:T(8,128)S(1)}) custom-call(bf16[2,2,128,1536]{3,2,1,0:T(8,128)(2,1)S(1)} %get-tuple-element.34.xs, bf16[2,1536,1536]{2,1,0:T(8,128)(2,1)S(1)} %get-tuple-element.27.refs_9_.refs_7_.p_ref, bf16[1536,1536]{1,0:T(8,128)(2,1)S(1)} %get-tuple-element.29.refs_8_.ds0, ...), custom_call_target="tpu_custom_call" | custom-call | tf_op jit(solution)/shard_map/key_grads/pallas_call | solution.py:260
  59.3 3.7 %collective-permute-start.10 = (bf16[512,384]{1,0:T(8,128)(2,1)S(1)}, bf16[512,384]{1,0:T(8,128)(2,1)S(1)}, u32[]{:S(2)}, u32[]{:S(2)}) collective-permute-start(bf16[512,384]{1,0:T(8,128)(2,1)S(1)} %get-tuple-element.35.after), channel_id=1, source_target_pairs={{0,1},{1,0},{2,3},{3,2},{4,5},{5,4},{6,7},{7,6},{8,9},{9,8},{10,11... | collective-permute-start | bytes 1179656 | tf_op jit(solution)/shard_map/ppermute | solution.py:357
  63.0 0.0 collective-permute-done.8.far
  63.1 0.1 query_mid.1
  63.1 3.8 %collective-permute-start.9 = (bf16[384,256]{1,0:T(8,128)(2,1)S(1)}, bf16[384,256]{1,0:T(8,128)(2,1)S(1)}, u32[]{:S(2)}, u32[]{:S(2)}) collective-permute-start(bf16[384,256]{1,0:T(8,128)(2,1)S(1)} %get-tuple-element.37.after), channel_id=1, source_target_pairs={{0,6},{1,7},{2,4},{3,5},{4,2},{5,3},{6,0},{7,1},{8,10},{9,11},{10,... | collective-permute-start | bytes 589832 | tf_op jit(solution)/shard_map/ppermute | solution.py:353
  66.9 1.1 %collective-permute-done.11.b = bf16[512,384]{1,0:T(8,128)(2,1)S(1)} collective-permute-done((bf16[512,384]{1,0:T(8,128)(2,1)S(1)}, bf16[512,384]{1,0:T(8,128)(2,1)S(1)}, u32[]{:S(2)}, u32[]{:S(2)}) %collective-permute-start.11) | collective-permute-done | bytes 393248 | tf_op jit(solution)/shard_map/ppermute | solution.py:357
  68.0 0.1 prior_sum.1
  68.0 4.2 %collective-permute-start.12 = (bf16[512,384]{1,0:T(8,128)(2,1)S(1)}, bf16[512,384]{1,0:T(8,128)(2,1)S(1)}, u32[]{:S(2)}, u32[]{:S(2)}) collective-permute-start(bf16[512,384]{1,0:T(8,128)(2,1)S(1)} %prior_sum.1), channel_id=1, source_target_pairs={{8,0},{9,1},{10,2},{11,3},{12,4},{13,5},{14,6},{15,7},{16,8},{17,9... | collective-permute-start | bytes 1179656 | tf_op jit(solution)/shard_map/ppermute | solution.py:375
  72.3 0.4 collective-permute-done.10.other
  72.7 0.1 own_sum.1.own
  72.8 0.0 collective-permute-done.9.pair
  72.8 0.7 query_sum.1
  73.5 4.1 %collective-permute-done.12.back = bf16[512,384]{1,0:T(8,128)(2,1)S(1)} collective-permute-done((bf16[512,384]{1,0:T(8,128)(2,1)S(1)}, bf16[512,384]{1,0:T(8,128)(2,1)S(1)}, u32[]{:S(2)}, u32[]{:S(2)}) %collective-permute-start.12) | collective-permute-done | bytes 393248 | tf_op jit(solution)/shard_map/ppermute | solution.py:375
  77.6 0.9 %key_sum.1 = (bf16[384,256]{1,0:T(8,128)(2,1)}, bf16[384,256]{1,0:T(8,128)(2,1)}) custom-call(f32[512,384]{1,0:T(8,128)S(1)} %own_sum.1.own, bf16[512,384]{1,0:T(8,128)(2,1)S(1)} %collective-permute-done.12.back), custom_call_target="tpu_custom_call" | custom-call | tf_op jit(solution)/shard_map/key_sum/pallas_call | solution.py:339
  (1 shorter events, 0.0 us)
Async XLA Ops:
  1.9 12.7 %collective-permute-start.3 = (bf16[512,384]{1,0:T(8,128)(2,1)S(1)}, bf16[512,384]{1,0:T(8,128)(2,1)S(1)}, u32[]{:S(2)}, u32[]{:S(2)}) collective-permute-start(bf16[512,384]{1,0:T(8,128)(2,1)S(1)} %pack_keys.1.k0.refs_4_), channel_id=1, source_target_pairs={{0,1},{1,0},{2,3},{3,2},{4,5},{5,4},{6,7},{7,6},{8,9},{9,8},{10,11... | collective-permute-start | bytes 1179656 | tf_op jit(solution)/shard_map/ppermute | solution.py:357
  6.7 14.5 %collective-permute-start = (bf16[528,384]{1,0:T(8,128)(2,1)S(1)}, bf16[528,384]{1,0:T(8,128)(2,1)S(1)}, u32[]{:S(2)}, u32[]{:S(2)}) collective-permute-start(bf16[528,384]{1,0:T(8,128)(2,1)S(1)} %pack_queries.1.own.refs_0_), channel_id=1, source_target_pairs={{0,6},{1,7},{2,4},{3,5},{4,2},{5,3},{6,0},{7,1},{8,10},{9,11},{10,... | collective-permute-start | bytes 1216520 | tf_op jit(solution)/shard_map/ppermute | solution.py:353
  10.2 16.1 %collective-permute-start.4 = (bf16[512,384]{1,0:T(8,128)(2,1)S(1)}, bf16[512,384]{1,0:T(8,128)(2,1)S(1)}, u32[]{:S(2)}, u32[]{:S(2)}) collective-permute-start(bf16[512,384]{1,0:T(8,128)(2,1)S(1)} %pack_keys.1.k0.refs_4_), channel_id=1, source_target_pairs={{0,8},{1,9},{2,10},{3,11},{4,12},{5,13},{6,14},{7,15},{8,16},{9,17... | collective-permute-start | bytes 1179656 | tf_op jit(solution)/shard_map/ppermute | solution.py:371
  14.6 17.6 %collective-permute-start.5 = (bf16[512,384]{1,0:T(8,128)(2,1)S(1)}, bf16[512,384]{1,0:T(8,128)(2,1)S(1)}, u32[]{:S(2)}, u32[]{:S(2)}) collective-permute-start(bf16[512,384]{1,0:T(8,128)(2,1)S(1)} %collective-permute-done.3.k1.refs_5_), channel_id=1, source_target_pairs={{0,8},{1,9},{2,10},{3,11},{4,12},{5,13},{6,14},{7,15},{8,16},{9,17... | collective-permute-start | bytes 1179656 | tf_op jit(solution)/shard_map/ppermute | solution.py:371
  16.5 18.3 %collective-permute-start.1 = (bf16[528,384]{1,0:T(8,128)(2,1)S(1)}, bf16[528,384]{1,0:T(8,128)(2,1)S(1)}, u32[]{:S(2)}, u32[]{:S(2)}) collective-permute-start(bf16[528,384]{1,0:T(8,128)(2,1)S(1)} %pack_queries.1.own.refs_0_), channel_id=1, source_target_pairs={{0,2},{1,3},{2,0},{3,1},{4,6},{5,7},{6,4},{7,5},{8,14},{9,15},{10,... | collective-permute-start | bytes 1216520 | tf_op jit(solution)/shard_map/ppermute | solution.py:353
  21.2 13.6 %collective-permute-start.2 = (bf16[528,384]{1,0:T(8,128)(2,1)S(1)}, bf16[528,384]{1,0:T(8,128)(2,1)S(1)}, u32[]{:S(2)}, u32[]{:S(2)}) collective-permute-start(bf16[528,384]{1,0:T(8,128)(2,1)S(1)} %collective-permute-done.first.refs_1_), channel_id=1, source_target_pairs={{0,2},{1,3},{2,0},{3,1},{4,6},{5,7},{6,4},{7,5},{8,14},{9,15},{10,... | collective-permute-start | bytes 1216520 | tf_op jit(solution)/shard_map/ppermute | solution.py:353
  37.3 6.3 %collective-permute-start.6 = (f32[8,1536]{1,0:T(8,128)S(1)}, f32[8,1536]{1,0:T(8,128)S(1)}, u32[]{:S(2)}, u32[]{:S(2)}) collective-permute-start(f32[8,1536]{1,0:T(8,128)S(1)} %get-tuple-element.26.a.refs_4_), channel_id=1, source_target_pairs={{0,6},{1,7},{2,4},{3,5},{4,2},{5,3},{6,0},{7,1},{8,10},{9,11},{10,... | collective-permute-start | bytes 147464 | tf_op jit(solution)/shard_map/ppermute | solution.py:353
  43.6 6.8 %collective-permute-start.7 = (f32[8,1536]{1,0:T(8,128)S(1)}, f32[8,1536]{1,0:T(8,128)S(1)}, u32[]{:S(2)}, u32[]{:S(2)}) collective-permute-start(f32[8,1536]{1,0:T(8,128)S(1)} %merge.1.refs_5_), channel_id=1, source_target_pairs={{0,2},{1,3},{2,0},{3,1},{4,6},{5,7},{6,4},{7,5},{8,14},{9,15},{10,... | collective-permute-start | bytes 147464 | tf_op jit(solution)/shard_map/ppermute | solution.py:353
  51.6 11.4 %collective-permute-start.8 = (bf16[768,256]{1,0:T(8,128)(2,1)S(1)}, bf16[768,256]{1,0:T(8,128)(2,1)S(1)}, u32[]{:S(2)}, u32[]{:S(2)}) collective-permute-start(bf16[768,256]{1,0:T(8,128)(2,1)S(1)} %get-tuple-element.33), channel_id=1, source_target_pairs={{0,2},{1,3},{2,0},{3,1},{4,6},{5,7},{6,4},{7,5},{8,14},{9,15},{10,... | collective-permute-start | bytes 1179656 | tf_op jit(solution)/shard_map/ppermute | solution.py:353
  54.6 13.4 %collective-permute-start.11 = (bf16[512,384]{1,0:T(8,128)(2,1)S(1)}, bf16[512,384]{1,0:T(8,128)(2,1)S(1)}, u32[]{:S(2)}, u32[]{:S(2)}) collective-permute-start(bf16[512,384]{1,0:T(8,128)(2,1)S(1)} %get-tuple-element.40), channel_id=1, source_target_pairs={{0,1},{1,0},{2,3},{3,2},{4,5},{5,4},{6,7},{7,6},{8,9},{9,8},{10,11... | collective-permute-start | bytes 1179656 | tf_op jit(solution)/shard_map/ppermute | solution.py:357
  59.3 13.3 %collective-permute-start.10 = (bf16[512,384]{1,0:T(8,128)(2,1)S(1)}, bf16[512,384]{1,0:T(8,128)(2,1)S(1)}, u32[]{:S(2)}, u32[]{:S(2)}) collective-permute-start(bf16[512,384]{1,0:T(8,128)(2,1)S(1)} %get-tuple-element.35.after), channel_id=1, source_target_pairs={{0,1},{1,0},{2,3},{3,2},{4,5},{5,4},{6,7},{7,6},{8,9},{9,8},{10,11... | collective-permute-start | bytes 1179656 | tf_op jit(solution)/shard_map/ppermute | solution.py:357
  63.1 9.6 %collective-permute-start.9 = (bf16[384,256]{1,0:T(8,128)(2,1)S(1)}, bf16[384,256]{1,0:T(8,128)(2,1)S(1)}, u32[]{:S(2)}, u32[]{:S(2)}) collective-permute-start(bf16[384,256]{1,0:T(8,128)(2,1)S(1)} %get-tuple-element.37.after), channel_id=1, source_target_pairs={{0,6},{1,7},{2,4},{3,5},{4,2},{5,3},{6,0},{7,1},{8,10},{9,11},{10,... | collective-permute-start | bytes 589832 | tf_op jit(solution)/shard_map/ppermute | solution.py:353
  68.0 9.5 %collective-permute-start.12 = (bf16[512,384]{1,0:T(8,128)(2,1)S(1)}, bf16[512,384]{1,0:T(8,128)(2,1)S(1)}, u32[]{:S(2)}, u32[]{:S(2)}) collective-permute-start(bf16[512,384]{1,0:T(8,128)(2,1)S(1)} %prior_sum.1), channel_id=1, source_target_pairs={{8,0},{9,1},{10,2},{11,3},{12,4},{13,5},{14,6},{15,7},{16,8},{17,9... | collective-permute-start | bytes 1179656 | tf_op jit(solution)/shard_map/ppermute | solution.py:375

commit v4 on v3

v4 whole, which is shorter than its diff:
```python
import jax
import jax.numpy as jnp
from jax import lax
from jax.experimental import pallas as pl
from jax.experimental.pallas import tpu as pltpu
from jax.sharding import PartitionSpec as P

R = 384
D = 128
SCALE = D ** -0.5
C = SCALE * 1.4426950408889634
NQ = 4 * R
NK = 4 * R
GROUPS = (slice(0, 3 * R), slice(3 * R, NK))
F32 = jnp.float32
BF = jnp.bfloat16
VM = pl.BlockSpec(memory_space=pltpu.VMEM)
HBM = pl.BlockSpec(memory_space=pltpu.HBM)
PARAMS = pltpu.CompilerParams(vmem_limit_bytes=16 * 1024 * 1024)
ALONE = pltpu.CompilerParams(vmem_limit_bytes=60 * 1024 * 1024)


def dot(a, b, ca, cb):
    return lax.dot_general(a, b, (((ca,), (cb,)), ((), ())), preferred_element_type=F32)


def chunk(n):
    return slice(n * R, (n + 1) * R)


def head(h, base=0):
    return slice(base + h * D, base + (h + 1) * D)


def turned(ref):
    return ref[...].astype(F32).T


def pack_keys_body(k, v, q, o, g, kv, qs, os, gs, ks, vs, sems):
    copies = [
        pltpu.make_async_copy(src, dst, sems.at[n])
        for n, (src, dst) in enumerate(((k, ks), (v, vs), (q, qs), (o, os), (g, gs)))
    ]
    for copy in copies:
        copy.start()
    copies[0].wait()
    kv[0:256] = turned(ks).astype(BF)
    copies[1].wait()
    kv[256:512] = turned(vs).astype(BF)
    for copy in copies[2:]:
        copy.wait()


def pack_keys(k, v, q, o, g):
    return pl.pallas_call(
        pack_keys_body,
        in_specs=[HBM] * 5,
        out_specs=[VM] * 4,
        out_shape=[pltpu.VMEM((512, R), BF)] + [pltpu.VMEM((R, 2 * D), BF)] * 3,
        scratch_shapes=[pltpu.VMEM((R, 2 * D), BF)] * 2 + [pltpu.SemaphoreType.DMA((5,))],
        compiler_params=ALONE,
        name="pack_keys",
    )(k, v, q, o, g)


def pack_queries_body(q, o, g, qg):
    qg[0:256] = turned(q).astype(BF)
    grads = turned(g)
    qg[256:512] = grads.astype(BF)
    prod = grads * turned(o)
    rows = []
    for h in range(2):
        d = jnp.sum(prod[head(h)], axis=0, keepdims=True)
        hi = d.astype(BF).astype(F32)
        mid = (d - hi).astype(BF).astype(F32)
        rows += [hi, mid, d - hi - mid]
    qg[512:528] = jnp.concatenate(rows + [jnp.zeros((10, R), F32)], axis=0).astype(BF)


def pack_queries(q, o, g):
    return pl.pallas_call(
        pack_queries_body,
        in_specs=[VM] * 3,
        out_specs=VM,
        out_shape=pltpu.VMEM((528, R), BF),
        compiler_params=PARAMS,
        name="pack_queries",
    )(q, o, g)


def score_tile(n, h, q, ks, group, cols, p_ref, st):
    scaled = q[head(h), :].astype(F32) * C
    high = scaled.astype(BF)
    low = (scaled - high.astype(F32)).astype(BF)
    s = dot(jnp.concatenate([high, low], axis=0), ks[h, :, cols], 0, 0)
    m = jnp.max(s, axis=1, keepdims=True)
    p = jnp.exp2(s - m)
    at = 4 * group + h
    st[n, :, at:at + 1] = m
    st[n, :, at + 2:at + 3] = jnp.sum(p, axis=1, keepdims=True)
    p_ref[h, chunk(n), cols] = p.astype(BF)
    return m


def lay_keys(ks, n, ref):
    for h in range(2):
        ks[h, 0:D, chunk(n)] = ref[head(h), :]
        ks[h, D:2 * D, chunk(n)] = ref[head(h), :]


def first_scores_body(own, first, second, k0, k1, k2, p_ref, st_ref, ks, st):
    for n, ref in enumerate((k0, k1, k2)):
        lay_keys(ks, n, ref)
    for n, q in enumerate((own, first, second)):
        for h in range(2):
            score_tile(n, h, q, ks, 0, GROUPS[0], p_ref, st)
        st_ref[0:4, chunk(n)] = st[n].T[0:4, :]


def first_scores(qg, kv):
    return pl.pallas_call(
        first_scores_body,
        in_specs=[VM] * 6,
        out_specs=[VM] * 3,
        out_shape=[pltpu.VMEM((2, NQ, NK), BF), pltpu.VMEM((8, NQ), F32), pltpu.VMEM((2, 2 * D, NK), BF)],
        scratch_shapes=[pltpu.VMEM((3, R, D), F32)],
        compiler_params=PARAMS,
        cost_estimate=pl.CostEstimate(flops=3 * 10 ** 9, bytes_accessed=0, transcendentals=0),
        name="first_scores",
    )(*qg[0:3], *kv[0:3])


def last_keys_body(k3, ks_in, ks):
    lay_keys(ks, 3, k3)


def last_keys(k3, ks):
    return pl.pallas_call(
        last_keys_body,
        in_specs=[VM] * 2,
        out_specs=VM,
        out_shape=pltpu.VMEM((2, 2 * D, NK), BF),
        input_output_aliases={1: 0},
        compiler_params=PARAMS,
        cost_estimate=pl.CostEstimate(flops=6 * 10 ** 9, bytes_accessed=0, transcendentals=0),
        name="last_keys",
    )(k3, ks)


def last_scores_body(own, first, second, third, ks, p_in, st_in, p_ref, st_ref, both_ref, st):
    st_ref[0:4, 0:3 * R] = st_in[0:4, 0:3 * R]
    for n, q in enumerate((own, first, second, third)):
        for h in range(2):
            if n == 3:
                m = score_tile(n, h, q, ks, 0, slice(0, NK), p_ref, st)
                st[n, :, 4 + h:5 + h] = m
                st[n, :, 6 + h:7 + h] = jnp.zeros((R, 1), F32)
            else:
                score_tile(n, h, q, ks, 1, GROUPS[1], p_ref, st)
        rows = st[n].T
        if n == 3:
            st_ref[0:4, chunk(n)] = rows[0:4, :]
        st_ref[4:8, chunk(n)] = rows[4:8, :]
    top, total = combined(st_ref[0:2], st_ref[2:4], st_ref[4:6], st_ref[6:8])
    both_ref[0:2] = top
    both_ref[2:4] = total
    both_ref[4:8] = jnp.zeros((4, NQ), F32)


def last_scores(qg, ks, p, st):
    return pl.pallas_call(
        last_scores_body,
        in_specs=[VM] * 7,
        out_specs=[VM] * 3,
        out_shape=[pltpu.VMEM((2, NQ, NK), BF), pltpu.VMEM((8, NQ), F32), pltpu.VMEM((8, NQ), F32)],
        scratch_shapes=[pltpu.VMEM((4, R, D), F32)],
        input_output_aliases={5: 0},
        compiler_params=PARAMS,
        cost_estimate=pl.CostEstimate(flops=2 * 10 ** 9, bytes_accessed=0, transcendentals=0),
        name="last_scores",
    )(*qg, ks, p, st)


def combined(m0, l0, m1, l1):
    top = jnp.maximum(m0, m1)
    return top, l0 * jnp.exp2(m0 - top) + l1 * jnp.exp2(m1 - top)


def merged(a, b, m):
    b = jnp.concatenate([b[0:4, chunk(n ^ m)] for n in range(4)], axis=1)
    return combined(a[0:2], a[2:4], b[0:2], b[2:4])


def merge_body(a, b, after, out):
    top, total = merged(a[...], b[...], 1)
    out[0:2] = top
    out[2:4] = total
    out[4:8] = jnp.zeros((4, NQ), F32)


def merge(a, b, after):
    return pl.pallas_call(
        merge_body,
        in_specs=[VM] * 3,
        out_specs=VM,
        out_shape=pltpu.VMEM((8, NQ), F32),
        compiler_params=PARAMS,
        name="merge",
    )(a, b, after)


def score_grads_body(h, *refs):
    qg, kv, ks, p_ref = refs[0:4], refs[4:8], refs[8], refs[9]
    ds_ref, dq_ref, vs, gs = refs[10:]
    row = lax.broadcasted_iota(jnp.int32, (16, NK), 0)
    for n in range(4):
        vs[0:D, chunk(n)] = kv[n][head(h, 256), :]
        gs[n, 0:D, :] = qg[n][head(h, 256), :]
        gs[n, D:D + 16, :] = qg[n][512:528, :]
    vs[D:D + 16, :] = jnp.where((row >= 3 * h) & (row < 3 * h + 3), -1.0, 0.0).astype(BF)
    for n in range(4):
        pg = dot(gs[n], vs[...], 0, 0)
        ds = (p_ref[h, chunk(n), :].astype(F32) * pg).astype(BF)
        ds_ref[chunk(n), :] = ds
        for group, cols in enumerate(GROUPS):
            dq_ref[group, chunk(n), :] = dot(ds[:, cols], ks[h, 0:D, cols], 1, 1)


def score_grads(h, qg, kv, ks, p):
    return pl.pallas_call(
        lambda *refs: score_grads_body(h, *refs),
        in_specs=[VM] * 10,
        out_specs=[VM] * 2,
        out_shape=[pltpu.VMEM((NQ, NK), BF), pltpu.VMEM((2, NQ, D), F32)],
        scratch_shapes=[
            pltpu.VMEM((D + 16, NK), BF),
            pltpu.VMEM((4, D + 16, R), BF),
        ],
        compiler_params=PARAMS,
        name="score_grads",
    )(*qg, *kv, ks, p)


def key_part(out, xs, ds, p_ref, cols):
    for h in range(2):
        out[head(h), :] = dot(xs[h, 0], ds[h][:, cols], 1, 0).astype(out.dtype)
        out[head(h, 256), :] = dot(xs[h, 1], p_ref[h, :, cols], 1, 0).astype(out.dtype)


def scaled_rows(xs, qg, f):
    for h in range(2):
        for n in range(4):
            fn = f[h:h + 1, chunk(n)]
            xs[h, 0, :, chunk(n)] = (qg[n][head(h), :].astype(F32) * (fn * SCALE)).astype(BF)
            xs[h, 1, :, chunk(n)] = (qg[n][head(h, 256), :].astype(F32) * fn).astype(BF)


def prior_partner_body(*refs):
    qg, st, pair, other, p_ref, ds, dqs = refs[0:4], *refs[4:8], refs[8:10], refs[10:12]
    out, f_ref, near, far, xs = refs[12:]
    top, total = merged(pair[...], other[...], 2)
    f = [jnp.exp2(st[4 * group:4 * group + 2] - top) / total for group in range(2)]
    f_ref[0:2] = f[0]
    f_ref[2:8] = jnp.zeros((6, NQ), F32)
    scaled_rows(xs, qg, f[1])
    key_part(out, xs, ds, p_ref, chunk(3))
    out[512:528] = jnp.zeros((16, R), BF)
    cols = (jnp.concatenate([*f, jnp.zeros((4, NQ), F32)], axis=0) * SCALE).T
    for n in range(4):
        rows = chunk(n)
        for h, dq in enumerate(dqs):
            total = dq[0, rows] * cols[rows, h:h + 1] + dq[1, rows] * cols[rows, 2 + h:3 + h]
            if n < 2:
                near[chunk(n), head(h)] = total
            else:
                far[chunk(n - 2), head(h)] = total.astype(BF)


def prior_partner(qg, st, pair, other, p, ds, dq):
    return pl.pallas_call(
        prior_partner_body,
        in_specs=[VM] * 12,
        out_specs=[VM] * 4,
        out_shape=[
            pltpu.VMEM((528, R), BF),
            pltpu.VMEM((8, NQ), F32),
            pltpu.VMEM((2 * R, 2 * D), F32),
            pltpu.VMEM((2 * R, 2 * D), BF),
        ],
        scratch_shapes=[pltpu.VMEM((2, 2, D, NQ), BF)],
        compiler_params=PARAMS,
        name="prior_partner",
    )(*qg, st, pair, other, p, *ds, *dq)


def key_grads_body(*refs):
    qg, f_ref, p_ref, ds = refs[0:4], refs[4], refs[5], refs[6:8]
    own_partner, prior, own, xs = refs[8:]
    scaled_rows(xs, qg, f_ref[0:2])
    key_part(own_partner, xs, ds, p_ref, chunk(1))
    key_part(prior, xs, ds, p_ref, chunk(2))
    key_part(own, xs, ds, p_ref, chunk(0))


def key_grads(qg, f, p, ds):
    part = pltpu.VMEM((512, R), F32)
    return pl.pallas_call(
        key_grads_body,
        in_specs=[VM] * 8,
        out_specs=[VM] * 3,
        out_shape=[pltpu.VMEM((512, R), BF), part, part],
        scratch_shapes=[pltpu.VMEM((2, 2, D, NQ), BF)],
        compiler_params=PARAMS,
        name="key_grads",
    )(*qg, f, p, *ds)


def middle_sums_body(prior, part, near, far, out, own, pair):
    out[...] = (prior[...] + part[0:512].astype(F32)).astype(BF)
    own[...] = near[chunk(0), :] + far[chunk(0), :].astype(F32)
    pair[...] = (near[chunk(1), :] + far[chunk(1), :].astype(F32)).astype(BF)


def middle_sums(prior, part, near, far):
    return pl.pallas_call(
        middle_sums_body,
        in_specs=[VM] * 4,
        out_specs=[VM] * 3,
        out_shape=[pltpu.VMEM((512, R), BF), pltpu.VMEM((R, 2 * D), F32), pltpu.VMEM((R, 2 * D), BF)],
        compiler_params=PARAMS,
        name="middle_sums",
    )(prior, part, near, far)


def query_sum_body(own, pair, out):
    out[...] = (own[...] + pair[...].astype(F32)).astype(BF)


def query_sum(own, pair):
    return pl.pallas_call(
        query_sum_body,
        in_specs=[VM] * 2,
        out_shape=jax.ShapeDtypeStruct((R, 2 * D), BF),
        compiler_params=PARAMS,
        cost_estimate=pl.CostEstimate(flops=2 * 10 ** 9, bytes_accessed=0, transcendentals=0),
        name="query_sum",
    )(own, pair)


def own_sum_body(own, other, out):
    out[...] = own[...] + other[...].astype(F32)


def own_sum(own, other):
    return pl.pallas_call(
        own_sum_body,
        in_specs=[VM] * 2,
        out_specs=VM,
        out_shape=pltpu.VMEM((512, R), F32),
        compiler_params=PARAMS,
        cost_estimate=pl.CostEstimate(flops=8 * 10 ** 9, bytes_accessed=0, transcendentals=0),
        name="own_sum",
    )(own, other)


def key_sum_body(own, back, dk, dv):
    total = own[...] + back[...].astype(F32)
    dk[...] = total[0:256].T.astype(BF)
    dv[...] = total[256:512].T.astype(BF)


def key_sum(own, back):
    return pl.pallas_call(
        key_sum_body,
        in_specs=[VM] * 2,
        out_shape=[jax.ShapeDtypeStruct((R, 2 * D), BF)] * 2,
        compiler_params=PARAMS,
        name="key_sum",
    )(own, back)


def along_y(value, turn):
    outer, inner = lax.axis_size("outer"), lax.axis_size("inner")
    pairs = [
        (o * inner + i, o * inner + (i ^ (6 if o % 2 == turn else 2))) for o in range(outer) for i in range(inner)
    ]
    return lax.ppermute(value, ("outer", "inner"), pairs)


def along_x(value):
    return lax.ppermute(value, "inner", [(i, i ^ 1) for i in range(8)])


def window_pairs():
    outer, inner = lax.axis_size("outer"), lax.axis_size("inner")
    turn = outer // 2
    return [
        (o * inner + i, (o + 1) % outer * inner + (i ^ 1 if o % turn == turn - 1 else i))
        for o in range(outer)
        for i in range(inner)
    ]


def to_next(value):
    return lax.ppermute(value, ("outer", "inner"), window_pairs())


def to_prior(value):
    return lax.ppermute(value, ("outer", "inner"), [(b, a) for a, b in window_pairs()])


def on_device(queries, key_rows, value_rows, outputs, out_grad):
    kv_own, *rest = pack_keys(key_rows, value_rows, queries, outputs, out_grad)
    qg_own = pack_queries(*rest)
    kv_prior = to_next(kv_own)
    kv_partner = along_x(kv_own)
    kv = [kv_own, kv_partner, kv_prior, to_next(kv_partner)]
    qg_first = along_y(qg_own, 0)
    qg = [qg_own, qg_first, along_y(qg_own, 1), along_y(qg_first, 1)]
    p, st, ks = first_scores(qg, kv)
    ks = last_keys(kv[3], ks)
    p, st, both = last_scores(qg, ks, p, st)
    both_pair = along_y(both, 0)
    ds0, dq0 = score_grads(0, qg, kv, ks, p)
    pair = merge(both, both_pair, dq0)
    pair_other = along_y(pair, 1)
    ds1, dq1 = score_grads(1, qg, kv, ks, p)
    ds, dq = (ds0, ds1), (dq0, dq1)
    part, f, near, far = prior_partner(qg, st, pair, pair_other, p, ds, dq)
    part = along_x(part)
    far = along_y(far, 1)
    own_partner, prior, own = key_grads(qg, f, p, ds)
    other = along_x(own_partner)
    prior, near, pair = middle_sums(prior, part, near, far)
    back = to_prior(prior)
    query_grad = query_sum(near, along_y(pair, 0))
    key_grad, value_grad = key_sum(own_sum(own, other), back)
    return query_grad, key_grad, value_grad


def solution(mesh):
    spec = P(("outer", "inner"), None)
    return jax.shard_map(
        on_device, mesh=mesh, in_specs=(spec,) * 5, out_specs=(spec,) * 3, check_vma=False
    )
```

time: 78.9 us -> 77.5 us (0.982)
  the two profiles are of different devices: /device:TPU:8 before, /device:TPU:24 now
where the time goes in v4:
time: 77.5 us; the launch traced here: 77 us
  starting transfers between devices  39.3 us (51%)
  Pallas kernels  18.8 us (24%)
  waiting for transfers between devices  18.1 us (23%)
  between operations  0.81 us (1%)
    ppermute x7, starting transfers between devices, along_y(): return lax.ppermute(value, ('outer', 'inner'), pairs)  21.9 us
    ppermute x7, waiting for transfers between devices, along_y(): return lax.ppermute(value, ('outer', 'inner'), pairs)  12.2 us
    ppermute x3, starting transfers between devices, along_x(): return lax.ppermute(value, 'inner', [(i, i ^ 1) for i in range(8)])  9.24 us
    ppermute x2, waiting for transfers between devices, to_next(): return lax.ppermute(value, ('outer', 'inner'), window_pairs())  5.74 us
    pallas_call x2, Pallas kernels, score_grads(): pl.pallas_call(lambda *refs: score_grads_body(h, *refs), in_specs=[VM] *...  5.52 us
    ppermute x1, starting transfers between devices, to_prior(): lax.ppermute(value, ('outer', 'inner'), [(b, a) for a, b in window_pairs()])  4.33 us
    ppermute x2, starting transfers between devices, to_next(): return lax.ppermute(value, ('outer', 'inner'), window_pairs())  3.84 us
    pallas_call x1, Pallas kernels, first_scores(): pl.pallas_call(first_scores_body, in_specs=[VM] * 6, out_specs=[VM] * 3,...  3 us
  transfers between devices with their start and end apart: 13, of which 8 were waited for; matrix products, arithmetic and copies ran while one was open for 0% of the time, Pallas kernels for 16%

profile of v4, /device:TPU:24, one launch (start us, length us, event | category | flops | bytes accessed | tf_op | source)
XLA Modules:
  0.0 77.0 jit_solution(2973994191387797273)
XLA Ops:
  0.6 1.3 %pack_keys.1 = (bf16[512,384]{1,0:T(8,128)(2,1)S(1)}, bf16[384,256]{1,0:T(8,128)(2,1)S(1)}, bf16[384,256]{1,0:T(8,128)(2,1)S(1)}, bf16[384,256]{1,0:T(8,128)(2,1)S(1)}) custom-call(bf16[384,256]{1,0:T(8,128)(2,1)} %k.1, bf16[384,256]{1,0:T(8,128)(2,1)} %v.1, bf16[384,256]{1,0:T(8,128)(2,1)} %q.1, bf16[384,256]{1,0:T(8,128)(2,1)} %o.1, bf16[384,256]{1,0:T(8,128)(2,1)} %g.1), custom_call_target="tpu_custom_call" | custom-call | tf_op jit(solution)/shard_map/pack_keys/pallas_call | solution.py:55
  2.0 3.4 %collective-permute-start.3 = (bf16[512,384]{1,0:T(8,128)(2,1)S(1)}, bf16[512,384]{1,0:T(8,128)(2,1)S(1)}, u32[]{:S(2)}, u32[]{:S(2)}) collective-permute-start(bf16[512,384]{1,0:T(8,128)(2,1)S(1)} %get-tuple-element.32.k0.refs_4_), channel_id=1, source_target_pairs={{0,1},{1,0},{2,3},{3,2},{4,5},{5,4},{6,7},{7,6},{8,9},{9,8},{10,11... | collective-permute-start | bytes 1179656 | tf_op jit(solution)/shard_map/ppermute | solution.py:391
  5.4 0.3 pack_queries.1.own.refs_0_
  5.6 6.0 %collective-permute-start = (bf16[528,384]{1,0:T(8,128)(2,1)S(1)}, bf16[528,384]{1,0:T(8,128)(2,1)S(1)}, u32[]{:S(2)}, u32[]{:S(2)}) collective-permute-start(bf16[528,384]{1,0:T(8,128)(2,1)S(1)} %pack_queries.1.own.refs_0_), channel_id=1, source_target_pairs={{0,6},{1,7},{2,4},{3,5},{4,2},{5,3},{6,0},{7,1},{8,10},{9,11},{10,... | collective-permute-start | bytes 1216520 | tf_op jit(solution)/shard_map/ppermute | solution.py:387
  11.7 1.9 %collective-permute-start.1 = (bf16[528,384]{1,0:T(8,128)(2,1)S(1)}, bf16[528,384]{1,0:T(8,128)(2,1)S(1)}, u32[]{:S(2)}, u32[]{:S(2)}) collective-permute-start(bf16[528,384]{1,0:T(8,128)(2,1)S(1)} %pack_queries.1.own.refs_0_), channel_id=1, source_target_pairs={{0,2},{1,3},{2,0},{3,1},{4,6},{5,7},{6,4},{7,5},{8,14},{9,15},{10,... | collective-permute-start | bytes 1216520 | tf_op jit(solution)/shard_map/ppermute | solution.py:387
  13.6 1.9 %collective-permute-start.5 = (bf16[512,384]{1,0:T(8,128)(2,1)S(1)}, bf16[512,384]{1,0:T(8,128)(2,1)S(1)}, u32[]{:S(2)}, u32[]{:S(2)}) collective-permute-start(bf16[512,384]{1,0:T(8,128)(2,1)S(1)} %get-tuple-element.32.k0.refs_4_), channel_id=1, source_target_pairs={{0,8},{1,9},{2,10},{3,11},{4,12},{5,13},{6,14},{7,15},{8,16},{9,17... | collective-permute-start | bytes 1179656 | tf_op jit(solution)/shard_map/ppermute | solution.py:405
  15.5 0.0 collective-permute-done.3.k1.refs_5_
  15.5 1.9 %collective-permute-start.4 = (bf16[512,384]{1,0:T(8,128)(2,1)S(1)}, bf16[512,384]{1,0:T(8,128)(2,1)S(1)}, u32[]{:S(2)}, u32[]{:S(2)}) collective-permute-start(bf16[512,384]{1,0:T(8,128)(2,1)S(1)} %collective-permute-done.3.k1.refs_5_), channel_id=1, source_target_pairs={{0,8},{1,9},{2,10},{3,11},{4,12},{5,13},{6,14},{7,15},{8,16},{9,17... | collective-permute-start | bytes 1179656 | tf_op jit(solution)/shard_map/ppermute | solution.py:405
  17.5 4.3 %collective-permute-done.first.refs_1_ = bf16[528,384]{1,0:T(8,128)(2,1)S(1)} collective-permute-done((bf16[528,384]{1,0:T(8,128)(2,1)S(1)}, bf16[528,384]{1,0:T(8,128)(2,1)S(1)}, u32[]{:S(2)}, u32[]{:S(2)}) %collective-permute-start) | collective-permute-done | bytes 405536 | tf_op jit(solution)/shard_map/ppermute | solution.py:387
  21.8 1.9 %collective-permute-start.2 = (bf16[528,384]{1,0:T(8,128)(2,1)S(1)}, bf16[528,384]{1,0:T(8,128)(2,1)S(1)}, u32[]{:S(2)}, u32[]{:S(2)}) collective-permute-start(bf16[528,384]{1,0:T(8,128)(2,1)S(1)} %collective-permute-done.first.refs_1_), channel_id=1, source_target_pairs={{0,2},{1,3},{2,0},{3,1},{4,6},{5,7},{6,4},{7,5},{8,14},{9,15},{10,... | collective-permute-start | bytes 1216520 | tf_op jit(solution)/shard_map/ppermute | solution.py:387
  23.7 4.5 %collective-permute-done.5.k2.refs_6_ = bf16[512,384]{1,0:T(8,128)(2,1)S(1)} collective-permute-done((bf16[512,384]{1,0:T(8,128)(2,1)S(1)}, bf16[512,384]{1,0:T(8,128)(2,1)S(1)}, u32[]{:S(2)}, u32[]{:S(2)}) %collective-permute-start.5) | collective-permute-done | bytes 393248 | tf_op jit(solution)/shard_map/ppermute | solution.py:405
  28.2 0.0 collective-permute-done.1.second.refs_2_
  28.2 3.0 %first_scores.1 = (bf16[2,1536,1536]{2,1,0:T(8,128)(2,1)S(1)}, f32[8,1536]{1,0:T(8,128)S(1)}, bf16[2,256,1536]{2,1,0:T(8,128)(2,1)S(1)}) custom-call(bf16[528,384]{1,0:T(8,128)(2,1)S(1)} %pack_queries.1.own.refs_0_, bf16[528,384]{1,0:T(8,128)(2,1)S(1)} %collective-permute-done.first.refs_1_, bf16[528,384]{1,0:T(8,128)(2,1)S(1)} %collective-permute-done.1.second.refs_2_, ...), custom_call_target="tpu_custom_call" | custom-call | flops 3000000000 | tf_op jit(solution)/shard_map/first_scores/pallas_call | solution.py:121
  31.2 1.2 %collective-permute-done.4.k3.refs_7_ = bf16[512,384]{1,0:T(8,128)(2,1)S(1)} collective-permute-done((bf16[512,384]{1,0:T(8,128)(2,1)S(1)}, bf16[512,384]{1,0:T(8,128)(2,1)S(1)}, u32[]{:S(2)}, u32[]{:S(2)}) %collective-permute-start.4) | collective-permute-done | bytes 393248 | tf_op jit(solution)/shard_map/ppermute | solution.py:405
  32.5 0.0 collective-permute-done.2.third.refs_3_
  32.5 2.6 %last_scores.1 = (bf16[2,1536,1536]{2,1,0:T(8,128)(2,1)S(1)}, f32[8,1536]{1,0:T(8,128)S(1)}, f32[8,1536]{1,0:T(8,128)S(1)}) custom-call(bf16[528,384]{1,0:T(8,128)(2,1)S(1)} %pack_queries.1.own.refs_0_, bf16[528,384]{1,0:T(8,128)(2,1)S(1)} %collective-permute-done.first.refs_1_, ...), custom_call_target="tpu_custom_call", output_to_operand_aliasing={{0}: (5, {})} | custom-call | flops 2000000000 | tf_op jit(solution)/shard_map/last_scores/pallas_call | solution.py:171
  35.1 4.1 %collective-permute-start.6 = (f32[8,1536]{1,0:T(8,128)S(1)}, f32[8,1536]{1,0:T(8,128)S(1)}, u32[]{:S(2)}, u32[]{:S(2)}) collective-permute-start(f32[8,1536]{1,0:T(8,128)S(1)} %get-tuple-element.37.a), channel_id=1, source_target_pairs={{0,6},{1,7},{2,4},{3,5},{4,2},{5,3},{6,0},{7,1},{8,10},{9,11},{10,... | collective-permute-start | bytes 147464 | tf_op jit(solution)/shard_map/ppermute | solution.py:387
  39.2 2.8 %score_grads.2 = (bf16[1536,1536]{1,0:T(8,128)(2,1)S(1)}, f32[2,1536,128]{2,1,0:T(8,128)S(1)}) custom-call(bf16[528,384]{1,0:T(8,128)(2,1)S(1)} %pack_queries.1.own.refs_0_, bf16[528,384]{1,0:T(8,128)(2,1)S(1)} %collective-permute-done.first.refs_1_, bf16[528,384]{1,0:T(8,128)(2,1)S(1)} %collective-permute-done.1.second.refs_2_, ...), custom_call_target="tpu_custom_call" | custom-call | tf_op jit(solution)/shard_map/score_grads/pallas_call | solution.py:230
  42.0 0.6 collective-permute-done.6.b
  42.7 2.1 %collective-permute-start.7 = (f32[8,1536]{1,0:T(8,128)S(1)}, f32[8,1536]{1,0:T(8,128)S(1)}, u32[]{:S(2)}, u32[]{:S(2)}) collective-permute-start(f32[8,1536]{1,0:T(8,128)S(1)} %merge.1.refs_5_), channel_id=1, source_target_pairs={{0,2},{1,3},{2,0},{3,1},{4,6},{5,7},{6,4},{7,5},{8,14},{9,15},{10,... | collective-permute-start | bytes 147464 | tf_op jit(solution)/shard_map/ppermute | solution.py:387
  44.8 2.8 %score_grads.3 = (bf16[1536,1536]{1,0:T(8,128)(2,1)S(1)}, f32[2,1536,128]{2,1,0:T(8,128)S(1)}) custom-call(bf16[528,384]{1,0:T(8,128)(2,1)S(1)} %pack_queries.1.own.refs_0_, bf16[528,384]{1,0:T(8,128)(2,1)S(1)} %collective-permute-done.first.refs_1_, bf16[528,384]{1,0:T(8,128)(2,1)S(1)} %collective-permute-done.1.second.refs_2_, ...), custom_call_target="tpu_custom_call" | custom-call | tf_op jit(solution)/shard_map/score_grads/pallas_call | solution.py:230
  47.5 1.1 %collective-permute-done.7.refs_6_ = f32[8,1536]{1,0:T(8,128)S(1)} collective-permute-done((f32[8,1536]{1,0:T(8,128)S(1)}, f32[8,1536]{1,0:T(8,128)S(1)}, u32[]{:S(2)}, u32[]{:S(2)}) %collective-permute-start.7) | collective-permute-done | bytes 49184 | tf_op jit(solution)/shard_map/ppermute | solution.py:387
  48.6 1.5 %prior_partner.1 = (bf16[528,384]{1,0:T(8,128)(2,1)S(1)}, f32[8,1536]{1,0:T(8,128)S(1)}, f32[768,256]{1,0:T(8,128)S(1)}, bf16[768,256]{1,0:T(8,128)(2,1)S(1)}) custom-call(bf16[528,384]{1,0:T(8,128)(2,1)S(1)} %pack_queries.1.own.refs_0_, bf16[528,384]{1,0:T(8,128)(2,1)S(1)} %collective-permute-done.first.refs_1_, ...), custom_call_target="tpu_custom_call" | custom-call | tf_op jit(solution)/shard_map/prior_partner/pallas_call | solution.py:280
  50.1 2.2 %collective-permute-start.8 = (bf16[528,384]{1,0:T(8,128)(2,1)S(1)}, bf16[528,384]{1,0:T(8,128)(2,1)S(1)}, u32[]{:S(2)}, u32[]{:S(2)}) collective-permute-start(bf16[528,384]{1,0:T(8,128)(2,1)S(1)} %get-tuple-element.45), channel_id=1, source_target_pairs={{0,1},{1,0},{2,3},{3,2},{4,5},{5,4},{6,7},{7,6},{8,9},{9,8},{10,11... | collective-permute-start | bytes 1216520 | tf_op jit(solution)/shard_map/ppermute | solution.py:391
  52.3 2.8 %collective-permute-start.9 = (bf16[768,256]{1,0:T(8,128)(2,1)S(1)}, bf16[768,256]{1,0:T(8,128)(2,1)S(1)}, u32[]{:S(2)}, u32[]{:S(2)}) collective-permute-start(bf16[768,256]{1,0:T(8,128)(2,1)S(1)} %get-tuple-element.47), channel_id=1, source_target_pairs={{0,2},{1,3},{2,0},{3,1},{4,6},{5,7},{6,4},{7,5},{8,14},{9,15},{10,... | collective-permute-start | bytes 1179656 | tf_op jit(solution)/shard_map/ppermute | solution.py:387
  55.1 2.7 %key_grads.1 = (bf16[512,384]{1,0:T(8,128)(2,1)S(1)}, f32[512,384]{1,0:T(8,128)S(1)}, f32[512,384]{1,0:T(8,128)S(1)}) custom-call(bf16[528,384]{1,0:T(8,128)(2,1)S(1)} %pack_queries.1.own.refs_0_, bf16[528,384]{1,0:T(8,128)(2,1)S(1)} %collective-permute-done.first.refs_1_, bf16[528,384]{1,0:T(8,128)(2,1)S(1)} %collective-permute-done.1.second.refs_2_, ...), custom_call_target="tpu_custom_call" | custom-call | tf_op jit(solution)/shard_map/key_grads/pallas_call | solution.py:307
  57.9 3.7 %collective-permute-start.11 = (bf16[512,384]{1,0:T(8,128)(2,1)S(1)}, bf16[512,384]{1,0:T(8,128)(2,1)S(1)}, u32[]{:S(2)}, u32[]{:S(2)}) collective-permute-start(bf16[512,384]{1,0:T(8,128)(2,1)S(1)} %get-tuple-element.51), channel_id=1, source_target_pairs={{0,1},{1,0},{2,3},{3,2},{4,5},{5,4},{6,7},{7,6},{8,9},{9,8},{10,11... | collective-permute-start | bytes 1179656 | tf_op jit(solution)/shard_map/ppermute | solution.py:391
  61.5 0.4 collective-permute-done.9.far
  62.0 0.2 collective-permute-done.8.part
  62.2 0.1 middle_sums.1
  62.3 4.3 %collective-permute-start.12 = (bf16[512,384]{1,0:T(8,128)(2,1)S(1)}, bf16[512,384]{1,0:T(8,128)(2,1)S(1)}, u32[]{:S(2)}, u32[]{:S(2)}) collective-permute-start(bf16[512,384]{1,0:T(8,128)(2,1)S(1)} %get-tuple-element.52), channel_id=1, source_target_pairs={{8,0},{9,1},{10,2},{11,3},{12,4},{13,5},{14,6},{15,7},{16,8},{17,9... | collective-permute-start | bytes 1179656 | tf_op jit(solution)/shard_map/ppermute | solution.py:409
  66.7 3.0 %collective-permute-start.10 = (bf16[384,256]{1,0:T(8,128)(2,1)S(1)}, bf16[384,256]{1,0:T(8,128)(2,1)S(1)}, u32[]{:S(2)}, u32[]{:S(2)}) collective-permute-start(bf16[384,256]{1,0:T(8,128)(2,1)S(1)} %get-tuple-element.49), channel_id=1, source_target_pairs={{0,6},{1,7},{2,4},{3,5},{4,2},{5,3},{6,0},{7,1},{8,10},{9,11},{10,... | collective-permute-start | bytes 589832 | tf_op jit(solution)/shard_map/ppermute | solution.py:387
  69.7 0.0 collective-permute-done.11.other
  69.7 0.1 own_sum.1.own
  69.8 5.6 %collective-permute-done.10.pair = bf16[384,256]{1,0:T(8,128)(2,1)S(1)} collective-permute-done((bf16[384,256]{1,0:T(8,128)(2,1)S(1)}, bf16[384,256]{1,0:T(8,128)(2,1)S(1)}, u32[]{:S(2)}, u32[]{:S(2)}) %collective-permute-start.10) | collective-permute-done | bytes 196640 | tf_op jit(solution)/shard_map/ppermute | solution.py:387
  75.4 0.7 query_sum.1
  76.1 0.0 collective-permute-done.12.back
  76.1 0.9 %key_sum.1 = (bf16[384,256]{1,0:T(8,128)(2,1)}, bf16[384,256]{1,0:T(8,128)(2,1)}) custom-call(f32[512,384]{1,0:T(8,128)S(1)} %own_sum.1.own, bf16[512,384]{1,0:T(8,128)(2,1)S(1)} %collective-permute-done.12.back), custom_call_target="tpu_custom_call" | custom-call | tf_op jit(solution)/shard_map/key_sum/pallas_call | solution.py:373
  (2 shorter events, 0.1 us)
Async XLA Ops:
  2.0 13.6 %collective-permute-start.3 = (bf16[512,384]{1,0:T(8,128)(2,1)S(1)}, bf16[512,384]{1,0:T(8,128)(2,1)S(1)}, u32[]{:S(2)}, u32[]{:S(2)}) collective-permute-start(bf16[512,384]{1,0:T(8,128)(2,1)S(1)} %get-tuple-element.32.k0.refs_4_), channel_id=1, source_target_pairs={{0,1},{1,0},{2,3},{3,2},{4,5},{5,4},{6,7},{7,6},{8,9},{9,8},{10,11... | collective-permute-start | bytes 1179656 | tf_op jit(solution)/shard_map/ppermute | solution.py:391
  5.6 16.2 %collective-permute-start = (bf16[528,384]{1,0:T(8,128)(2,1)S(1)}, bf16[528,384]{1,0:T(8,128)(2,1)S(1)}, u32[]{:S(2)}, u32[]{:S(2)}) collective-permute-start(bf16[528,384]{1,0:T(8,128)(2,1)S(1)} %pack_queries.1.own.refs_0_), channel_id=1, source_target_pairs={{0,6},{1,7},{2,4},{3,5},{4,2},{5,3},{6,0},{7,1},{8,10},{9,11},{10,... | collective-permute-start | bytes 1216520 | tf_op jit(solution)/shard_map/ppermute | solution.py:387
  11.7 16.6 %collective-permute-start.1 = (bf16[528,384]{1,0:T(8,128)(2,1)S(1)}, bf16[528,384]{1,0:T(8,128)(2,1)S(1)}, u32[]{:S(2)}, u32[]{:S(2)}) collective-permute-start(bf16[528,384]{1,0:T(8,128)(2,1)S(1)} %pack_queries.1.own.refs_0_), channel_id=1, source_target_pairs={{0,2},{1,3},{2,0},{3,1},{4,6},{5,7},{6,4},{7,5},{8,14},{9,15},{10,... | collective-permute-start | bytes 1216520 | tf_op jit(solution)/shard_map/ppermute | solution.py:387
  13.6 14.7 %collective-permute-start.5 = (bf16[512,384]{1,0:T(8,128)(2,1)S(1)}, bf16[512,384]{1,0:T(8,128)(2,1)S(1)}, u32[]{:S(2)}, u32[]{:S(2)}) collective-permute-start(bf16[512,384]{1,0:T(8,128)(2,1)S(1)} %get-tuple-element.32.k0.refs_4_), channel_id=1, source_target_pairs={{0,8},{1,9},{2,10},{3,11},{4,12},{5,13},{6,14},{7,15},{8,16},{9,17... | collective-permute-start | bytes 1179656 | tf_op jit(solution)/shard_map/ppermute | solution.py:405
  15.5 16.9 %collective-permute-start.4 = (bf16[512,384]{1,0:T(8,128)(2,1)S(1)}, bf16[512,384]{1,0:T(8,128)(2,1)S(1)}, u32[]{:S(2)}, u32[]{:S(2)}) collective-permute-start(bf16[512,384]{1,0:T(8,128)(2,1)S(1)} %collective-permute-done.3.k1.refs_5_), channel_id=1, source_target_pairs={{0,8},{1,9},{2,10},{3,11},{4,12},{5,13},{6,14},{7,15},{8,16},{9,17... | collective-permute-start | bytes 1179656 | tf_op jit(solution)/shard_map/ppermute | solution.py:405
  21.8 10.7 %collective-permute-start.2 = (bf16[528,384]{1,0:T(8,128)(2,1)S(1)}, bf16[528,384]{1,0:T(8,128)(2,1)S(1)}, u32[]{:S(2)}, u32[]{:S(2)}) collective-permute-start(bf16[528,384]{1,0:T(8,128)(2,1)S(1)} %collective-permute-done.first.refs_1_), channel_id=1, source_target_pairs={{0,2},{1,3},{2,0},{3,1},{4,6},{5,7},{6,4},{7,5},{8,14},{9,15},{10,... | collective-permute-start | bytes 1216520 | tf_op jit(solution)/shard_map/ppermute | solution.py:387
  35.1 7.5 %collective-permute-start.6 = (f32[8,1536]{1,0:T(8,128)S(1)}, f32[8,1536]{1,0:T(8,128)S(1)}, u32[]{:S(2)}, u32[]{:S(2)}) collective-permute-start(f32[8,1536]{1,0:T(8,128)S(1)} %get-tuple-element.37.a), channel_id=1, source_target_pairs={{0,6},{1,7},{2,4},{3,5},{4,2},{5,3},{6,0},{7,1},{8,10},{9,11},{10,... | collective-permute-start | bytes 147464 | tf_op jit(solution)/shard_map/ppermute | solution.py:387
  42.7 6.0 %collective-permute-start.7 = (f32[8,1536]{1,0:T(8,128)S(1)}, f32[8,1536]{1,0:T(8,128)S(1)}, u32[]{:S(2)}, u32[]{:S(2)}) collective-permute-start(f32[8,1536]{1,0:T(8,128)S(1)} %merge.1.refs_5_), channel_id=1, source_target_pairs={{0,2},{1,3},{2,0},{3,1},{4,6},{5,7},{6,4},{7,5},{8,14},{9,15},{10,... | collective-permute-start | bytes 147464 | tf_op jit(solution)/shard_map/ppermute | solution.py:387
  50.1 12.1 %collective-permute-start.8 = (bf16[528,384]{1,0:T(8,128)(2,1)S(1)}, bf16[528,384]{1,0:T(8,128)(2,1)S(1)}, u32[]{:S(2)}, u32[]{:S(2)}) collective-permute-start(bf16[528,384]{1,0:T(8,128)(2,1)S(1)} %get-tuple-element.45), channel_id=1, source_target_pairs={{0,1},{1,0},{2,3},{3,2},{4,5},{5,4},{6,7},{7,6},{8,9},{9,8},{10,11... | collective-permute-start | bytes 1216520 | tf_op jit(solution)/shard_map/ppermute | solution.py:391
  52.3 9.7 %collective-permute-start.9 = (bf16[768,256]{1,0:T(8,128)(2,1)S(1)}, bf16[768,256]{1,0:T(8,128)(2,1)S(1)}, u32[]{:S(2)}, u32[]{:S(2)}) collective-permute-start(bf16[768,256]{1,0:T(8,128)(2,1)S(1)} %get-tuple-element.47), channel_id=1, source_target_pairs={{0,2},{1,3},{2,0},{3,1},{4,6},{5,7},{6,4},{7,5},{8,14},{9,15},{10,... | collective-permute-start | bytes 1179656 | tf_op jit(solution)/shard_map/ppermute | solution.py:387
  57.9 11.8 %collective-permute-start.11 = (bf16[512,384]{1,0:T(8,128)(2,1)S(1)}, bf16[512,384]{1,0:T(8,128)(2,1)S(1)}, u32[]{:S(2)}, u32[]{:S(2)}) collective-permute-start(bf16[512,384]{1,0:T(8,128)(2,1)S(1)} %get-tuple-element.51), channel_id=1, source_target_pairs={{0,1},{1,0},{2,3},{3,2},{4,5},{5,4},{6,7},{7,6},{8,9},{9,8},{10,11... | collective-permute-start | bytes 1179656 | tf_op jit(solution)/shard_map/ppermute | solution.py:391
  62.3 13.8 %collective-permute-start.12 = (bf16[512,384]{1,0:T(8,128)(2,1)S(1)}, bf16[512,384]{1,0:T(8,128)(2,1)S(1)}, u32[]{:S(2)}, u32[]{:S(2)}) collective-permute-start(bf16[512,384]{1,0:T(8,128)(2,1)S(1)} %get-tuple-element.52), channel_id=1, source_target_pairs={{8,0},{9,1},{10,2},{11,3},{12,4},{13,5},{14,6},{15,7},{16,8},{17,9... | collective-permute-start | bytes 1179656 | tf_op jit(solution)/shard_map/ppermute | solution.py:409
  66.7 8.8 %collective-permute-start.10 = (bf16[384,256]{1,0:T(8,128)(2,1)S(1)}, bf16[384,256]{1,0:T(8,128)(2,1)S(1)}, u32[]{:S(2)}, u32[]{:S(2)}) collective-permute-start(bf16[384,256]{1,0:T(8,128)(2,1)S(1)} %get-tuple-element.49), channel_id=1, source_target_pairs={{0,6},{1,7},{2,4},{3,5},{4,2},{5,3},{6,0},{7,1},{8,10},{9,11},{10,... | collective-permute-start | bytes 589832 | tf_op jit(solution)/shard_map/ppermute | solution.py:387

commit v5 on v4

--- a/solution.py
+++ b/solution.py
@@ -36,7 +36,7 @@
     return ref[...].astype(F32).T
 
 
-def pack_keys_body(k, v, q, o, g, kv, qs, os, gs, ks, vs, sems):
+def pack_keys_body(k, v, q, o, g, kv, padded, qs, os, gs, ks, vs, sems):
     copies = [
         pltpu.make_async_copy(src, dst, sems.at[n])
         for n, (src, dst) in enumerate(((k, ks), (v, vs), (q, qs), (o, os), (g, gs)))
@@ -47,6 +47,8 @@
     kv[0:256] = turned(ks).astype(BF)
     copies[1].wait()
     kv[256:512] = turned(vs).astype(BF)
+    padded[0:512] = kv[...]
+    padded[512:544] = jnp.zeros((32, R), BF)
     for copy in copies[2:]:
         copy.wait()
 
@@ -55,8 +57,8 @@
     return pl.pallas_call(
         pack_keys_body,
         in_specs=[HBM] * 5,
-        out_specs=[VM] * 4,
-        out_shape=[pltpu.VMEM((512, R), BF)] + [pltpu.VMEM((R, 2 * D), BF)] * 3,
+        out_specs=[VM] * 5,
+        out_shape=[pltpu.VMEM((512, R), BF), pltpu.VMEM((544, R), BF)] + [pltpu.VMEM((R, 2 * D), BF)] * 3,
         scratch_shapes=[pltpu.VMEM((R, 2 * D), BF)] * 2 + [pltpu.SemaphoreType.DMA((5,))],
         compiler_params=ALONE,
         name="pack_keys",
@@ -125,7 +127,7 @@
         out_shape=[pltpu.VMEM((2, NQ, NK), BF), pltpu.VMEM((8, NQ), F32), pltpu.VMEM((2, 2 * D, NK), BF)],
         scratch_shapes=[pltpu.VMEM((3, R, D), F32)],
         compiler_params=PARAMS,
-        cost_estimate=pl.CostEstimate(flops=3 * 10 ** 9, bytes_accessed=0, transcendentals=0),
+        cost_estimate=pl.CostEstimate(flops=15 * 10 ** 8, bytes_accessed=0, transcendentals=0),
         name="first_scores",
     )(*qg[0:3], *kv[0:3])
 
@@ -142,7 +144,7 @@
         out_shape=pltpu.VMEM((2, 2 * D, NK), BF),
         input_output_aliases={1: 0},
         compiler_params=PARAMS,
-        cost_estimate=pl.CostEstimate(flops=6 * 10 ** 9, bytes_accessed=0, transcendentals=0),
+        cost_estimate=pl.CostEstimate(flops=10 * 10 ** 8, bytes_accessed=0, transcendentals=0),
         name="last_keys",
     )(k3, ks)
 
@@ -332,19 +334,19 @@
     )(prior, part, near, far)
 
 
-def query_sum_body(own, pair, out):
+def query_sum_body(own, pair, after, out):
     out[...] = (own[...] + pair[...].astype(F32)).astype(BF)
 
 
-def query_sum(own, pair):
+def query_sum(own, pair, after):
     return pl.pallas_call(
         query_sum_body,
-        in_specs=[VM] * 2,
+        in_specs=[VM] * 3,
         out_shape=jax.ShapeDtypeStruct((R, 2 * D), BF),
         compiler_params=PARAMS,
         cost_estimate=pl.CostEstimate(flops=2 * 10 ** 9, bytes_accessed=0, transcendentals=0),
         name="query_sum",
-    )(own, pair)
+    )(own, pair, after)
 
 
 def own_sum_body(own, other, out):
@@ -363,7 +365,8 @@
     )(own, other)
 
 
-def key_sum_body(own, back, dk, dv):
+def key_sum_body(own, back, dk, dv, done):
+    done[...] = jnp.zeros((8, D), F32)
     total = own[...] + back[...].astype(F32)
     dk[...] = total[0:256].T.astype(BF)
     dv[...] = total[256:512].T.astype(BF)
@@ -373,7 +376,7 @@
     return pl.pallas_call(
         key_sum_body,
         in_specs=[VM] * 2,
-        out_shape=[jax.ShapeDtypeStruct((R, 2 * D), BF)] * 2,
+        out_shape=[jax.ShapeDtypeStruct((R, 2 * D), BF)] * 2 + [pltpu.VMEM((8, D), F32)],
         compiler_params=PARAMS,
         name="key_sum",
     )(own, back)
@@ -410,9 +413,9 @@
 
 
 def on_device(queries, key_rows, value_rows, outputs, out_grad):
-    kv_own, *rest = pack_keys(key_rows, value_rows, queries, outputs, out_grad)
+    kv_own, padded, *rest = pack_keys(key_rows, value_rows, queries, outputs, out_grad)
     qg_own = pack_queries(*rest)
-    kv_prior = to_next(kv_own)
+    kv_prior = to_next(padded)
     kv_partner = along_x(kv_own)
     kv = [kv_own, kv_partner, kv_prior, to_next(kv_partner)]
     qg_first = along_y(qg_own, 0)
@@ -433,8 +436,9 @@
     other = along_x(own_partner)
     prior, near, pair = middle_sums(prior, part, near, far)
     back = to_prior(prior)
-    query_grad = query_sum(near, along_y(pair, 0))
-    key_grad, value_grad = key_sum(own_sum(own, other), back)
+    pair = along_y(pair, 0)
+    key_grad, value_grad, done = key_sum(own_sum(own, other), back)
+    query_grad = query_sum(near, pair, done)
     return query_grad, key_grad, value_grad
 
 

time: 77.5 us -> 76.7 us (0.990)
  waiting for transfers between devices: 18.1 us -> 15.9 us
    ppermute x7, waiting for transfers between devices: 12.2 us -> 8.4 us  [along_y(): return lax.ppermute(value, ('outer', 'inner'), pairs)]
    ppermute x1, waiting for transfers between devices: 0.01 us -> 1.46 us  [to_prior(): lax.ppermute(value, ('outer', 'inner'), [(b, a) for a, b in window_pairs()])]
    ppermute x2, starting transfers between devices: 3.84 us -> 4.68 us  [to_next(): return lax.ppermute(value, ('outer', 'inner'), window_pairs())]
  transfers between devices with their start and end apart: 13 -> 13, of which waited for: 8 -> 9; matrix products, arithmetic and copies ran while one was open for 0% -> 0% of each run, Pallas kernels for 16% -> 17%
where the time goes in v5:
time: 76.7 us; the launch traced here: 75.6 us
  starting transfers between devices  39.9 us (52%)
  Pallas kernels  18.9 us (25%)
  waiting for transfers between devices  15.9 us (21%)
  between operations  0.82 us (1%)
    ppermute x7, starting transfers between devices, along_y(): return lax.ppermute(value, ('outer', 'inner'), pairs)  21.8 us
    ppermute x3, starting transfers between devices, along_x(): return lax.ppermute(value, 'inner', [(i, i ^ 1) for i in range(8)])  9.25 us
    ppermute x7, waiting for transfers between devices, along_y(): return lax.ppermute(value, ('outer', 'inner'), pairs)  8.4 us
    ppermute x2, waiting for transfers between devices, to_next(): return lax.ppermute(value, ('outer', 'inner'), window_pairs())  5.91 us
    pallas_call x2, Pallas kernels, score_grads(): pl.pallas_call(lambda *refs: score_grads_body(h, *refs), in_specs=[VM] *...  5.52 us
    ppermute x2, starting transfers between devices, to_next(): return lax.ppermute(value, ('outer', 'inner'), window_pairs())  4.68 us
    ppermute x1, starting transfers between devices, to_prior(): lax.ppermute(value, ('outer', 'inner'), [(b, a) for a, b in window_pairs()])  4.24 us
    pallas_call x1, Pallas kernels, first_scores(): pl.pallas_call(first_scores_body, in_specs=[VM] * 6, out_specs=[VM] * 3,...  3.02 us
  transfers between devices with their start and end apart: 13, of which 9 were waited for; matrix products, arithmetic and copies ran while one was open for 0% of the time, Pallas kernels for 17%

profile of v5, /device:TPU:24, one launch (start us, length us, event | category | flops | bytes accessed | tf_op | source)
XLA Modules:
  0.0 75.6 jit_solution(4929511403961017881)
XLA Ops:
  0.6 1.3 %pack_keys.1 = (bf16[512,384]{1,0:T(8,128)(2,1)S(1)}, bf16[544,384]{1,0:T(8,128)(2,1)S(1)}, bf16[384,256]{1,0:T(8,128)(2,1)S(1)}, bf16[384,256]{1,0:T(8,128)(2,1)S(1)}, bf16[384,256]{1,0:T(8,128)(2,1)S(1)}) custom-call(bf16[384,256]{1,0:T(8,128)(2,1)} %k.1, bf16[384,256]{1,0:T(8,128)(2,1)} %v.1, bf16[384,256]{1,0:T(8,128)(2,1)} %q.1, bf16[384,256]{1,0:T(8,128)(2,1)} %o.1, ...), custom_call_target="tpu_custom_call" | custom-call | tf_op jit(solution)/shard_map/pack_keys/pallas_call | solution.py:57
  2.0 3.4 %collective-permute-start.3 = (bf16[512,384]{1,0:T(8,128)(2,1)S(1)}, bf16[512,384]{1,0:T(8,128)(2,1)S(1)}, u32[]{:S(2)}, u32[]{:S(2)}) collective-permute-start(bf16[512,384]{1,0:T(8,128)(2,1)S(1)} %get-tuple-element.34.k0.refs_4_), channel_id=1, source_target_pairs={{0,1},{1,0},{2,3},{3,2},{4,5},{5,4},{6,7},{7,6},{8,9},{9,8},{10,11... | collective-permute-start | bytes 1179656 | tf_op jit(solution)/shard_map/ppermute | solution.py:394
  5.4 0.3 pack_queries.1.own.refs_0_
  5.6 6.0 %collective-permute-start = (bf16[528,384]{1,0:T(8,128)(2,1)S(1)}, bf16[528,384]{1,0:T(8,128)(2,1)S(1)}, u32[]{:S(2)}, u32[]{:S(2)}) collective-permute-start(bf16[528,384]{1,0:T(8,128)(2,1)S(1)} %pack_queries.1.own.refs_0_), channel_id=1, source_target_pairs={{0,6},{1,7},{2,4},{3,5},{4,2},{5,3},{6,0},{7,1},{8,10},{9,11},{10,... | collective-permute-start | bytes 1216520 | tf_op jit(solution)/shard_map/ppermute | solution.py:390
  11.7 1.9 %collective-permute-start.5 = (bf16[544,384]{1,0:T(8,128)(2,1)S(1)}, bf16[544,384]{1,0:T(8,128)(2,1)S(1)}, u32[]{:S(2)}, u32[]{:S(2)}) collective-permute-start(bf16[544,384]{1,0:T(8,128)(2,1)S(1)} %get-tuple-element.35), channel_id=1, source_target_pairs={{0,8},{1,9},{2,10},{3,11},{4,12},{5,13},{6,14},{7,15},{8,16},{9,17... | collective-permute-start | bytes 1253384 | tf_op jit(solution)/shard_map/ppermute | solution.py:408
  13.6 1.9 %collective-permute-start.1 = (bf16[528,384]{1,0:T(8,128)(2,1)S(1)}, bf16[528,384]{1,0:T(8,128)(2,1)S(1)}, u32[]{:S(2)}, u32[]{:S(2)}) collective-permute-start(bf16[528,384]{1,0:T(8,128)(2,1)S(1)} %pack_queries.1.own.refs_0_), channel_id=1, source_target_pairs={{0,2},{1,3},{2,0},{3,1},{4,6},{5,7},{6,4},{7,5},{8,14},{9,15},{10,... | collective-permute-start | bytes 1216520 | tf_op jit(solution)/shard_map/ppermute | solution.py:390
  15.5 0.0 collective-permute-done.3.k1.refs_5_
  15.5 2.8 %collective-permute-start.4 = (bf16[512,384]{1,0:T(8,128)(2,1)S(1)}, bf16[512,384]{1,0:T(8,128)(2,1)S(1)}, u32[]{:S(2)}, u32[]{:S(2)}) collective-permute-start(bf16[512,384]{1,0:T(8,128)(2,1)S(1)} %collective-permute-done.3.k1.refs_5_), channel_id=1, source_target_pairs={{0,8},{1,9},{2,10},{3,11},{4,12},{5,13},{6,14},{7,15},{8,16},{9,17... | collective-permute-start | bytes 1179656 | tf_op jit(solution)/shard_map/ppermute | solution.py:408
  18.3 0.0 collective-permute-done.first.refs_1_
  18.3 3.1 %collective-permute-start.2 = (bf16[528,384]{1,0:T(8,128)(2,1)S(1)}, bf16[528,384]{1,0:T(8,128)(2,1)S(1)}, u32[]{:S(2)}, u32[]{:S(2)}) collective-permute-start(bf16[528,384]{1,0:T(8,128)(2,1)S(1)} %collective-permute-done.first.refs_1_), channel_id=1, source_target_pairs={{0,2},{1,3},{2,0},{3,1},{4,6},{5,7},{6,4},{7,5},{8,14},{9,15},{10,... | collective-permute-start | bytes 1216520 | tf_op jit(solution)/shard_map/ppermute | solution.py:390
  21.4 2.0 %collective-permute-done.1.second.refs_2_ = bf16[528,384]{1,0:T(8,128)(2,1)S(1)} collective-permute-done((bf16[528,384]{1,0:T(8,128)(2,1)S(1)}, bf16[528,384]{1,0:T(8,128)(2,1)S(1)}, u32[]{:S(2)}, u32[]{:S(2)}) %collective-permute-start.1) | collective-permute-done | bytes 405536 | tf_op jit(solution)/shard_map/ppermute | solution.py:390
  23.4 2.4 %collective-permute-done.5.k2.refs_6_ = bf16[544,384]{1,0:T(8,128)(2,1)S(1)} collective-permute-done((bf16[544,384]{1,0:T(8,128)(2,1)S(1)}, bf16[544,384]{1,0:T(8,128)(2,1)S(1)}, u32[]{:S(2)}, u32[]{:S(2)}) %collective-permute-start.5) | collective-permute-done | bytes 417824 | tf_op jit(solution)/shard_map/ppermute | solution.py:408
  25.8 3.0 %first_scores.1 = (bf16[2,1536,1536]{2,1,0:T(8,128)(2,1)S(1)}, f32[8,1536]{1,0:T(8,128)S(1)}, bf16[2,256,1536]{2,1,0:T(8,128)(2,1)S(1)}) custom-call(bf16[528,384]{1,0:T(8,128)(2,1)S(1)} %pack_queries.1.own.refs_0_, bf16[528,384]{1,0:T(8,128)(2,1)S(1)} %collective-permute-done.first.refs_1_, bf16[528,384]{1,0:T(8,128)(2,1)S(1)} %collective-permute-done.1.second.refs_2_, ...), custom_call_target="tpu_custom_call" | custom-call | flops 1500000000 | tf_op jit(solution)/shard_map/first_scores/pallas_call | solution.py:123
  28.8 3.5 %collective-permute-done.4.k3.refs_7_ = bf16[512,384]{1,0:T(8,128)(2,1)S(1)} collective-permute-done((bf16[512,384]{1,0:T(8,128)(2,1)S(1)}, bf16[512,384]{1,0:T(8,128)(2,1)S(1)}, u32[]{:S(2)}, u32[]{:S(2)}) %collective-permute-start.4) | collective-permute-done | bytes 393248 | tf_op jit(solution)/shard_map/ppermute | solution.py:408
  32.4 0.0 collective-permute-done.2.third.refs_3_
  32.4 2.6 %last_scores.1 = (bf16[2,1536,1536]{2,1,0:T(8,128)(2,1)S(1)}, f32[8,1536]{1,0:T(8,128)S(1)}, f32[8,1536]{1,0:T(8,128)S(1)}) custom-call(bf16[528,384]{1,0:T(8,128)(2,1)S(1)} %pack_queries.1.own.refs_0_, bf16[528,384]{1,0:T(8,128)(2,1)S(1)} %collective-permute-done.first.refs_1_, ...), custom_call_target="tpu_custom_call", output_to_operand_aliasing={{0}: (5, {})} | custom-call | flops 2000000000 | tf_op jit(solution)/shard_map/last_scores/pallas_call | solution.py:173
  35.0 2.1 %collective-permute-start.6 = (f32[8,1536]{1,0:T(8,128)S(1)}, f32[8,1536]{1,0:T(8,128)S(1)}, u32[]{:S(2)}, u32[]{:S(2)}) collective-permute-start(f32[8,1536]{1,0:T(8,128)S(1)} %get-tuple-element.40.a), channel_id=1, source_target_pairs={{0,6},{1,7},{2,4},{3,5},{4,2},{5,3},{6,0},{7,1},{8,10},{9,11},{10,... | collective-permute-start | bytes 147464 | tf_op jit(solution)/shard_map/ppermute | solution.py:390
  37.1 2.8 %score_grads.2 = (bf16[1536,1536]{1,0:T(8,128)(2,1)S(1)}, f32[2,1536,128]{2,1,0:T(8,128)S(1)}) custom-call(bf16[528,384]{1,0:T(8,128)(2,1)S(1)} %pack_queries.1.own.refs_0_, bf16[528,384]{1,0:T(8,128)(2,1)S(1)} %collective-permute-done.first.refs_1_, bf16[528,384]{1,0:T(8,128)(2,1)S(1)} %collective-permute-done.1.second.refs_2_, ...), custom_call_target="tpu_custom_call" | custom-call | tf_op jit(solution)/shard_map/score_grads/pallas_call | solution.py:232
  39.9 2.5 %collective-permute-done.6.b = f32[8,1536]{1,0:T(8,128)S(1)} collective-permute-done((f32[8,1536]{1,0:T(8,128)S(1)}, f32[8,1536]{1,0:T(8,128)S(1)}, u32[]{:S(2)}, u32[]{:S(2)}) %collective-permute-start.6) | collective-permute-done | bytes 49184 | tf_op jit(solution)/shard_map/ppermute | solution.py:390
  42.4 2.1 %collective-permute-start.7 = (f32[8,1536]{1,0:T(8,128)S(1)}, f32[8,1536]{1,0:T(8,128)S(1)}, u32[]{:S(2)}, u32[]{:S(2)}) collective-permute-start(f32[8,1536]{1,0:T(8,128)S(1)} %merge.1.refs_5_), channel_id=1, source_target_pairs={{0,2},{1,3},{2,0},{3,1},{4,6},{5,7},{6,4},{7,5},{8,14},{9,15},{10,... | collective-permute-start | bytes 147464 | tf_op jit(solution)/shard_map/ppermute | solution.py:390
  44.5 2.8 %score_grads.3 = (bf16[1536,1536]{1,0:T(8,128)(2,1)S(1)}, f32[2,1536,128]{2,1,0:T(8,128)S(1)}) custom-call(bf16[528,384]{1,0:T(8,128)(2,1)S(1)} %pack_queries.1.own.refs_0_, bf16[528,384]{1,0:T(8,128)(2,1)S(1)} %collective-permute-done.first.refs_1_, bf16[528,384]{1,0:T(8,128)(2,1)S(1)} %collective-permute-done.1.second.refs_2_, ...), custom_call_target="tpu_custom_call" | custom-call | tf_op jit(solution)/shard_map/score_grads/pallas_call | solution.py:232
  47.3 1.1 %collective-permute-done.7.refs_6_ = f32[8,1536]{1,0:T(8,128)S(1)} collective-permute-done((f32[8,1536]{1,0:T(8,128)S(1)}, f32[8,1536]{1,0:T(8,128)S(1)}, u32[]{:S(2)}, u32[]{:S(2)}) %collective-permute-start.7) | collective-permute-done | bytes 49184 | tf_op jit(solution)/shard_map/ppermute | solution.py:390
  48.4 1.6 %prior_partner.1 = (bf16[528,384]{1,0:T(8,128)(2,1)S(1)}, f32[8,1536]{1,0:T(8,128)S(1)}, f32[768,256]{1,0:T(8,128)S(1)}, bf16[768,256]{1,0:T(8,128)(2,1)S(1)}) custom-call(bf16[528,384]{1,0:T(8,128)(2,1)S(1)} %pack_queries.1.own.refs_0_, bf16[528,384]{1,0:T(8,128)(2,1)S(1)} %collective-permute-done.first.refs_1_, ...), custom_call_target="tpu_custom_call" | custom-call | tf_op jit(solution)/shard_map/prior_partner/pallas_call | solution.py:282
  49.9 2.0 %collective-permute-start.8 = (bf16[528,384]{1,0:T(8,128)(2,1)S(1)}, bf16[528,384]{1,0:T(8,128)(2,1)S(1)}, u32[]{:S(2)}, u32[]{:S(2)}) collective-permute-start(bf16[528,384]{1,0:T(8,128)(2,1)S(1)} %get-tuple-element.48), channel_id=1, source_target_pairs={{0,1},{1,0},{2,3},{3,2},{4,5},{5,4},{6,7},{7,6},{8,9},{9,8},{10,11... | collective-permute-start | bytes 1216520 | tf_op jit(solution)/shard_map/ppermute | solution.py:394
  51.9 2.8 %collective-permute-start.9 = (bf16[768,256]{1,0:T(8,128)(2,1)S(1)}, bf16[768,256]{1,0:T(8,128)(2,1)S(1)}, u32[]{:S(2)}, u32[]{:S(2)}) collective-permute-start(bf16[768,256]{1,0:T(8,128)(2,1)S(1)} %get-tuple-element.50), channel_id=1, source_target_pairs={{0,2},{1,3},{2,0},{3,1},{4,6},{5,7},{6,4},{7,5},{8,14},{9,15},{10,... | collective-permute-start | bytes 1179656 | tf_op jit(solution)/shard_map/ppermute | solution.py:390
  54.7 2.7 %key_grads.1 = (bf16[512,384]{1,0:T(8,128)(2,1)S(1)}, f32[512,384]{1,0:T(8,128)S(1)}, f32[512,384]{1,0:T(8,128)S(1)}) custom-call(bf16[528,384]{1,0:T(8,128)(2,1)S(1)} %pack_queries.1.own.refs_0_, bf16[528,384]{1,0:T(8,128)(2,1)S(1)} %collective-permute-done.first.refs_1_, bf16[528,384]{1,0:T(8,128)(2,1)S(1)} %collective-permute-done.1.second.refs_2_, ...), custom_call_target="tpu_custom_call" | custom-call | tf_op jit(solution)/shard_map/key_grads/pallas_call | solution.py:309
  57.5 3.9 %collective-permute-start.11 = (bf16[512,384]{1,0:T(8,128)(2,1)S(1)}, bf16[512,384]{1,0:T(8,128)(2,1)S(1)}, u32[]{:S(2)}, u32[]{:S(2)}) collective-permute-start(bf16[512,384]{1,0:T(8,128)(2,1)S(1)} %get-tuple-element.54), channel_id=1, source_target_pairs={{0,1},{1,0},{2,3},{3,2},{4,5},{5,4},{6,7},{7,6},{8,9},{9,8},{10,11... | collective-permute-start | bytes 1179656 | tf_op jit(solution)/shard_map/ppermute | solution.py:394
  61.4 0.2 collective-permute-done.9.far
  61.6 0.1 collective-permute-done.8.part
  61.7 0.1 middle_sums.1
  61.8 4.2 %collective-permute-start.12 = (bf16[512,384]{1,0:T(8,128)(2,1)S(1)}, bf16[512,384]{1,0:T(8,128)(2,1)S(1)}, u32[]{:S(2)}, u32[]{:S(2)}) collective-permute-start(bf16[512,384]{1,0:T(8,128)(2,1)S(1)} %get-tuple-element.55), channel_id=1, source_target_pairs={{8,0},{9,1},{10,2},{11,3},{12,4},{13,5},{14,6},{15,7},{16,8},{17,9... | collective-permute-start | bytes 1179656 | tf_op jit(solution)/shard_map/ppermute | solution.py:412
  66.1 3.7 %collective-permute-start.10 = (bf16[384,256]{1,0:T(8,128)(2,1)S(1)}, bf16[384,256]{1,0:T(8,128)(2,1)S(1)}, u32[]{:S(2)}, u32[]{:S(2)}) collective-permute-start(bf16[384,256]{1,0:T(8,128)(2,1)S(1)} %get-tuple-element.52), channel_id=1, source_target_pairs={{0,6},{1,7},{2,4},{3,5},{4,2},{5,3},{6,0},{7,1},{8,10},{9,11},{10,... | collective-permute-start | bytes 589832 | tf_op jit(solution)/shard_map/ppermute | solution.py:390
  69.8 0.0 collective-permute-done.11.other
  69.8 0.1 own_sum.1.own
  69.9 1.5 %collective-permute-done.12.back = bf16[512,384]{1,0:T(8,128)(2,1)S(1)} collective-permute-done((bf16[512,384]{1,0:T(8,128)(2,1)S(1)}, bf16[512,384]{1,0:T(8,128)(2,1)S(1)}, u32[]{:S(2)}, u32[]{:S(2)}) %collective-permute-start.12) | collective-permute-done | bytes 393248 | tf_op jit(solution)/shard_map/ppermute | solution.py:412
  71.4 0.9 %key_sum.1 = (bf16[384,256]{1,0:T(8,128)(2,1)}, bf16[384,256]{1,0:T(8,128)(2,1)}, f32[8,128]{1,0:T(8,128)S(1)}) custom-call(f32[512,384]{1,0:T(8,128)S(1)} %own_sum.1.own, bf16[512,384]{1,0:T(8,128)(2,1)S(1)} %collective-permute-done.12.back), custom_call_target="tpu_custom_call" | custom-call | tf_op jit(solution)/shard_map/key_sum/pallas_call | solution.py:376
  72.2 2.6 %collective-permute-done.10.pair = bf16[384,256]{1,0:T(8,128)(2,1)S(1)} collective-permute-done((bf16[384,256]{1,0:T(8,128)(2,1)S(1)}, bf16[384,256]{1,0:T(8,128)(2,1)S(1)}, u32[]{:S(2)}, u32[]{:S(2)}) %collective-permute-start.10) | collective-permute-done | bytes 196640 | tf_op jit(solution)/shard_map/ppermute | solution.py:390
  74.9 0.7 query_sum.1
  (2 shorter events, 0.1 us)
Async XLA Ops:
  2.0 13.6 %collective-permute-start.3 = (bf16[512,384]{1,0:T(8,128)(2,1)S(1)}, bf16[512,384]{1,0:T(8,128)(2,1)S(1)}, u32[]{:S(2)}, u32[]{:S(2)}) collective-permute-start(bf16[512,384]{1,0:T(8,128)(2,1)S(1)} %get-tuple-element.34.k0.refs_4_), channel_id=1, source_target_pairs={{0,1},{1,0},{2,3},{3,2},{4,5},{5,4},{6,7},{7,6},{8,9},{9,8},{10,11... | collective-permute-start | bytes 1179656 | tf_op jit(solution)/shard_map/ppermute | solution.py:394
  5.6 12.7 %collective-permute-start = (bf16[528,384]{1,0:T(8,128)(2,1)S(1)}, bf16[528,384]{1,0:T(8,128)(2,1)S(1)}, u32[]{:S(2)}, u32[]{:S(2)}) collective-permute-start(bf16[528,384]{1,0:T(8,128)(2,1)S(1)} %pack_queries.1.own.refs_0_), channel_id=1, source_target_pairs={{0,6},{1,7},{2,4},{3,5},{4,2},{5,3},{6,0},{7,1},{8,10},{9,11},{10,... | collective-permute-start | bytes 1216520 | tf_op jit(solution)/shard_map/ppermute | solution.py:390
  11.7 14.2 %collective-permute-start.5 = (bf16[544,384]{1,0:T(8,128)(2,1)S(1)}, bf16[544,384]{1,0:T(8,128)(2,1)S(1)}, u32[]{:S(2)}, u32[]{:S(2)}) collective-permute-start(bf16[544,384]{1,0:T(8,128)(2,1)S(1)} %get-tuple-element.35), channel_id=1, source_target_pairs={{0,8},{1,9},{2,10},{3,11},{4,12},{5,13},{6,14},{7,15},{8,16},{9,17... | collective-permute-start | bytes 1253384 | tf_op jit(solution)/shard_map/ppermute | solution.py:408
  13.6 9.8 %collective-permute-start.1 = (bf16[528,384]{1,0:T(8,128)(2,1)S(1)}, bf16[528,384]{1,0:T(8,128)(2,1)S(1)}, u32[]{:S(2)}, u32[]{:S(2)}) collective-permute-start(bf16[528,384]{1,0:T(8,128)(2,1)S(1)} %pack_queries.1.own.refs_0_), channel_id=1, source_target_pairs={{0,2},{1,3},{2,0},{3,1},{4,6},{5,7},{6,4},{7,5},{8,14},{9,15},{10,... | collective-permute-start | bytes 1216520 | tf_op jit(solution)/shard_map/ppermute | solution.py:390
  15.5 16.8 %collective-permute-start.4 = (bf16[512,384]{1,0:T(8,128)(2,1)S(1)}, bf16[512,384]{1,0:T(8,128)(2,1)S(1)}, u32[]{:S(2)}, u32[]{:S(2)}) collective-permute-start(bf16[512,384]{1,0:T(8,128)(2,1)S(1)} %collective-permute-done.3.k1.refs_5_), channel_id=1, source_target_pairs={{0,8},{1,9},{2,10},{3,11},{4,12},{5,13},{6,14},{7,15},{8,16},{9,17... | collective-permute-start | bytes 1179656 | tf_op jit(solution)/shard_map/ppermute | solution.py:408
  18.3 14.1 %collective-permute-start.2 = (bf16[528,384]{1,0:T(8,128)(2,1)S(1)}, bf16[528,384]{1,0:T(8,128)(2,1)S(1)}, u32[]{:S(2)}, u32[]{:S(2)}) collective-permute-start(bf16[528,384]{1,0:T(8,128)(2,1)S(1)} %collective-permute-done.first.refs_1_), channel_id=1, source_target_pairs={{0,2},{1,3},{2,0},{3,1},{4,6},{5,7},{6,4},{7,5},{8,14},{9,15},{10,... | collective-permute-start | bytes 1216520 | tf_op jit(solution)/shard_map/ppermute | solution.py:390
  35.0 7.4 %collective-permute-start.6 = (f32[8,1536]{1,0:T(8,128)S(1)}, f32[8,1536]{1,0:T(8,128)S(1)}, u32[]{:S(2)}, u32[]{:S(2)}) collective-permute-start(f32[8,1536]{1,0:T(8,128)S(1)} %get-tuple-element.40.a), channel_id=1, source_target_pairs={{0,6},{1,7},{2,4},{3,5},{4,2},{5,3},{6,0},{7,1},{8,10},{9,11},{10,... | collective-permute-start | bytes 147464 | tf_op jit(solution)/shard_map/ppermute | solution.py:390
  42.4 6.0 %collective-permute-start.7 = (f32[8,1536]{1,0:T(8,128)S(1)}, f32[8,1536]{1,0:T(8,128)S(1)}, u32[]{:S(2)}, u32[]{:S(2)}) collective-permute-start(f32[8,1536]{1,0:T(8,128)S(1)} %merge.1.refs_5_), channel_id=1, source_target_pairs={{0,2},{1,3},{2,0},{3,1},{4,6},{5,7},{6,4},{7,5},{8,14},{9,15},{10,... | collective-permute-start | bytes 147464 | tf_op jit(solution)/shard_map/ppermute | solution.py:390
  49.9 11.8 %collective-permute-start.8 = (bf16[528,384]{1,0:T(8,128)(2,1)S(1)}, bf16[528,384]{1,0:T(8,128)(2,1)S(1)}, u32[]{:S(2)}, u32[]{:S(2)}) collective-permute-start(bf16[528,384]{1,0:T(8,128)(2,1)S(1)} %get-tuple-element.48), channel_id=1, source_target_pairs={{0,1},{1,0},{2,3},{3,2},{4,5},{5,4},{6,7},{7,6},{8,9},{9,8},{10,11... | collective-permute-start | bytes 1216520 | tf_op jit(solution)/shard_map/ppermute | solution.py:394
  51.9 9.7 %collective-permute-start.9 = (bf16[768,256]{1,0:T(8,128)(2,1)S(1)}, bf16[768,256]{1,0:T(8,128)(2,1)S(1)}, u32[]{:S(2)}, u32[]{:S(2)}) collective-permute-start(bf16[768,256]{1,0:T(8,128)(2,1)S(1)} %get-tuple-element.50), channel_id=1, source_target_pairs={{0,2},{1,3},{2,0},{3,1},{4,6},{5,7},{6,4},{7,5},{8,14},{9,15},{10,... | collective-permute-start | bytes 1179656 | tf_op jit(solution)/shard_map/ppermute | solution.py:390
  57.5 12.3 %collective-permute-start.11 = (bf16[512,384]{1,0:T(8,128)(2,1)S(1)}, bf16[512,384]{1,0:T(8,128)(2,1)S(1)}, u32[]{:S(2)}, u32[]{:S(2)}) collective-permute-start(bf16[512,384]{1,0:T(8,128)(2,1)S(1)} %get-tuple-element.54), channel_id=1, source_target_pairs={{0,1},{1,0},{2,3},{3,2},{4,5},{5,4},{6,7},{7,6},{8,9},{9,8},{10,11... | collective-permute-start | bytes 1179656 | tf_op jit(solution)/shard_map/ppermute | solution.py:394
  61.8 9.5 %collective-permute-start.12 = (bf16[512,384]{1,0:T(8,128)(2,1)S(1)}, bf16[512,384]{1,0:T(8,128)(2,1)S(1)}, u32[]{:S(2)}, u32[]{:S(2)}) collective-permute-start(bf16[512,384]{1,0:T(8,128)(2,1)S(1)} %get-tuple-element.55), channel_id=1, source_target_pairs={{8,0},{9,1},{10,2},{11,3},{12,4},{13,5},{14,6},{15,7},{16,8},{17,9... | collective-permute-start | bytes 1179656 | tf_op jit(solution)/shard_map/ppermute | solution.py:412
  66.1 8.8 %collective-permute-start.10 = (bf16[384,256]{1,0:T(8,128)(2,1)S(1)}, bf16[384,256]{1,0:T(8,128)(2,1)S(1)}, u32[]{:S(2)}, u32[]{:S(2)}) collective-permute-start(bf16[384,256]{1,0:T(8,128)(2,1)S(1)} %get-tuple-element.52), channel_id=1, source_target_pairs={{0,6},{1,7},{2,4},{3,5},{4,2},{5,3},{6,0},{7,1},{8,10},{9,11},{10,... | collective-permute-start | bytes 589832 | tf_op jit(solution)/shard_map/ppermute | solution.py:390

commit v6 on v5

--- a/solution.py
+++ b/solution.py
@@ -149,38 +149,54 @@
     )(k3, ks)
 
 
-def last_scores_body(own, first, second, third, ks, p_in, st_in, p_ref, st_ref, both_ref, st):
+def rest_scores_body(own, first, second, ks, p_in, st_in, p_ref, st_ref, st):
     st_ref[0:4, 0:3 * R] = st_in[0:4, 0:3 * R]
-    for n, q in enumerate((own, first, second, third)):
+    st_ref[:, chunk(3)] = jnp.zeros((8, R), F32)
+    for n, q in enumerate((own, first, second)):
         for h in range(2):
-            if n == 3:
-                m = score_tile(n, h, q, ks, 0, slice(0, NK), p_ref, st)
-                st[n, :, 4 + h:5 + h] = m
-                st[n, :, 6 + h:7 + h] = jnp.zeros((R, 1), F32)
-            else:
-                score_tile(n, h, q, ks, 1, GROUPS[1], p_ref, st)
-        rows = st[n].T
-        if n == 3:
-            st_ref[0:4, chunk(n)] = rows[0:4, :]
-        st_ref[4:8, chunk(n)] = rows[4:8, :]
+            score_tile(n, h, q, ks, 1, GROUPS[1], p_ref, st)
+        st_ref[4:8, chunk(n)] = st[n].T[4:8, :]
+
+
+def rest_scores(qg, ks, p, st):
+    return pl.pallas_call(
+        rest_scores_body,
+        in_specs=[VM] * 6,
+        out_specs=[VM] * 2,
+        out_shape=[pltpu.VMEM((2, NQ, NK), BF), pltpu.VMEM((8, NQ), F32)],
+        scratch_shapes=[pltpu.VMEM((3, R, D), F32)],
+        input_output_aliases={4: 0},
+        compiler_params=PARAMS,
+        cost_estimate=pl.CostEstimate(flops=10 ** 9, bytes_accessed=0, transcendentals=0),
+        name="rest_scores",
+    )(*qg[0:3], ks, p, st)
+
+
+def last_scores_body(third, ks, p_in, st_in, p_ref, st_ref, both_ref, st):
+    st_ref[:, 0:3 * R] = st_in[:, 0:3 * R]
+    for h in range(2):
+        m = score_tile(3, h, third, ks, 0, slice(0, NK), p_ref, st)
+        st[3, :, 4 + h:5 + h] = m
+        st[3, :, 6 + h:7 + h] = jnp.zeros((R, 1), F32)
+    st_ref[:, chunk(3)] = st[3].T[0:8, :]
     top, total = combined(st_ref[0:2], st_ref[2:4], st_ref[4:6], st_ref[6:8])
     both_ref[0:2] = top
     both_ref[2:4] = total
     both_ref[4:8] = jnp.zeros((4, NQ), F32)
 
 
-def last_scores(qg, ks, p, st):
+def last_scores(third, ks, p, st):
     return pl.pallas_call(
         last_scores_body,
-        in_specs=[VM] * 7,
+        in_specs=[VM] * 4,
         out_specs=[VM] * 3,
         out_shape=[pltpu.VMEM((2, NQ, NK), BF), pltpu.VMEM((8, NQ), F32), pltpu.VMEM((8, NQ), F32)],
         scratch_shapes=[pltpu.VMEM((4, R, D), F32)],
-        input_output_aliases={5: 0},
-        compiler_params=PARAMS,
-        cost_estimate=pl.CostEstimate(flops=2 * 10 ** 9, bytes_accessed=0, transcendentals=0),
+        input_output_aliases={2: 0},
+        compiler_params=PARAMS,
+        cost_estimate=pl.CostEstimate(flops=10 ** 9, bytes_accessed=0, transcendentals=0),
         name="last_scores",
-    )(*qg, ks, p, st)
+    )(third, ks, p, st)
 
 
 def combined(m0, l0, m1, l1):
@@ -422,7 +438,8 @@
     qg = [qg_own, qg_first, along_y(qg_own, 1), along_y(qg_first, 1)]
     p, st, ks = first_scores(qg, kv)
     ks = last_keys(kv[3], ks)
-    p, st, both = last_scores(qg, ks, p, st)
+    p, st = rest_scores(qg, ks, p, st)
+    p, st, both = last_scores(qg[3], ks, p, st)
     both_pair = along_y(both, 0)
     ds0, dq0 = score_grads(0, qg, kv, ks, p)
     pair = merge(both, both_pair, dq0)

time: 76.7 us -> 76 us (level)
  starting transfers between devices: 39.9 us -> 36.6 us
  waiting for transfers between devices: 15.9 us -> 18.6 us
    ppermute x1, starting transfers between devices: 4.24 us -> 1.92 us  [to_prior(): lax.ppermute(value, ('outer', 'inner'), [(b, a) for a, b in window_pairs()])]
    ppermute x3, waiting for transfers between devices: 0.15 us -> 1.39 us  [along_x(): return lax.ppermute(value, 'inner', [(i, i ^ 1) for i in range(8)])]
    ppermute x1, waiting for transfers between devices: 1.46 us -> 2.53 us  [to_prior(): lax.ppermute(value, ('outer', 'inner'), [(b, a) for a, b in window_pairs()])]
    ppermute x7, starting transfers between devices: 21.8 us -> 20.7 us  [along_y(): return lax.ppermute(value, ('outer', 'inner'), pairs)]
    pallas_call x1 -> x2, Pallas kernels: 2.61 us -> 3.29 us  [the longest x1 1.79 us: rest_scores(): pl.pallas_call(rest_scores_body, in_specs=[VM] * 6, out_specs=[VM] * 2, o...]
  transfers between devices with their start and end apart: 13 -> 13, of which waited for: 9 -> 9; matrix products, arithmetic and copies ran while one was open for 0% -> 0% of each run, Pallas kernels for 17% -> 19%
where the time goes in v6:
time: 76 us; the launch traced here: 75.5 us
  starting transfers between devices  36.6 us (48%)
  Pallas kernels  19.5 us (26%)
  waiting for transfers between devices  18.6 us (24%)
  between operations  0.81 us (1%)
    ppermute x7, starting transfers between devices, along_y(): return lax.ppermute(value, ('outer', 'inner'), pairs)  20.7 us
    ppermute x3, starting transfers between devices, along_x(): return lax.ppermute(value, 'inner', [(i, i ^ 1) for i in range(8)])  9.25 us
    ppermute x7, waiting for transfers between devices, along_y(): return lax.ppermute(value, ('outer', 'inner'), pairs)  8.75 us
    ppermute x2, waiting for transfers between devices, to_next(): return lax.ppermute(value, ('outer', 'inner'), window_pairs())  5.91 us
    pallas_call x2, Pallas kernels, score_grads(): pl.pallas_call(lambda *refs: score_grads_body(h, *refs), in_specs=[VM] *...  5.51 us
    ppermute x2, starting transfers between devices, to_next(): return lax.ppermute(value, ('outer', 'inner'), window_pairs())  4.68 us
    pallas_call x1, Pallas kernels, first_scores(): pl.pallas_call(first_scores_body, in_specs=[VM] * 6, out_specs=[VM] * 3,...  3.02 us
    pallas_call x1, Pallas kernels, key_grads(): pl.pallas_call(key_grads_body, in_specs=[VM] * 8, out_specs=[VM] * 3, out...  2.73 us
  transfers between devices with their start and end apart: 13, of which 9 were waited for; matrix products, arithmetic and copies ran while one was open for 0% of the time, Pallas kernels for 19%

profile of v6, /device:TPU:24, one launch (start us, length us, event | category | flops | bytes accessed | tf_op | source)
XLA Modules:
  0.0 75.5 jit_solution(15894260365724305562)
XLA Ops:
  0.6 1.3 %pack_keys.1 = (bf16[512,384]{1,0:T(8,128)(2,1)S(1)}, bf16[544,384]{1,0:T(8,128)(2,1)S(1)}, bf16[384,256]{1,0:T(8,128)(2,1)S(1)}, bf16[384,256]{1,0:T(8,128)(2,1)S(1)}, bf16[384,256]{1,0:T(8,128)(2,1)S(1)}) custom-call(bf16[384,256]{1,0:T(8,128)(2,1)} %k.1, bf16[384,256]{1,0:T(8,128)(2,1)} %v.1, bf16[384,256]{1,0:T(8,128)(2,1)} %q.1, bf16[384,256]{1,0:T(8,128)(2,1)} %o.1, ...), custom_call_target="tpu_custom_call" | custom-call | tf_op jit(solution)/shard_map/pack_keys/pallas_call | solution.py:57
  2.0 3.4 %collective-permute-start.3 = (bf16[512,384]{1,0:T(8,128)(2,1)S(1)}, bf16[512,384]{1,0:T(8,128)(2,1)S(1)}, u32[]{:S(2)}, u32[]{:S(2)}) collective-permute-start(bf16[512,384]{1,0:T(8,128)(2,1)S(1)} %get-tuple-element.36.k0.refs_4_), channel_id=1, source_target_pairs={{0,1},{1,0},{2,3},{3,2},{4,5},{5,4},{6,7},{7,6},{8,9},{9,8},{10,11... | collective-permute-start | bytes 1179656 | tf_op jit(solution)/shard_map/ppermute | solution.py:410
  5.4 0.3 pack_queries.1.own.refs_0_
  5.6 6.0 %collective-permute-start = (bf16[528,384]{1,0:T(8,128)(2,1)S(1)}, bf16[528,384]{1,0:T(8,128)(2,1)S(1)}, u32[]{:S(2)}, u32[]{:S(2)}) collective-permute-start(bf16[528,384]{1,0:T(8,128)(2,1)S(1)} %pack_queries.1.own.refs_0_), channel_id=1, source_target_pairs={{0,6},{1,7},{2,4},{3,5},{4,2},{5,3},{6,0},{7,1},{8,10},{9,11},{10,... | collective-permute-start | bytes 1216520 | tf_op jit(solution)/shard_map/ppermute | solution.py:406
  11.7 1.9 %collective-permute-start.5 = (bf16[544,384]{1,0:T(8,128)(2,1)S(1)}, bf16[544,384]{1,0:T(8,128)(2,1)S(1)}, u32[]{:S(2)}, u32[]{:S(2)}) collective-permute-start(bf16[544,384]{1,0:T(8,128)(2,1)S(1)} %get-tuple-element.37), channel_id=1, source_target_pairs={{0,8},{1,9},{2,10},{3,11},{4,12},{5,13},{6,14},{7,15},{8,16},{9,17... | collective-permute-start | bytes 1253384 | tf_op jit(solution)/shard_map/ppermute | solution.py:424
  13.6 1.9 %collective-permute-start.1 = (bf16[528,384]{1,0:T(8,128)(2,1)S(1)}, bf16[528,384]{1,0:T(8,128)(2,1)S(1)}, u32[]{:S(2)}, u32[]{:S(2)}) collective-permute-start(bf16[528,384]{1,0:T(8,128)(2,1)S(1)} %pack_queries.1.own.refs_0_), channel_id=1, source_target_pairs={{0,2},{1,3},{2,0},{3,1},{4,6},{5,7},{6,4},{7,5},{8,14},{9,15},{10,... | collective-permute-start | bytes 1216520 | tf_op jit(solution)/shard_map/ppermute | solution.py:406
  15.5 0.0 collective-permute-done.3.k1.refs_5_
  15.5 2.8 %collective-permute-start.4 = (bf16[512,384]{1,0:T(8,128)(2,1)S(1)}, bf16[512,384]{1,0:T(8,128)(2,1)S(1)}, u32[]{:S(2)}, u32[]{:S(2)}) collective-permute-start(bf16[512,384]{1,0:T(8,128)(2,1)S(1)} %collective-permute-done.3.k1.refs_5_), channel_id=1, source_target_pairs={{0,8},{1,9},{2,10},{3,11},{4,12},{5,13},{6,14},{7,15},{8,16},{9,17... | collective-permute-start | bytes 1179656 | tf_op jit(solution)/shard_map/ppermute | solution.py:424
  18.3 0.0 collective-permute-done.first.refs_1_
  18.3 3.1 %collective-permute-start.2 = (bf16[528,384]{1,0:T(8,128)(2,1)S(1)}, bf16[528,384]{1,0:T(8,128)(2,1)S(1)}, u32[]{:S(2)}, u32[]{:S(2)}) collective-permute-start(bf16[528,384]{1,0:T(8,128)(2,1)S(1)} %collective-permute-done.first.refs_1_), channel_id=1, source_target_pairs={{0,2},{1,3},{2,0},{3,1},{4,6},{5,7},{6,4},{7,5},{8,14},{9,15},{10,... | collective-permute-start | bytes 1216520 | tf_op jit(solution)/shard_map/ppermute | solution.py:406
  21.4 2.0 %collective-permute-done.1.second.refs_2_ = bf16[528,384]{1,0:T(8,128)(2,1)S(1)} collective-permute-done((bf16[528,384]{1,0:T(8,128)(2,1)S(1)}, bf16[528,384]{1,0:T(8,128)(2,1)S(1)}, u32[]{:S(2)}, u32[]{:S(2)}) %collective-permute-start.1) | collective-permute-done | bytes 405536 | tf_op jit(solution)/shard_map/ppermute | solution.py:406
  23.4 2.4 %collective-permute-done.5.k2.refs_6_ = bf16[544,384]{1,0:T(8,128)(2,1)S(1)} collective-permute-done((bf16[544,384]{1,0:T(8,128)(2,1)S(1)}, bf16[544,384]{1,0:T(8,128)(2,1)S(1)}, u32[]{:S(2)}, u32[]{:S(2)}) %collective-permute-start.5) | collective-permute-done | bytes 417824 | tf_op jit(solution)/shard_map/ppermute | solution.py:424
  25.8 3.0 %first_scores.1 = (bf16[2,1536,1536]{2,1,0:T(8,128)(2,1)S(1)}, f32[8,1536]{1,0:T(8,128)S(1)}, bf16[2,256,1536]{2,1,0:T(8,128)(2,1)S(1)}) custom-call(bf16[528,384]{1,0:T(8,128)(2,1)S(1)} %pack_queries.1.own.refs_0_, bf16[528,384]{1,0:T(8,128)(2,1)S(1)} %collective-permute-done.first.refs_1_, bf16[528,384]{1,0:T(8,128)(2,1)S(1)} %collective-permute-done.1.second.refs_2_, ...), custom_call_target="tpu_custom_call" | custom-call | flops 1500000000 | tf_op jit(solution)/shard_map/first_scores/pallas_call | solution.py:123
  28.8 3.5 %collective-permute-done.4.k3.refs_7_ = bf16[512,384]{1,0:T(8,128)(2,1)S(1)} collective-permute-done((bf16[512,384]{1,0:T(8,128)(2,1)S(1)}, bf16[512,384]{1,0:T(8,128)(2,1)S(1)}, u32[]{:S(2)}, u32[]{:S(2)}) %collective-permute-start.4) | collective-permute-done | bytes 393248 | tf_op jit(solution)/shard_map/ppermute | solution.py:424
  32.4 1.8 %rest_scores.1 = (bf16[2,1536,1536]{2,1,0:T(8,128)(2,1)S(1)}, f32[8,1536]{1,0:T(8,128)S(1)}) custom-call(bf16[528,384]{1,0:T(8,128)(2,1)S(1)} %pack_queries.1.own.refs_0_, bf16[528,384]{1,0:T(8,128)(2,1)S(1)} %collective-permute-done.first.refs_1_, bf16[528,384]{1,0:T(8,128)(2,1)S(1)} %collective-permute-done.1.second.refs_2_, ...), custom_call_target="tpu_custom_call", output_to_operand_aliasing={{0}: (4, {})} | custom-call | flops 1000000000 | tf_op jit(solution)/shard_map/rest_scores/pallas_call | solution.py:162
  34.1 0.0 collective-permute-done.2.third.refs_3_
  34.2 1.5 %last_scores.1 = (bf16[2,1536,1536]{2,1,0:T(8,128)(2,1)S(1)}, f32[8,1536]{1,0:T(8,128)S(1)}, f32[8,1536]{1,0:T(8,128)S(1)}) custom-call(bf16[528,384]{1,0:T(8,128)(2,1)S(1)} %collective-permute-done.2.third.refs_3_, bf16[2,256,1536]{2,1,0:T(8,128)(2,1)S(1)} %last_keys.1.ks.refs_8_, ...), custom_call_target="tpu_custom_call", output_to_operand_aliasing={{0}: (2, {})} | custom-call | flops 1000000000 | tf_op jit(solution)/shard_map/last_scores/pallas_call | solution.py:189
  35.6 2.1 %collective-permute-start.6 = (f32[8,1536]{1,0:T(8,128)S(1)}, f32[8,1536]{1,0:T(8,128)S(1)}, u32[]{:S(2)}, u32[]{:S(2)}) collective-permute-start(f32[8,1536]{1,0:T(8,128)S(1)} %get-tuple-element.44.a), channel_id=1, source_target_pairs={{0,6},{1,7},{2,4},{3,5},{4,2},{5,3},{6,0},{7,1},{8,10},{9,11},{10,... | collective-permute-start | bytes 147464 | tf_op jit(solution)/shard_map/ppermute | solution.py:406
  37.8 2.8 %score_grads.2 = (bf16[1536,1536]{1,0:T(8,128)(2,1)S(1)}, f32[2,1536,128]{2,1,0:T(8,128)S(1)}) custom-call(bf16[528,384]{1,0:T(8,128)(2,1)S(1)} %pack_queries.1.own.refs_0_, bf16[528,384]{1,0:T(8,128)(2,1)S(1)} %collective-permute-done.first.refs_1_, bf16[528,384]{1,0:T(8,128)(2,1)S(1)} %collective-permute-done.1.second.refs_2_, ...), custom_call_target="tpu_custom_call" | custom-call | tf_op jit(solution)/shard_map/score_grads/pallas_call | solution.py:248
  40.5 2.3 %collective-permute-done.6.b = f32[8,1536]{1,0:T(8,128)S(1)} collective-permute-done((f32[8,1536]{1,0:T(8,128)S(1)}, f32[8,1536]{1,0:T(8,128)S(1)}, u32[]{:S(2)}, u32[]{:S(2)}) %collective-permute-start.6) | collective-permute-done | bytes 49184 | tf_op jit(solution)/shard_map/ppermute | solution.py:406
  42.9 2.1 %collective-permute-start.7 = (f32[8,1536]{1,0:T(8,128)S(1)}, f32[8,1536]{1,0:T(8,128)S(1)}, u32[]{:S(2)}, u32[]{:S(2)}) collective-permute-start(f32[8,1536]{1,0:T(8,128)S(1)} %merge.1.refs_5_), channel_id=1, source_target_pairs={{0,2},{1,3},{2,0},{3,1},{4,6},{5,7},{6,4},{7,5},{8,14},{9,15},{10,... | collective-permute-start | bytes 147464 | tf_op jit(solution)/shard_map/ppermute | solution.py:406
  45.0 2.8 %score_grads.3 = (bf16[1536,1536]{1,0:T(8,128)(2,1)S(1)}, f32[2,1536,128]{2,1,0:T(8,128)S(1)}) custom-call(bf16[528,384]{1,0:T(8,128)(2,1)S(1)} %pack_queries.1.own.refs_0_, bf16[528,384]{1,0:T(8,128)(2,1)S(1)} %collective-permute-done.first.refs_1_, bf16[528,384]{1,0:T(8,128)(2,1)S(1)} %collective-permute-done.1.second.refs_2_, ...), custom_call_target="tpu_custom_call" | custom-call | tf_op jit(solution)/shard_map/score_grads/pallas_call | solution.py:248
  47.7 1.1 %collective-permute-done.7.refs_6_ = f32[8,1536]{1,0:T(8,128)S(1)} collective-permute-done((f32[8,1536]{1,0:T(8,128)S(1)}, f32[8,1536]{1,0:T(8,128)S(1)}, u32[]{:S(2)}, u32[]{:S(2)}) %collective-permute-start.7) | collective-permute-done | bytes 49184 | tf_op jit(solution)/shard_map/ppermute | solution.py:406
  48.9 1.5 %prior_partner.1 = (bf16[528,384]{1,0:T(8,128)(2,1)S(1)}, f32[8,1536]{1,0:T(8,128)S(1)}, f32[768,256]{1,0:T(8,128)S(1)}, bf16[768,256]{1,0:T(8,128)(2,1)S(1)}) custom-call(bf16[528,384]{1,0:T(8,128)(2,1)S(1)} %pack_queries.1.own.refs_0_, bf16[528,384]{1,0:T(8,128)(2,1)S(1)} %collective-permute-done.first.refs_1_, ...), custom_call_target="tpu_custom_call" | custom-call | tf_op jit(solution)/shard_map/prior_partner/pallas_call | solution.py:298
  50.4 2.5 %collective-permute-start.8 = (bf16[528,384]{1,0:T(8,128)(2,1)S(1)}, bf16[528,384]{1,0:T(8,128)(2,1)S(1)}, u32[]{:S(2)}, u32[]{:S(2)}) collective-permute-start(bf16[528,384]{1,0:T(8,128)(2,1)S(1)} %get-tuple-element.52), channel_id=1, source_target_pairs={{0,1},{1,0},{2,3},{3,2},{4,5},{5,4},{6,7},{7,6},{8,9},{9,8},{10,11... | collective-permute-start | bytes 1216520 | tf_op jit(solution)/shard_map/ppermute | solution.py:410
  52.9 2.8 %collective-permute-start.9 = (bf16[768,256]{1,0:T(8,128)(2,1)S(1)}, bf16[768,256]{1,0:T(8,128)(2,1)S(1)}, u32[]{:S(2)}, u32[]{:S(2)}) collective-permute-start(bf16[768,256]{1,0:T(8,128)(2,1)S(1)} %get-tuple-element.54), channel_id=1, source_target_pairs={{0,2},{1,3},{2,0},{3,1},{4,6},{5,7},{6,4},{7,5},{8,14},{9,15},{10,... | collective-permute-start | bytes 1179656 | tf_op jit(solution)/shard_map/ppermute | solution.py:406
  55.7 2.7 %key_grads.1 = (bf16[512,384]{1,0:T(8,128)(2,1)S(1)}, f32[512,384]{1,0:T(8,128)S(1)}, f32[512,384]{1,0:T(8,128)S(1)}) custom-call(bf16[528,384]{1,0:T(8,128)(2,1)S(1)} %pack_queries.1.own.refs_0_, bf16[528,384]{1,0:T(8,128)(2,1)S(1)} %collective-permute-done.first.refs_1_, bf16[528,384]{1,0:T(8,128)(2,1)S(1)} %collective-permute-done.1.second.refs_2_, ...), custom_call_target="tpu_custom_call" | custom-call | tf_op jit(solution)/shard_map/key_grads/pallas_call | solution.py:325
  58.4 3.4 %collective-permute-start.11 = (bf16[512,384]{1,0:T(8,128)(2,1)S(1)}, bf16[512,384]{1,0:T(8,128)(2,1)S(1)}, u32[]{:S(2)}, u32[]{:S(2)}) collective-permute-start(bf16[512,384]{1,0:T(8,128)(2,1)S(1)} %get-tuple-element.58), channel_id=1, source_target_pairs={{0,1},{1,0},{2,3},{3,2},{4,5},{5,4},{6,7},{7,6},{8,9},{9,8},{10,11... | collective-permute-start | bytes 1179656 | tf_op jit(solution)/shard_map/ppermute | solution.py:410
  61.8 0.7 collective-permute-done.9.far
  62.5 1.4 %collective-permute-done.8.part = bf16[528,384]{1,0:T(8,128)(2,1)S(1)} collective-permute-done((bf16[528,384]{1,0:T(8,128)(2,1)S(1)}, bf16[528,384]{1,0:T(8,128)(2,1)S(1)}, u32[]{:S(2)}, u32[]{:S(2)}) %collective-permute-start.8) | collective-permute-done | bytes 405536 | tf_op jit(solution)/shard_map/ppermute | solution.py:410
  63.9 0.1 middle_sums.1
  64.1 1.9 %collective-permute-start.12 = (bf16[512,384]{1,0:T(8,128)(2,1)S(1)}, bf16[512,384]{1,0:T(8,128)(2,1)S(1)}, u32[]{:S(2)}, u32[]{:S(2)}) collective-permute-start(bf16[512,384]{1,0:T(8,128)(2,1)S(1)} %get-tuple-element.59), channel_id=1, source_target_pairs={{8,0},{9,1},{10,2},{11,3},{12,4},{13,5},{14,6},{15,7},{16,8},{17,9... | collective-permute-start | bytes 1179656 | tf_op jit(solution)/shard_map/ppermute | solution.py:428
  66.0 2.6 %collective-permute-start.10 = (bf16[384,256]{1,0:T(8,128)(2,1)S(1)}, bf16[384,256]{1,0:T(8,128)(2,1)S(1)}, u32[]{:S(2)}, u32[]{:S(2)}) collective-permute-start(bf16[384,256]{1,0:T(8,128)(2,1)S(1)} %get-tuple-element.56), channel_id=1, source_target_pairs={{0,6},{1,7},{2,4},{3,5},{4,2},{5,3},{6,0},{7,1},{8,10},{9,11},{10,... | collective-permute-start | bytes 589832 | tf_op jit(solution)/shard_map/ppermute | solution.py:406
  68.6 0.0 collective-permute-done.11.other
  68.7 0.1 own_sum.1.own
  68.7 2.5 %collective-permute-done.12.back = bf16[512,384]{1,0:T(8,128)(2,1)S(1)} collective-permute-done((bf16[512,384]{1,0:T(8,128)(2,1)S(1)}, bf16[512,384]{1,0:T(8,128)(2,1)S(1)}, u32[]{:S(2)}, u32[]{:S(2)}) %collective-permute-start.12) | collective-permute-done | bytes 393248 | tf_op jit(solution)/shard_map/ppermute | solution.py:428
  71.3 0.9 %key_sum.1 = (bf16[384,256]{1,0:T(8,128)(2,1)}, bf16[384,256]{1,0:T(8,128)(2,1)}, f32[8,128]{1,0:T(8,128)S(1)}) custom-call(f32[512,384]{1,0:T(8,128)S(1)} %own_sum.1.own, bf16[512,384]{1,0:T(8,128)(2,1)S(1)} %collective-permute-done.12.back), custom_call_target="tpu_custom_call" | custom-call | tf_op jit(solution)/shard_map/key_sum/pallas_call | solution.py:392
  72.2 2.6 %collective-permute-done.10.pair = bf16[384,256]{1,0:T(8,128)(2,1)S(1)} collective-permute-done((bf16[384,256]{1,0:T(8,128)(2,1)S(1)}, bf16[384,256]{1,0:T(8,128)(2,1)S(1)}, u32[]{:S(2)}, u32[]{:S(2)}) %collective-permute-start.10) | collective-permute-done | bytes 196640 | tf_op jit(solution)/shard_map/ppermute | solution.py:406
  74.8 0.7 query_sum.1
  (2 shorter events, 0.1 us)
Async XLA Ops:
  2.0 13.6 %collective-permute-start.3 = (bf16[512,384]{1,0:T(8,128)(2,1)S(1)}, bf16[512,384]{1,0:T(8,128)(2,1)S(1)}, u32[]{:S(2)}, u32[]{:S(2)}) collective-permute-start(bf16[512,384]{1,0:T(8,128)(2,1)S(1)} %get-tuple-element.36.k0.refs_4_), channel_id=1, source_target_pairs={{0,1},{1,0},{2,3},{3,2},{4,5},{5,4},{6,7},{7,6},{8,9},{9,8},{10,11... | collective-permute-start | bytes 1179656 | tf_op jit(solution)/shard_map/ppermute | solution.py:410
  5.6 12.7 %collective-permute-start = (bf16[528,384]{1,0:T(8,128)(2,1)S(1)}, bf16[528,384]{1,0:T(8,128)(2,1)S(1)}, u32[]{:S(2)}, u32[]{:S(2)}) collective-permute-start(bf16[528,384]{1,0:T(8,128)(2,1)S(1)} %pack_queries.1.own.refs_0_), channel_id=1, source_target_pairs={{0,6},{1,7},{2,4},{3,5},{4,2},{5,3},{6,0},{7,1},{8,10},{9,11},{10,... | collective-permute-start | bytes 1216520 | tf_op jit(solution)/shard_map/ppermute | solution.py:406
  11.7 14.2 %collective-permute-start.5 = (bf16[544,384]{1,0:T(8,128)(2,1)S(1)}, bf16[544,384]{1,0:T(8,128)(2,1)S(1)}, u32[]{:S(2)}, u32[]{:S(2)}) collective-permute-start(bf16[544,384]{1,0:T(8,128)(2,1)S(1)} %get-tuple-element.37), channel_id=1, source_target_pairs={{0,8},{1,9},{2,10},{3,11},{4,12},{5,13},{6,14},{7,15},{8,16},{9,17... | collective-permute-start | bytes 1253384 | tf_op jit(solution)/shard_map/ppermute | solution.py:424
  13.6 9.8 %collective-permute-start.1 = (bf16[528,384]{1,0:T(8,128)(2,1)S(1)}, bf16[528,384]{1,0:T(8,128)(2,1)S(1)}, u32[]{:S(2)}, u32[]{:S(2)}) collective-permute-start(bf16[528,384]{1,0:T(8,128)(2,1)S(1)} %pack_queries.1.own.refs_0_), channel_id=1, source_target_pairs={{0,2},{1,3},{2,0},{3,1},{4,6},{5,7},{6,4},{7,5},{8,14},{9,15},{10,... | collective-permute-start | bytes 1216520 | tf_op jit(solution)/shard_map/ppermute | solution.py:406
  15.5 16.8 %collective-permute-start.4 = (bf16[512,384]{1,0:T(8,128)(2,1)S(1)}, bf16[512,384]{1,0:T(8,128)(2,1)S(1)}, u32[]{:S(2)}, u32[]{:S(2)}) collective-permute-start(bf16[512,384]{1,0:T(8,128)(2,1)S(1)} %collective-permute-done.3.k1.refs_5_), channel_id=1, source_target_pairs={{0,8},{1,9},{2,10},{3,11},{4,12},{5,13},{6,14},{7,15},{8,16},{9,17... | collective-permute-start | bytes 1179656 | tf_op jit(solution)/shard_map/ppermute | solution.py:424
  18.3 15.9 %collective-permute-start.2 = (bf16[528,384]{1,0:T(8,128)(2,1)S(1)}, bf16[528,384]{1,0:T(8,128)(2,1)S(1)}, u32[]{:S(2)}, u32[]{:S(2)}) collective-permute-start(bf16[528,384]{1,0:T(8,128)(2,1)S(1)} %collective-permute-done.first.refs_1_), channel_id=1, source_target_pairs={{0,2},{1,3},{2,0},{3,1},{4,6},{5,7},{6,4},{7,5},{8,14},{9,15},{10,... | collective-permute-start | bytes 1216520 | tf_op jit(solution)/shard_map/ppermute | solution.py:406
  35.6 7.2 %collective-permute-start.6 = (f32[8,1536]{1,0:T(8,128)S(1)}, f32[8,1536]{1,0:T(8,128)S(1)}, u32[]{:S(2)}, u32[]{:S(2)}) collective-permute-start(f32[8,1536]{1,0:T(8,128)S(1)} %get-tuple-element.44.a), channel_id=1, source_target_pairs={{0,6},{1,7},{2,4},{3,5},{4,2},{5,3},{6,0},{7,1},{8,10},{9,11},{10,... | collective-permute-start | bytes 147464 | tf_op jit(solution)/shard_map/ppermute | solution.py:406
  42.9 6.0 %collective-permute-start.7 = (f32[8,1536]{1,0:T(8,128)S(1)}, f32[8,1536]{1,0:T(8,128)S(1)}, u32[]{:S(2)}, u32[]{:S(2)}) collective-permute-start(f32[8,1536]{1,0:T(8,128)S(1)} %merge.1.refs_5_), channel_id=1, source_target_pairs={{0,2},{1,3},{2,0},{3,1},{4,6},{5,7},{6,4},{7,5},{8,14},{9,15},{10,... | collective-permute-start | bytes 147464 | tf_op jit(solution)/shard_map/ppermute | solution.py:406
  50.4 13.5 %collective-permute-start.8 = (bf16[528,384]{1,0:T(8,128)(2,1)S(1)}, bf16[528,384]{1,0:T(8,128)(2,1)S(1)}, u32[]{:S(2)}, u32[]{:S(2)}) collective-permute-start(bf16[528,384]{1,0:T(8,128)(2,1)S(1)} %get-tuple-element.52), channel_id=1, source_target_pairs={{0,1},{1,0},{2,3},{3,2},{4,5},{5,4},{6,7},{7,6},{8,9},{9,8},{10,11... | collective-permute-start | bytes 1216520 | tf_op jit(solution)/shard_map/ppermute | solution.py:410
  52.9 9.7 %collective-permute-start.9 = (bf16[768,256]{1,0:T(8,128)(2,1)S(1)}, bf16[768,256]{1,0:T(8,128)(2,1)S(1)}, u32[]{:S(2)}, u32[]{:S(2)}) collective-permute-start(bf16[768,256]{1,0:T(8,128)(2,1)S(1)} %get-tuple-element.54), channel_id=1, source_target_pairs={{0,2},{1,3},{2,0},{3,1},{4,6},{5,7},{6,4},{7,5},{8,14},{9,15},{10,... | collective-permute-start | bytes 1179656 | tf_op jit(solution)/shard_map/ppermute | solution.py:406
  58.4 10.2 %collective-permute-start.11 = (bf16[512,384]{1,0:T(8,128)(2,1)S(1)}, bf16[512,384]{1,0:T(8,128)(2,1)S(1)}, u32[]{:S(2)}, u32[]{:S(2)}) collective-permute-start(bf16[512,384]{1,0:T(8,128)(2,1)S(1)} %get-tuple-element.58), channel_id=1, source_target_pairs={{0,1},{1,0},{2,3},{3,2},{4,5},{5,4},{6,7},{7,6},{8,9},{9,8},{10,11... | collective-permute-start | bytes 1179656 | tf_op jit(solution)/shard_map/ppermute | solution.py:410
  64.1 7.2 %collective-permute-start.12 = (bf16[512,384]{1,0:T(8,128)(2,1)S(1)}, bf16[512,384]{1,0:T(8,128)(2,1)S(1)}, u32[]{:S(2)}, u32[]{:S(2)}) collective-permute-start(bf16[512,384]{1,0:T(8,128)(2,1)S(1)} %get-tuple-element.59), channel_id=1, source_target_pairs={{8,0},{9,1},{10,2},{11,3},{12,4},{13,5},{14,6},{15,7},{16,8},{17,9... | collective-permute-start | bytes 1179656 | tf_op jit(solution)/shard_map/ppermute | solution.py:428
  66.0 8.8 %collective-permute-start.10 = (bf16[384,256]{1,0:T(8,128)(2,1)S(1)}, bf16[384,256]{1,0:T(8,128)(2,1)S(1)}, u32[]{:S(2)}, u32[]{:S(2)}) collective-permute-start(bf16[384,256]{1,0:T(8,128)(2,1)S(1)} %get-tuple-element.56), channel_id=1, source_target_pairs={{0,6},{1,7},{2,4},{3,5},{4,2},{5,3},{6,0},{7,1},{8,10},{9,11},{10,... | collective-permute-start | bytes 589832 | tf_op jit(solution)/shard_map/ppermute | solution.py:406

commit v7 on v6

--- a/solution.py
+++ b/solution.py
@@ -150,12 +150,20 @@
 
 
 def rest_scores_body(own, first, second, ks, p_in, st_in, p_ref, st_ref, st):
-    st_ref[0:4, 0:3 * R] = st_in[0:4, 0:3 * R]
+    rows = slice(0, 3 * R)
+    st_ref[0:4, rows] = st_in[0:4, rows]
     st_ref[:, chunk(3)] = jnp.zeros((8, R), F32)
-    for n, q in enumerate((own, first, second)):
-        for h in range(2):
-            score_tile(n, h, q, ks, 1, GROUPS[1], p_ref, st)
-        st_ref[4:8, chunk(n)] = st[n].T[4:8, :]
+    for h in range(2):
+        scaled = jnp.concatenate([q[head(h), :] for q in (own, first, second)], axis=1).astype(F32) * C
+        high = scaled.astype(BF)
+        low = (scaled - high.astype(F32)).astype(BF)
+        s = dot(jnp.concatenate([high, low], axis=0), ks[h, :, GROUPS[1]], 0, 0)
+        m = jnp.max(s, axis=1, keepdims=True)
+        p = jnp.exp2(s - m)
+        st[:, 4 + h:5 + h] = m
+        st[:, 6 + h:7 + h] = jnp.sum(p, axis=1, keepdims=True)
+        p_ref[h, rows, GROUPS[1]] = p.astype(BF)
+    st_ref[4:8, rows] = st[...].T[4:8, :]
 
 
 def rest_scores(qg, ks, p, st):
@@ -164,7 +172,7 @@
         in_specs=[VM] * 6,
         out_specs=[VM] * 2,
         out_shape=[pltpu.VMEM((2, NQ, NK), BF), pltpu.VMEM((8, NQ), F32)],
-        scratch_shapes=[pltpu.VMEM((3, R, D), F32)],
+        scratch_shapes=[pltpu.VMEM((3 * R, D), F32)],
         input_output_aliases={4: 0},
         compiler_params=PARAMS,
         cost_estimate=pl.CostEstimate(flops=10 ** 9, bytes_accessed=0, transcendentals=0),

time: 76 us -> 75.6 us (level)
  waiting for transfers between devices: 18.6 us -> 17.3 us
  starting transfers between devices: 36.6 us -> 37.4 us
    ppermute x7, starting transfers between devices: 20.7 us -> 21.6 us  [along_y(): return lax.ppermute(value, ('outer', 'inner'), pairs)]
    ppermute x1, waiting for transfers between devices: 2.53 us -> 1.69 us  [to_prior(): lax.ppermute(value, ('outer', 'inner'), [(b, a) for a, b in window_pairs()])]
where the time goes in v7:
time: 75.6 us; the launch traced here: 74.7 us
  starting transfers between devices  37.4 us (49%)
  Pallas kernels  19.1 us (25%)
  waiting for transfers between devices  17.3 us (23%)
  between operations  0.81 us (1%)
    ppermute x7, starting transfers between devices, along_y(): return lax.ppermute(value, ('outer', 'inner'), pairs)  21.6 us
    ppermute x3, starting transfers between devices, along_x(): return lax.ppermute(value, 'inner', [(i, i ^ 1) for i in range(8)])  9.24 us
    ppermute x7, waiting for transfers between devices, along_y(): return lax.ppermute(value, ('outer', 'inner'), pairs)  8.73 us
    ppermute x2, waiting for transfers between devices, to_next(): return lax.ppermute(value, ('outer', 'inner'), window_pairs())  5.91 us
    pallas_call x2, Pallas kernels, score_grads(): pl.pallas_call(lambda *refs: score_grads_body(h, *refs), in_specs=[VM] *...  5.51 us
    ppermute x2, starting transfers between devices, to_next(): return lax.ppermute(value, ('outer', 'inner'), window_pairs())  4.68 us
    pallas_call x1, Pallas kernels, first_scores(): pl.pallas_call(first_scores_body, in_specs=[VM] * 6, out_specs=[VM] * 3,...  3.02 us
    pallas_call x1, Pallas kernels, key_grads(): pl.pallas_call(key_grads_body, in_specs=[VM] * 8, out_specs=[VM] * 3, out...  2.73 us
  transfers between devices with their start and end apart: 13, of which 9 were waited for; matrix products, arithmetic and copies ran while one was open for 0% of the time, Pallas kernels for 19%

profile of v7, /device:TPU:24, one launch (start us, length us, event | category | flops | bytes accessed | tf_op | source)
XLA Modules:
  0.0 74.7 jit_solution(14318078472407956219)
XLA Ops:
  0.6 1.3 %pack_keys.1 = (bf16[512,384]{1,0:T(8,128)(2,1)S(1)}, bf16[544,384]{1,0:T(8,128)(2,1)S(1)}, bf16[384,256]{1,0:T(8,128)(2,1)S(1)}, bf16[384,256]{1,0:T(8,128)(2,1)S(1)}, bf16[384,256]{1,0:T(8,128)(2,1)S(1)}) custom-call(bf16[384,256]{1,0:T(8,128)(2,1)} %k.1, bf16[384,256]{1,0:T(8,128)(2,1)} %v.1, bf16[384,256]{1,0:T(8,128)(2,1)} %q.1, bf16[384,256]{1,0:T(8,128)(2,1)} %o.1, ...), custom_call_target="tpu_custom_call" | custom-call | tf_op jit(solution)/shard_map/pack_keys/pallas_call | solution.py:57
  2.0 3.4 %collective-permute-start.3 = (bf16[512,384]{1,0:T(8,128)(2,1)S(1)}, bf16[512,384]{1,0:T(8,128)(2,1)S(1)}, u32[]{:S(2)}, u32[]{:S(2)}) collective-permute-start(bf16[512,384]{1,0:T(8,128)(2,1)S(1)} %get-tuple-element.36.k0.refs_4_), channel_id=1, source_target_pairs={{0,1},{1,0},{2,3},{3,2},{4,5},{5,4},{6,7},{7,6},{8,9},{9,8},{10,11... | collective-permute-start | bytes 1179656 | tf_op jit(solution)/shard_map/ppermute | solution.py:418
  5.4 0.3 pack_queries.1.own.refs_0_
  5.6 6.0 %collective-permute-start = (bf16[528,384]{1,0:T(8,128)(2,1)S(1)}, bf16[528,384]{1,0:T(8,128)(2,1)S(1)}, u32[]{:S(2)}, u32[]{:S(2)}) collective-permute-start(bf16[528,384]{1,0:T(8,128)(2,1)S(1)} %pack_queries.1.own.refs_0_), channel_id=1, source_target_pairs={{0,6},{1,7},{2,4},{3,5},{4,2},{5,3},{6,0},{7,1},{8,10},{9,11},{10,... | collective-permute-start | bytes 1216520 | tf_op jit(solution)/shard_map/ppermute | solution.py:414
  11.7 1.9 %collective-permute-start.5 = (bf16[544,384]{1,0:T(8,128)(2,1)S(1)}, bf16[544,384]{1,0:T(8,128)(2,1)S(1)}, u32[]{:S(2)}, u32[]{:S(2)}) collective-permute-start(bf16[544,384]{1,0:T(8,128)(2,1)S(1)} %get-tuple-element.37), channel_id=1, source_target_pairs={{0,8},{1,9},{2,10},{3,11},{4,12},{5,13},{6,14},{7,15},{8,16},{9,17... | collective-permute-start | bytes 1253384 | tf_op jit(solution)/shard_map/ppermute | solution.py:432
  13.6 1.9 %collective-permute-start.1 = (bf16[528,384]{1,0:T(8,128)(2,1)S(1)}, bf16[528,384]{1,0:T(8,128)(2,1)S(1)}, u32[]{:S(2)}, u32[]{:S(2)}) collective-permute-start(bf16[528,384]{1,0:T(8,128)(2,1)S(1)} %pack_queries.1.own.refs_0_), channel_id=1, source_target_pairs={{0,2},{1,3},{2,0},{3,1},{4,6},{5,7},{6,4},{7,5},{8,14},{9,15},{10,... | collective-permute-start | bytes 1216520 | tf_op jit(solution)/shard_map/ppermute | solution.py:414
  15.5 0.0 collective-permute-done.3.k1.refs_5_
  15.5 2.8 %collective-permute-start.4 = (bf16[512,384]{1,0:T(8,128)(2,1)S(1)}, bf16[512,384]{1,0:T(8,128)(2,1)S(1)}, u32[]{:S(2)}, u32[]{:S(2)}) collective-permute-start(bf16[512,384]{1,0:T(8,128)(2,1)S(1)} %collective-permute-done.3.k1.refs_5_), channel_id=1, source_target_pairs={{0,8},{1,9},{2,10},{3,11},{4,12},{5,13},{6,14},{7,15},{8,16},{9,17... | collective-permute-start | bytes 1179656 | tf_op jit(solution)/shard_map/ppermute | solution.py:432
  18.3 0.0 collective-permute-done.first.refs_1_
  18.3 3.1 %collective-permute-start.2 = (bf16[528,384]{1,0:T(8,128)(2,1)S(1)}, bf16[528,384]{1,0:T(8,128)(2,1)S(1)}, u32[]{:S(2)}, u32[]{:S(2)}) collective-permute-start(bf16[528,384]{1,0:T(8,128)(2,1)S(1)} %collective-permute-done.first.refs_1_), channel_id=1, source_target_pairs={{0,2},{1,3},{2,0},{3,1},{4,6},{5,7},{6,4},{7,5},{8,14},{9,15},{10,... | collective-permute-start | bytes 1216520 | tf_op jit(solution)/shard_map/ppermute | solution.py:414
  21.4 2.0 %collective-permute-done.1.second.refs_2_ = bf16[528,384]{1,0:T(8,128)(2,1)S(1)} collective-permute-done((bf16[528,384]{1,0:T(8,128)(2,1)S(1)}, bf16[528,384]{1,0:T(8,128)(2,1)S(1)}, u32[]{:S(2)}, u32[]{:S(2)}) %collective-permute-start.1) | collective-permute-done | bytes 405536 | tf_op jit(solution)/shard_map/ppermute | solution.py:414
  23.4 2.4 %collective-permute-done.5.k2.refs_6_ = bf16[544,384]{1,0:T(8,128)(2,1)S(1)} collective-permute-done((bf16[544,384]{1,0:T(8,128)(2,1)S(1)}, bf16[544,384]{1,0:T(8,128)(2,1)S(1)}, u32[]{:S(2)}, u32[]{:S(2)}) %collective-permute-start.5) | collective-permute-done | bytes 417824 | tf_op jit(solution)/shard_map/ppermute | solution.py:432
  25.8 3.0 %first_scores.1 = (bf16[2,1536,1536]{2,1,0:T(8,128)(2,1)S(1)}, f32[8,1536]{1,0:T(8,128)S(1)}, bf16[2,256,1536]{2,1,0:T(8,128)(2,1)S(1)}) custom-call(bf16[528,384]{1,0:T(8,128)(2,1)S(1)} %pack_queries.1.own.refs_0_, bf16[528,384]{1,0:T(8,128)(2,1)S(1)} %collective-permute-done.first.refs_1_, bf16[528,384]{1,0:T(8,128)(2,1)S(1)} %collective-permute-done.1.second.refs_2_, ...), custom_call_target="tpu_custom_call" | custom-call | flops 1500000000 | tf_op jit(solution)/shard_map/first_scores/pallas_call | solution.py:123
  28.8 3.5 %collective-permute-done.4.k3.refs_7_ = bf16[512,384]{1,0:T(8,128)(2,1)S(1)} collective-permute-done((bf16[512,384]{1,0:T(8,128)(2,1)S(1)}, bf16[512,384]{1,0:T(8,128)(2,1)S(1)}, u32[]{:S(2)}, u32[]{:S(2)}) %collective-permute-start.4) | collective-permute-done | bytes 393248 | tf_op jit(solution)/shard_map/ppermute | solution.py:432
  32.4 1.4 %rest_scores.1 = (bf16[2,1536,1536]{2,1,0:T(8,128)(2,1)S(1)}, f32[8,1536]{1,0:T(8,128)S(1)}) custom-call(bf16[528,384]{1,0:T(8,128)(2,1)S(1)} %pack_queries.1.own.refs_0_, bf16[528,384]{1,0:T(8,128)(2,1)S(1)} %collective-permute-done.first.refs_1_, bf16[528,384]{1,0:T(8,128)(2,1)S(1)} %collective-permute-done.1.second.refs_2_, ...), custom_call_target="tpu_custom_call", output_to_operand_aliasing={{0}: (4, {})} | custom-call | flops 1000000000 | tf_op jit(solution)/shard_map/rest_scores/pallas_call | solution.py:170
  33.8 0.0 collective-permute-done.2.third.refs_3_
  33.8 1.5 %last_scores.1 = (bf16[2,1536,1536]{2,1,0:T(8,128)(2,1)S(1)}, f32[8,1536]{1,0:T(8,128)S(1)}, f32[8,1536]{1,0:T(8,128)S(1)}) custom-call(bf16[528,384]{1,0:T(8,128)(2,1)S(1)} %collective-permute-done.2.third.refs_3_, bf16[2,256,1536]{2,1,0:T(8,128)(2,1)S(1)} %last_keys.1.ks.refs_8_, ...), custom_call_target="tpu_custom_call", output_to_operand_aliasing={{0}: (2, {})} | custom-call | flops 1000000000 | tf_op jit(solution)/shard_map/last_scores/pallas_call | solution.py:197
  35.3 2.1 %collective-permute-start.6 = (f32[8,1536]{1,0:T(8,128)S(1)}, f32[8,1536]{1,0:T(8,128)S(1)}, u32[]{:S(2)}, u32[]{:S(2)}) collective-permute-start(f32[8,1536]{1,0:T(8,128)S(1)} %get-tuple-element.44.a), channel_id=1, source_target_pairs={{0,6},{1,7},{2,4},{3,5},{4,2},{5,3},{6,0},{7,1},{8,10},{9,11},{10,... | collective-permute-start | bytes 147464 | tf_op jit(solution)/shard_map/ppermute | solution.py:414
  37.4 2.8 %score_grads.2 = (bf16[1536,1536]{1,0:T(8,128)(2,1)S(1)}, f32[2,1536,128]{2,1,0:T(8,128)S(1)}) custom-call(bf16[528,384]{1,0:T(8,128)(2,1)S(1)} %pack_queries.1.own.refs_0_, bf16[528,384]{1,0:T(8,128)(2,1)S(1)} %collective-permute-done.first.refs_1_, bf16[528,384]{1,0:T(8,128)(2,1)S(1)} %collective-permute-done.1.second.refs_2_, ...), custom_call_target="tpu_custom_call" | custom-call | tf_op jit(solution)/shard_map/score_grads/pallas_call | solution.py:256
  40.2 2.3 %collective-permute-done.6.b = f32[8,1536]{1,0:T(8,128)S(1)} collective-permute-done((f32[8,1536]{1,0:T(8,128)S(1)}, f32[8,1536]{1,0:T(8,128)S(1)}, u32[]{:S(2)}, u32[]{:S(2)}) %collective-permute-start.6) | collective-permute-done | bytes 49184 | tf_op jit(solution)/shard_map/ppermute | solution.py:414
  42.5 2.1 %collective-permute-start.7 = (f32[8,1536]{1,0:T(8,128)S(1)}, f32[8,1536]{1,0:T(8,128)S(1)}, u32[]{:S(2)}, u32[]{:S(2)}) collective-permute-start(f32[8,1536]{1,0:T(8,128)S(1)} %merge.1.refs_5_), channel_id=1, source_target_pairs={{0,2},{1,3},{2,0},{3,1},{4,6},{5,7},{6,4},{7,5},{8,14},{9,15},{10,... | collective-permute-start | bytes 147464 | tf_op jit(solution)/shard_map/ppermute | solution.py:414
  44.6 2.8 %score_grads.3 = (bf16[1536,1536]{1,0:T(8,128)(2,1)S(1)}, f32[2,1536,128]{2,1,0:T(8,128)S(1)}) custom-call(bf16[528,384]{1,0:T(8,128)(2,1)S(1)} %pack_queries.1.own.refs_0_, bf16[528,384]{1,0:T(8,128)(2,1)S(1)} %collective-permute-done.first.refs_1_, bf16[528,384]{1,0:T(8,128)(2,1)S(1)} %collective-permute-done.1.second.refs_2_, ...), custom_call_target="tpu_custom_call" | custom-call | tf_op jit(solution)/shard_map/score_grads/pallas_call | solution.py:256
  47.4 1.1 %collective-permute-done.7.refs_6_ = f32[8,1536]{1,0:T(8,128)S(1)} collective-permute-done((f32[8,1536]{1,0:T(8,128)S(1)}, f32[8,1536]{1,0:T(8,128)S(1)}, u32[]{:S(2)}, u32[]{:S(2)}) %collective-permute-start.7) | collective-permute-done | bytes 49184 | tf_op jit(solution)/shard_map/ppermute | solution.py:414
  48.5 1.5 %prior_partner.1 = (bf16[528,384]{1,0:T(8,128)(2,1)S(1)}, f32[8,1536]{1,0:T(8,128)S(1)}, f32[768,256]{1,0:T(8,128)S(1)}, bf16[768,256]{1,0:T(8,128)(2,1)S(1)}) custom-call(bf16[528,384]{1,0:T(8,128)(2,1)S(1)} %pack_queries.1.own.refs_0_, bf16[528,384]{1,0:T(8,128)(2,1)S(1)} %collective-permute-done.first.refs_1_, ...), custom_call_target="tpu_custom_call" | custom-call | tf_op jit(solution)/shard_map/prior_partner/pallas_call | solution.py:306
  50.0 2.5 %collective-permute-start.8 = (bf16[528,384]{1,0:T(8,128)(2,1)S(1)}, bf16[528,384]{1,0:T(8,128)(2,1)S(1)}, u32[]{:S(2)}, u32[]{:S(2)}) collective-permute-start(bf16[528,384]{1,0:T(8,128)(2,1)S(1)} %get-tuple-element.52), channel_id=1, source_target_pairs={{0,1},{1,0},{2,3},{3,2},{4,5},{5,4},{6,7},{7,6},{8,9},{9,8},{10,11... | collective-permute-start | bytes 1216520 | tf_op jit(solution)/shard_map/ppermute | solution.py:418
  52.5 2.8 %collective-permute-start.9 = (bf16[768,256]{1,0:T(8,128)(2,1)S(1)}, bf16[768,256]{1,0:T(8,128)(2,1)S(1)}, u32[]{:S(2)}, u32[]{:S(2)}) collective-permute-start(bf16[768,256]{1,0:T(8,128)(2,1)S(1)} %get-tuple-element.54), channel_id=1, source_target_pairs={{0,2},{1,3},{2,0},{3,1},{4,6},{5,7},{6,4},{7,5},{8,14},{9,15},{10,... | collective-permute-start | bytes 1179656 | tf_op jit(solution)/shard_map/ppermute | solution.py:414
  55.3 2.7 %key_grads.1 = (bf16[512,384]{1,0:T(8,128)(2,1)S(1)}, f32[512,384]{1,0:T(8,128)S(1)}, f32[512,384]{1,0:T(8,128)S(1)}) custom-call(bf16[528,384]{1,0:T(8,128)(2,1)S(1)} %pack_queries.1.own.refs_0_, bf16[528,384]{1,0:T(8,128)(2,1)S(1)} %collective-permute-done.first.refs_1_, bf16[528,384]{1,0:T(8,128)(2,1)S(1)} %collective-permute-done.1.second.refs_2_, ...), custom_call_target="tpu_custom_call" | custom-call | tf_op jit(solution)/shard_map/key_grads/pallas_call | solution.py:333
  58.1 3.4 %collective-permute-start.11 = (bf16[512,384]{1,0:T(8,128)(2,1)S(1)}, bf16[512,384]{1,0:T(8,128)(2,1)S(1)}, u32[]{:S(2)}, u32[]{:S(2)}) collective-permute-start(bf16[512,384]{1,0:T(8,128)(2,1)S(1)} %get-tuple-element.58), channel_id=1, source_target_pairs={{0,1},{1,0},{2,3},{3,2},{4,5},{5,4},{6,7},{7,6},{8,9},{9,8},{10,11... | collective-permute-start | bytes 1179656 | tf_op jit(solution)/shard_map/ppermute | solution.py:418
  61.4 0.7 collective-permute-done.9.far
  62.2 0.9 %collective-permute-done.8.part = bf16[528,384]{1,0:T(8,128)(2,1)S(1)} collective-permute-done((bf16[528,384]{1,0:T(8,128)(2,1)S(1)}, bf16[528,384]{1,0:T(8,128)(2,1)S(1)}, u32[]{:S(2)}, u32[]{:S(2)}) %collective-permute-start.8) | collective-permute-done | bytes 405536 | tf_op jit(solution)/shard_map/ppermute | solution.py:418
  63.1 0.1 middle_sums.1
  63.2 1.9 %collective-permute-start.12 = (bf16[512,384]{1,0:T(8,128)(2,1)S(1)}, bf16[512,384]{1,0:T(8,128)(2,1)S(1)}, u32[]{:S(2)}, u32[]{:S(2)}) collective-permute-start(bf16[512,384]{1,0:T(8,128)(2,1)S(1)} %get-tuple-element.59), channel_id=1, source_target_pairs={{8,0},{9,1},{10,2},{11,3},{12,4},{13,5},{14,6},{15,7},{16,8},{17,9... | collective-permute-start | bytes 1179656 | tf_op jit(solution)/shard_map/ppermute | solution.py:436
  65.2 3.5 %collective-permute-start.10 = (bf16[384,256]{1,0:T(8,128)(2,1)S(1)}, bf16[384,256]{1,0:T(8,128)(2,1)S(1)}, u32[]{:S(2)}, u32[]{:S(2)}) collective-permute-start(bf16[384,256]{1,0:T(8,128)(2,1)S(1)} %get-tuple-element.56), channel_id=1, source_target_pairs={{0,6},{1,7},{2,4},{3,5},{4,2},{5,3},{6,0},{7,1},{8,10},{9,11},{10,... | collective-permute-start | bytes 589832 | tf_op jit(solution)/shard_map/ppermute | solution.py:414
  68.6 0.0 collective-permute-done.11.other
  68.7 0.1 own_sum.1.own
  68.7 1.7 %collective-permute-done.12.back = bf16[512,384]{1,0:T(8,128)(2,1)S(1)} collective-permute-done((bf16[512,384]{1,0:T(8,128)(2,1)S(1)}, bf16[512,384]{1,0:T(8,128)(2,1)S(1)}, u32[]{:S(2)}, u32[]{:S(2)}) %collective-permute-start.12) | collective-permute-done | bytes 393248 | tf_op jit(solution)/shard_map/ppermute | solution.py:436
  70.4 0.9 %key_sum.1 = (bf16[384,256]{1,0:T(8,128)(2,1)}, bf16[384,256]{1,0:T(8,128)(2,1)}, f32[8,128]{1,0:T(8,128)S(1)}) custom-call(f32[512,384]{1,0:T(8,128)S(1)} %own_sum.1.own, bf16[512,384]{1,0:T(8,128)(2,1)S(1)} %collective-permute-done.12.back), custom_call_target="tpu_custom_call" | custom-call | tf_op jit(solution)/shard_map/key_sum/pallas_call | solution.py:400
  71.3 2.6 %collective-permute-done.10.pair = bf16[384,256]{1,0:T(8,128)(2,1)S(1)} collective-permute-done((bf16[384,256]{1,0:T(8,128)(2,1)S(1)}, bf16[384,256]{1,0:T(8,128)(2,1)S(1)}, u32[]{:S(2)}, u32[]{:S(2)}) %collective-permute-start.10) | collective-permute-done | bytes 196640 | tf_op jit(solution)/shard_map/ppermute | solution.py:414
  73.9 0.7 query_sum.1
  (2 shorter events, 0.1 us)
Async XLA Ops:
  2.0 13.6 %collective-permute-start.3 = (bf16[512,384]{1,0:T(8,128)(2,1)S(1)}, bf16[512,384]{1,0:T(8,128)(2,1)S(1)}, u32[]{:S(2)}, u32[]{:S(2)}) collective-permute-start(bf16[512,384]{1,0:T(8,128)(2,1)S(1)} %get-tuple-element.36.k0.refs_4_), channel_id=1, source_target_pairs={{0,1},{1,0},{2,3},{3,2},{4,5},{5,4},{6,7},{7,6},{8,9},{9,8},{10,11... | collective-permute-start | bytes 1179656 | tf_op jit(solution)/shard_map/ppermute | solution.py:418
  5.6 12.7 %collective-permute-start = (bf16[528,384]{1,0:T(8,128)(2,1)S(1)}, bf16[528,384]{1,0:T(8,128)(2,1)S(1)}, u32[]{:S(2)}, u32[]{:S(2)}) collective-permute-start(bf16[528,384]{1,0:T(8,128)(2,1)S(1)} %pack_queries.1.own.refs_0_), channel_id=1, source_target_pairs={{0,6},{1,7},{2,4},{3,5},{4,2},{5,3},{6,0},{7,1},{8,10},{9,11},{10,... | collective-permute-start | bytes 1216520 | tf_op jit(solution)/shard_map/ppermute | solution.py:414
  11.7 14.2 %collective-permute-start.5 = (bf16[544,384]{1,0:T(8,128)(2,1)S(1)}, bf16[544,384]{1,0:T(8,128)(2,1)S(1)}, u32[]{:S(2)}, u32[]{:S(2)}) collective-permute-start(bf16[544,384]{1,0:T(8,128)(2,1)S(1)} %get-tuple-element.37), channel_id=1, source_target_pairs={{0,8},{1,9},{2,10},{3,11},{4,12},{5,13},{6,14},{7,15},{8,16},{9,17... | collective-permute-start | bytes 1253384 | tf_op jit(solution)/shard_map/ppermute | solution.py:432
  13.6 9.8 %collective-permute-start.1 = (bf16[528,384]{1,0:T(8,128)(2,1)S(1)}, bf16[528,384]{1,0:T(8,128)(2,1)S(1)}, u32[]{:S(2)}, u32[]{:S(2)}) collective-permute-start(bf16[528,384]{1,0:T(8,128)(2,1)S(1)} %pack_queries.1.own.refs_0_), channel_id=1, source_target_pairs={{0,2},{1,3},{2,0},{3,1},{4,6},{5,7},{6,4},{7,5},{8,14},{9,15},{10,... | collective-permute-start | bytes 1216520 | tf_op jit(solution)/shard_map/ppermute | solution.py:414
  15.5 16.8 %collective-permute-start.4 = (bf16[512,384]{1,0:T(8,128)(2,1)S(1)}, bf16[512,384]{1,0:T(8,128)(2,1)S(1)}, u32[]{:S(2)}, u32[]{:S(2)}) collective-permute-start(bf16[512,384]{1,0:T(8,128)(2,1)S(1)} %collective-permute-done.3.k1.refs_5_), channel_id=1, source_target_pairs={{0,8},{1,9},{2,10},{3,11},{4,12},{5,13},{6,14},{7,15},{8,16},{9,17... | collective-permute-start | bytes 1179656 | tf_op jit(solution)/shard_map/ppermute | solution.py:432
  18.3 15.5 %collective-permute-start.2 = (bf16[528,384]{1,0:T(8,128)(2,1)S(1)}, bf16[528,384]{1,0:T(8,128)(2,1)S(1)}, u32[]{:S(2)}, u32[]{:S(2)}) collective-permute-start(bf16[528,384]{1,0:T(8,128)(2,1)S(1)} %collective-permute-done.first.refs_1_), channel_id=1, source_target_pairs={{0,2},{1,3},{2,0},{3,1},{4,6},{5,7},{6,4},{7,5},{8,14},{9,15},{10,... | collective-permute-start | bytes 1216520 | tf_op jit(solution)/shard_map/ppermute | solution.py:414
  35.3 7.2 %collective-permute-start.6 = (f32[8,1536]{1,0:T(8,128)S(1)}, f32[8,1536]{1,0:T(8,128)S(1)}, u32[]{:S(2)}, u32[]{:S(2)}) collective-permute-start(f32[8,1536]{1,0:T(8,128)S(1)} %get-tuple-element.44.a), channel_id=1, source_target_pairs={{0,6},{1,7},{2,4},{3,5},{4,2},{5,3},{6,0},{7,1},{8,10},{9,11},{10,... | collective-permute-start | bytes 147464 | tf_op jit(solution)/shard_map/ppermute | solution.py:414
  42.5 6.0 %collective-permute-start.7 = (f32[8,1536]{1,0:T(8,128)S(1)}, f32[8,1536]{1,0:T(8,128)S(1)}, u32[]{:S(2)}, u32[]{:S(2)}) collective-permute-start(f32[8,1536]{1,0:T(8,128)S(1)} %merge.1.refs_5_), channel_id=1, source_target_pairs={{0,2},{1,3},{2,0},{3,1},{4,6},{5,7},{6,4},{7,5},{8,14},{9,15},{10,... | collective-permute-start | bytes 147464 | tf_op jit(solution)/shard_map/ppermute | solution.py:414
  50.0 13.1 %collective-permute-start.8 = (bf16[528,384]{1,0:T(8,128)(2,1)S(1)}, bf16[528,384]{1,0:T(8,128)(2,1)S(1)}, u32[]{:S(2)}, u32[]{:S(2)}) collective-permute-start(bf16[528,384]{1,0:T(8,128)(2,1)S(1)} %get-tuple-element.52), channel_id=1, source_target_pairs={{0,1},{1,0},{2,3},{3,2},{4,5},{5,4},{6,7},{7,6},{8,9},{9,8},{10,11... | collective-permute-start | bytes 1216520 | tf_op jit(solution)/shard_map/ppermute | solution.py:418
  52.5 9.7 %collective-permute-start.9 = (bf16[768,256]{1,0:T(8,128)(2,1)S(1)}, bf16[768,256]{1,0:T(8,128)(2,1)S(1)}, u32[]{:S(2)}, u32[]{:S(2)}) collective-permute-start(bf16[768,256]{1,0:T(8,128)(2,1)S(1)} %get-tuple-element.54), channel_id=1, source_target_pairs={{0,2},{1,3},{2,0},{3,1},{4,6},{5,7},{6,4},{7,5},{8,14},{9,15},{10,... | collective-permute-start | bytes 1179656 | tf_op jit(solution)/shard_map/ppermute | solution.py:414
  58.1 10.6 %collective-permute-start.11 = (bf16[512,384]{1,0:T(8,128)(2,1)S(1)}, bf16[512,384]{1,0:T(8,128)(2,1)S(1)}, u32[]{:S(2)}, u32[]{:S(2)}) collective-permute-start(bf16[512,384]{1,0:T(8,128)(2,1)S(1)} %get-tuple-element.58), channel_id=1, source_target_pairs={{0,1},{1,0},{2,3},{3,2},{4,5},{5,4},{6,7},{7,6},{8,9},{9,8},{10,11... | collective-permute-start | bytes 1179656 | tf_op jit(solution)/shard_map/ppermute | solution.py:418
  63.2 7.2 %collective-permute-start.12 = (bf16[512,384]{1,0:T(8,128)(2,1)S(1)}, bf16[512,384]{1,0:T(8,128)(2,1)S(1)}, u32[]{:S(2)}, u32[]{:S(2)}) collective-permute-start(bf16[512,384]{1,0:T(8,128)(2,1)S(1)} %get-tuple-element.59), channel_id=1, source_target_pairs={{8,0},{9,1},{10,2},{11,3},{12,4},{13,5},{14,6},{15,7},{16,8},{17,9... | collective-permute-start | bytes 1179656 | tf_op jit(solution)/shard_map/ppermute | solution.py:436
  65.2 8.8 %collective-permute-start.10 = (bf16[384,256]{1,0:T(8,128)(2,1)S(1)}, bf16[384,256]{1,0:T(8,128)(2,1)S(1)}, u32[]{:S(2)}, u32[]{:S(2)}) collective-permute-start(bf16[384,256]{1,0:T(8,128)(2,1)S(1)} %get-tuple-element.56), channel_id=1, source_target_pairs={{0,6},{1,7},{2,4},{3,5},{4,2},{5,3},{6,0},{7,1},{8,10},{9,11},{10,... | collective-permute-start | bytes 589832 | tf_op jit(solution)/shard_map/ppermute | solution.py:414
